TPU v7x, 32 devices: a whole 2x2x4 slice. The times are simulated.
32 devices in a mesh: case: 2 (over y), span: 8 (over z, x), sect: 2 (over core).
Axes of the slice: x: 2, y: 2, z: 4, core: 2. Of those that a mesh axis runs over, the one named last changes fastest.
Arguments:
- fine_field: bfloat16 [16, 3, 32, 128, 128], P('case', None, 'sect', 'span'), parts along dimension 0, may hold values from -16 to 16
- stored: bfloat16 [248, 49152], P(None, ('case', 'span', 'sect')), parts along dimension 1, may hold values from -16 to 16
- filter_taps: float32 [3, 17], replicated, may hold values from 0.1 to 0.5
Outputs:
- coarse_new: bfloat16 [8, 49152], P(None, ('case', 'span', 'sect')), parts along dimension 1
- factor: float32 [512, 256], P('case'), parts along dimension 0
- basis: float32 [256, 49152], P(None, ('case', 'span', 'sect')), parts along dimension 1
There are 2 independent parts, one for each index of `case`. A program takes and returns all parts, laid end to end along the dimension named above; an argument that names none is the same for every part. Nothing has to cross between parts.
All inputs are finite; a program needn't handle non-finite values.
Results may differ from a plain program's by a relative error of at most 0.011.
Values may be sent and summed in bfloat16 or wider, within the bound.
No kernel may reach another device: no remote copies, remote signals or barrier semaphores. Data moves between devices by JAX's collectives and lax.ppermute only.
A program may use at most 64 MiB of HBM per device.

v0:
```python
import jax
import jax.numpy as jnp
from jax import lax
from jax.sharding import PartitionSpec as P


def with_halo(cells, sides, width):
    for axis, dim in sides:
        count = lax.axis_size(axis)
        ends = count - 1
        head = lax.slice_in_dim(cells, 0, width, axis=dim)
        tail = lax.slice_in_dim(cells, cells.shape[dim] - width, cells.shape[dim], axis=dim)
        cells = jnp.concatenate(
            [
                lax.ppermute(tail, axis, [(i, (i + 1) % count) for i in range(ends)]),
                cells,
                lax.ppermute(head, axis, [((i + 1) % count, i) for i in range(ends)]),
            ],
            axis=dim,
        )
    return cells


def band_matrix(weights, n_in, n_out, shift):
    rows_in = jnp.arange(n_in, dtype=jnp.int32)[:, None]
    cols_out = jnp.arange(n_out, dtype=jnp.int32)[None, :]
    offset = rows_in - 4 * cols_out + shift
    taps = jnp.arange(17, dtype=jnp.int32)
    hits = offset[:, :, None] == taps[None, None, :]
    return jnp.sum(jnp.where(hits, weights[None, None, :], 0.0), axis=2)


def contract(form, values, matrix):
    return jnp.einsum(
        form, values, matrix, precision=lax.Precision.HIGHEST, preferred_element_type=jnp.float32
    )


def local(fine_field, stored, filter_taps):
    snapshots, comps, cells_y, cells_z, cells_x = fine_field.shape
    coarse_y, coarse_z, coarse_x = (cells_y // 4, cells_z // 4, cells_x // 4)
    stream_matrix = band_matrix(filter_taps[2], cells_x, coarse_x, 8)
    padded = with_halo(fine_field, (("span", 3), ("sect", 2)), 8)
    coarse = contract("ncyzx,xj->ncyzj", padded, stream_matrix)
    coarse = contract(
        "ncyzj,yk->nckzj", coarse, band_matrix(filter_taps[0], cells_y + 16, coarse_y, 0)
    )
    coarse = contract(
        "nckzj,zl->ncklj", coarse, band_matrix(filter_taps[1], cells_z + 16, coarse_z, 0)
    )
    rows_dev = comps * coarse_y * coarse_z * coarse_x
    coarse_new = coarse.astype(jnp.bfloat16).reshape(snapshots, rows_dev)
    window = jnp.concatenate([stored, coarse_new], axis=0)
    groups = lax.axis_size("span") * lax.axis_size("sect")
    total_rows = rows_dev * groups
    local_gram = jnp.dot(window, window.T, preferred_element_type=jnp.float32) / total_rows
    gram = lax.psum(local_gram, ("span", "sect"))
    lower = jnp.linalg.cholesky(gram)
    basis = jax.scipy.linalg.solve_triangular(lower, window.astype(jnp.float32), lower=True)
    return (coarse_new, lower, basis)


def solution(mesh):
    in_specs = (P("case", None, "sect", "span", None), P(None, ("case", "span", "sect")), P())
    out_specs = (
        P(None, ("case", "span", "sect")),
        P("case", None),
        P(None, ("case", "span", "sect")),
    )
    return jax.shard_map(local, mesh=mesh, in_specs=in_specs, out_specs=out_specs, check_vma=False)
```

profile of v0, /device:TPU:0, one launch (start us, length us, event | category | flops | bytes accessed | tf_op | source)
XLA Modules:
  0.0 240.3 jit_solution(8893587395195759437)
XLA Ops:
  7.2 0.0 copy-start
  7.2 0.0 all-reduce.3.cloned.1.call-start
  7.2 1.6 fusion.32
  8.8 4.9 %collective-permute-start = (bf16[8,3,16,8,128]{4,3,2,1,0:T(8,128)(2,1)S(1)}, bf16[8,3,16,8,128]{4,3,2,1,0:T(8,128)(2,1)S(1)}, u32[]{:S(2)}, u32[]{:S(2)}) collective-permute-start(bf16[8,3,16,8,128]{4,3,2,1,0:T(8,128)(2,1)S(1)} %get-tuple-element.28), channel_id=1, source_target_pairs={{0,2},{2,4},{4,6},{6,8},{8,10},{10,12},{12,14},{1,3},{3,5},{5,7},{... | collective-permute-start | bytes 2359304 | tf_op jit(solution)/shard_map/ppermute | solution.py:15
  13.7 1.3 collective-permute-start.1
  15.0 32.3 %collective-permute-done = bf16[8,3,16,8,128]{4,3,2,1,0:T(8,128)(2,1)S(1)} collective-permute-done((bf16[8,3,16,8,128]{4,3,2,1,0:T(8,128)(2,1)S(1)}, bf16[8,3,16,8,128]{4,3,2,1,0:T(8,128)(2,1)S(1)}, u32[]{:S(2)}, u32[]{:S(2)}) %collective-permute-start) | collective-permute-done | bytes 786464 | tf_op jit(solution)/shard_map/ppermute | solution.py:15
  47.3 0.1 constant_dynamic-update-slice_fusion.2
  47.4 0.0 copy-done
  47.5 0.4 constant_dynamic-update-slice_fusion.1
  47.9 0.0 collective-permute-done.1
  47.9 0.2 constant_dynamic-update-slice_fusion
  48.1 0.0 copy-start.3
  48.1 0.0 copy-start.1
  48.1 0.5 fusion.31
  48.6 1.4 collective-permute-start.2
  50.0 1.5 collective-permute-start.3
  51.5 0.1 iota_subtract_fusion
  51.6 0.0 copy-done.3
  51.6 0.1 select_reduce_fusion.4
  51.7 0.1 subtract_add_fusion
  51.8 0.1 select_reduce_fusion
  51.9 0.0 copy-done.1
  51.9 0.1 constant_dynamic-update-slice_fusion.4
  52.0 1.0 collective-permute-done.2
  53.0 2.4 collective-permute-done.3
  55.3 5.1 %fusion.2 = f32[8,3,32,32,32]{4,3,2,1,0:T(8,128)S(1)} fusion(bf16[8,3,8,32,128]{4,3,2,1,0:T(8,128)(2,1)S(1)} %collective-permute-done.3, bf16[8,3,16,32,128]{4,3,2,1,0:T(8,128)(2,1)S(1)} %constant_dynamic-update-slice_fusion, bf16[8,3,8,32,128]{4,3,2,1,0:T(8,128)(2,1)S(1)} %collective-permute-done.2, f32[128,32]{0,1:T(8,128)S(1)} %select_reduce_fusion), kind=kOutput, calls=%fused_computation.4 | convolution fusion | flops 1214251008 | bytes 9453568 | tf_op jit(solution)/shard_map/ncyzx,xj->ncyzj/dot_general | solution.py:34
  60.5 13.1 %fusion = f32[4,8,3,32,32]{4,0,3,2,1:T(4,128)S(1)} fusion(f32[8,3,32,32,32]{4,3,2,1,0:T(8,128)S(1)} %fusion.2, f32[32,4]{0,1:T(4,128)S(1)} %get-tuple-element.12), kind=kOutput, calls=%fused_computation.2 | convolution fusion | flops 37748736 | bytes 3539456 | tf_op jit(solution)/shard_map/ncyzj,yk->nckzj/dot_general | solution.py:34
  73.6 0.9 fusion.14
  74.4 0.1 reshape.80
  74.6 0.0 copy-start.2
  74.6 1.1 convolution_multiply_fusion
  75.7 0.0 all-reduce.3.cloned.1.call-update
  75.7 91.1 %all-reduce.3.cloned.1.call-done = f32[256,256]{0,1:T(8,128)} async-done(((f32[256,256]{0,1:T(8,128)}), f32[256,256]{0,1:T(8,128)}) %all-reduce.3.cloned.1.call-update) | async-done | bytes 262160 | tf_op jit(solution)/shard_map/psum | solution.py:57
  166.9 1.1 copy.9
  168.0 1.0 fusion.19
  169.0 11.9 %cholesky.50 = f32[128,128]{1,0:T(8,128)S(1)} custom-call(f32[128,128]{1,0:T(8,128)S(1)} %cholesky.118), custom_call_target="Cholesky" | custom-call | tf_op jit(solution)/shard_map/jit(cholesky)/cholesky | solution.py:58
  181.0 9.8 %custom-call.15 = f32[1,128,128]{1,2,0:T(8,128)S(1)} custom-call(f32[1,128,128]{2,1,0:T(8,128)S(1)} %get-tuple-element.32), custom_call_target="InvertDiagBlocksLowerTriangular" | custom-call | tf_op jit(solution)/shard_map/jit(cholesky)/cholesky | solution.py:58
  190.8 0.2 constant_dynamic-update-slice_fusion.6
  191.0 0.3 convolution_subtract_fusion.1
  191.3 11.7 %cholesky.105 = f32[128,128]{1,0:T(8,128)S(1)} custom-call(f32[128,128]{1,0:T(8,128)S(1)} %convolution_subtract_fusion.1), custom_call_target="Cholesky" | custom-call | tf_op jit(solution)/shard_map/jit(cholesky)/cholesky | solution.py:58
  203.0 0.6 compare_reduce_fusion
  205.0 0.7 fusion.20
  205.7 0.1 triangular_solve.44
  205.8 0.0 copy-done.2
  205.8 4.1 %while.1 = (s32[]{:T(128)}, f32[256,256]{1,0:T(8,128)S(1)}, s32[2,2]{1,0:T(2,128)S(1)}, f32[2,128,128]{2,1,0:T(8,128)S(1)}, s32[]{:T(128)}) while((s32[]{:T(128)}, f32[256,256]{1,0:T(8,128)S(1)}, s32[2,2]{1,0:T(2,128)S(1)}, f32[2,128,128]{2,1,0:T(8,128)S(1)}, s32[]{:T(128)}) %tuple.33), condition=%wide.while_cond, body=%wide.while_body.sunk | while | flops 2 | bytes 131181 | solution.py:59
  205.8 0.6 fusion.40
  206.4 1.4 bitcast_dynamic-update-slice_fusion.2
  207.9 0.6 fusion.40
  208.5 1.4 bitcast_dynamic-update-slice_fusion.2
  209.9 19.7 %custom-call.16 = f32[2,128,128]{1,2,0:T(8,128)S(1)} custom-call(f32[2,128,128]{2,1,0:T(8,128)S(1)} %get-tuple-element.10), custom_call_target="InvertDiagBlocksLowerTriangular" | custom-call | tf_op jit(solution)/shard_map/jit(_solve_triangular)/triangular_solve | solution.py:59
  229.6 0.5 fusion.17
  230.1 0.8 convolution_subtract_fusion
  230.9 0.8 fusion.22
  231.8 1.3 pad_maximum_fusion
  (12 shorter events, 0.1 us)
Async XLA Ops:
  7.2 40.3 %copy-start = (bf16[8,3,16,16,128]{4,3,2,1,0:T(8,128)(2,1)S(1)}, bf16[8,3,16,16,128]{4,3,2,1,0:T(8,128)(2,1)}, u32[]{:S(2)}) copy-start(bf16[8,3,16,16,128]{4,3,2,1,0:T(8,128)(2,1)} %param.3) | copy-start | bytes 4718596
  7.2 159.7 %all-reduce.3.cloned.1.call-start = ((), (), s32[]{:S(2)}) async-start(), calls=%async_computation | async-start | bytes 524288 | tf_op jit(solution)/shard_map/psum | solution.py:57
  8.8 38.5 %collective-permute-start = (bf16[8,3,16,8,128]{4,3,2,1,0:T(8,128)(2,1)S(1)}, bf16[8,3,16,8,128]{4,3,2,1,0:T(8,128)(2,1)S(1)}, u32[]{:S(2)}, u32[]{:S(2)}) collective-permute-start(bf16[8,3,16,8,128]{4,3,2,1,0:T(8,128)(2,1)S(1)} %get-tuple-element.28), channel_id=1, source_target_pairs={{0,2},{2,4},{4,6},{6,8},{8,10},{10,12},{12,14},{1,3},{3,5},{5,7},{... | collective-permute-start | bytes 2359304 | tf_op jit(solution)/shard_map/ppermute | solution.py:15
  13.7 34.2 %collective-permute-start.1 = (bf16[8,3,16,8,128]{4,3,2,1,0:T(8,128)(2,1)S(1)}, bf16[8,3,16,8,128]{4,3,2,1,0:T(8,128)(2,1)S(1)}, u32[]{:S(2)}, u32[]{:S(2)}) collective-permute-start(bf16[8,3,16,8,128]{4,3,2,1,0:T(8,128)(2,1)S(1)} %get-tuple-element.27), channel_id=1, source_target_pairs={{2,0},{4,2},{6,4},{8,6},{10,8},{12,10},{14,12},{3,1},{5,3},{7,5},{... | collective-permute-start | bytes 2359304 | tf_op jit(solution)/shard_map/ppermute | solution.py:17
  48.1 3.5 %copy-start.3 = (f32[3,17]{1,0:T(4,128)S(1)}, f32[3,17]{1,0:T(4,128)}, u32[]{:S(2)}) copy-start(f32[3,17]{1,0:T(4,128)} %param.5) | copy-start | bytes 616
  48.1 3.8 %copy-start.1 = (bf16[248,1536]{1,0:T(8,128)(2,1)S(1)}, bf16[248,1536]{1,0:T(8,128)(2,1)}, u32[]{:S(2)}) copy-start(bf16[248,1536]{1,0:T(8,128)(2,1)} %param.4) | copy-start | bytes 2285572
  48.6 4.3 %collective-permute-start.2 = (bf16[8,3,8,32,128]{4,3,2,1,0:T(8,128)(2,1)S(1)}, bf16[8,3,8,32,128]{4,3,2,1,0:T(8,128)(2,1)S(1)}, u32[]{:S(2)}, u32[]{:S(2)}) collective-permute-start(bf16[8,3,8,32,128]{4,3,2,1,0:T(8,128)(2,1)S(1)} %get-tuple-element.25), channel_id=1, source_target_pairs={{0,1},{2,3},{4,5},{6,7},{8,9},{10,11},{12,13},{14,15},{16,17},{18,... | collective-permute-start | bytes 4718600 | tf_op jit(solution)/shard_map/ppermute | solution.py:15
  50.0 5.3 %collective-permute-start.3 = (bf16[8,3,8,32,128]{4,3,2,1,0:T(8,128)(2,1)S(1)}, bf16[8,3,8,32,128]{4,3,2,1,0:T(8,128)(2,1)S(1)}, u32[]{:S(2)}, u32[]{:S(2)}) collective-permute-start(bf16[8,3,8,32,128]{4,3,2,1,0:T(8,128)(2,1)S(1)} %get-tuple-element.26), channel_id=1, source_target_pairs={{1,0},{3,2},{5,4},{7,6},{9,8},{11,10},{13,12},{15,14},{17,16},{19,... | collective-permute-start | bytes 4718600 | tf_op jit(solution)/shard_map/ppermute | solution.py:17
  74.6 131.2 %copy-start.2 = (bf16[8,1536]{1,0:T(8,128)(2,1)}, bf16[8,1536]{1,0:T(8,128)(2,1)S(1)}, u32[]{:S(2)}) copy-start(bf16[8,1536]{1,0:T(8,128)(2,1)S(1)} %reshape.80) | copy-start | bytes 73732
Sparse Core Ops, SparseCore 0:
  75.8 90.9 all-reduce.2
where the time goes:
time: 243 us; the launch traced here: 240 us
  waiting for transfers between devices  127 us (52%)
  other arithmetic  57.2 us (24%)
  matrix products  22.8 us (9%)
  between operations  16 us (7%)
  starting transfers between devices  9.08 us (4%)
  local copies, waits for them, and re-layouts  8.3 us (3%)
    psum x1, waiting for transfers between devices, local(): gram = lax.psum(local_gram, ('span', 'sect'))  91.1 us
    another operation x6, other arithmetic, local(): lower = jnp.linalg.cholesky(gram)  34.2 us
    ppermute x2, waiting for transfers between devices, with_halo(): lax.ppermute(tail, axis, [(i, (i + 1) % count) for i in range(ends)])  33.3 us
    another operation x4, other arithmetic, local(): jax.scipy.linalg.solve_triangular(lower, window.astype(jnp.float32), lowe...  21.7 us
    dot_general x3, matrix products, contract(): jnp.einsum(form, values, matrix, precision=lax.Precision.HIGHEST, preferr...  19.1 us
    ppermute x2, starting transfers between devices, with_halo(): lax.ppermute(tail, axis, [(i, (i + 1) % count) for i in range(ends)])  6.28 us
  transfers between devices with their start and end apart: 5, of which 4 were waited for; matrix products, arithmetic and copies ran while one was open for 0% of the time, Pallas kernels for 0%

commit v1 on v0

--- a/solution.py
+++ b/solution.py
@@ -36,6 +36,30 @@
     )
 
 
+def swap(values, axis, bit):
+    count = lax.axis_size(axis)
+    return lax.ppermute(values, axis, [(i, i ^ bit) for i in range(count)])
+
+
+def sum_over_group(terms):
+    spans = lax.axis_size("span")
+    if spans & (spans - 1) or lax.axis_size("sect") != 2:
+        return lax.psum(terms, ("span", "sect"))
+    me = lax.axis_index("sect")
+    half = terms.shape[0] // 2
+    kept = lax.dynamic_slice_in_dim(terms, me * half, half, 0)
+    sent = lax.dynamic_slice_in_dim(terms, (1 - me) * half, half, 0)
+    kept = kept + swap(sent, "sect", 1)
+    bit = 1
+    while bit < spans:
+        kept = kept + swap(kept, "span", bit)
+        bit *= 2
+    other = swap(kept, "sect", 1)
+    first = jnp.where(me == 0, kept, other)
+    second = jnp.where(me == 0, other, kept)
+    return jnp.concatenate([first, second], axis=0)
+
+
 def local(fine_field, stored, filter_taps):
     snapshots, comps, cells_y, cells_z, cells_x = fine_field.shape
     coarse_y, coarse_z, coarse_x = (cells_y // 4, cells_z // 4, cells_x // 4)
@@ -54,7 +78,7 @@
     groups = lax.axis_size("span") * lax.axis_size("sect")
     total_rows = rows_dev * groups
     local_gram = jnp.dot(window, window.T, preferred_element_type=jnp.float32) / total_rows
-    gram = lax.psum(local_gram, ("span", "sect"))
+    gram = sum_over_group(local_gram)
     lower = jnp.linalg.cholesky(gram)
     basis = jax.scipy.linalg.solve_triangular(lower, window.astype(jnp.float32), lower=True)
     return (coarse_new, lower, basis)

time: 243 us -> 160 us (0.66); the launches traced: 240 us -> 160 us
  waiting for transfers between devices: 127 us -> 49.9 us
  between operations: 16 us -> 2.28 us
  starting transfers between devices: 9.08 us -> 18.6 us
    psum x1 -> x0, waiting for transfers between devices: 91.1 us -> none  [local(): gram = lax.psum(local_gram, ('span', 'sect'))]
    ppermute x0 -> x5, waiting for transfers between devices: none -> 14 us  [swap(): return lax.ppermute(values, axis, [(i, i ^ bit) for i in range(count)])]
    ppermute x0 -> x5, starting transfers between devices: none -> 8.71 us  [swap(): return lax.ppermute(values, axis, [(i, i ^ bit) for i in range(count)])]
  transfers between devices with their start and end apart: 5 -> 9, of which waited for: 4 -> 8; matrix products, arithmetic and copies ran while one was open for 0% -> 1% of each run, Pallas kernels for 0% -> 0%
where the time goes in v1:
time: 160 us
  other arithmetic  56.4 us (35%)
  waiting for transfers between devices  49.9 us (31%)
  matrix products  24.1 us (15%)
  starting transfers between devices  18.6 us (12%)
  local copies, waits for them, and re-layouts  8.76 us (5%)
  between operations  2.28 us (1%)
    another operation x6, other arithmetic, local(): lower = jnp.linalg.cholesky(gram)  34.2 us
    ppermute x2, waiting for transfers between devices, with_halo(): lax.ppermute(tail, axis, [(i, (i + 1) % count) for i in range(ends)])  32.7 us
    another operation x4, other arithmetic, local(): jax.scipy.linalg.solve_triangular(lower, window.astype(jnp.float32), lowe...  21.7 us
    dot_general x3, matrix products, contract(): jnp.einsum(form, values, matrix, precision=lax.Precision.HIGHEST, preferr...  21.1 us
    ppermute x5, waiting for transfers between devices, swap(): return lax.ppermute(values, axis, [(i, i ^ bit) for i in range(count)])  14 us
    ppermute x5, starting transfers between devices, swap(): return lax.ppermute(values, axis, [(i, i ^ bit) for i in range(count)])  8.71 us
    ppermute x2, starting transfers between devices, with_halo(): lax.ppermute(tail, axis, [(i, (i + 1) % count) for i in range(ends)])  7.34 us
    another operation x6, local copies, waits for them, and re-layouts  3.78 us
  transfers between devices with their start and end apart: 9, of which 8 were waited for; matrix products, arithmetic and copies ran while one was open for 1% of the time, Pallas kernels for 0%

profile of v1, /device:TPU:0, one launch (start us, length us, event | category | flops | bytes accessed | tf_op | source)
XLA Modules:
  0.0 160.1 jit_solution(9927196366269390847)
XLA Ops:
  0.6 0.0 copy-start
  0.6 1.6 %fusion.32 = (bf16[8,3,16,8,128]{4,3,2,1,0:T(8,128)(2,1)S(1)}, bf16[8,3,16,8,128]{4,3,2,1,0:T(8,128)(2,1)S(1)}) fusion(bf16[8,3,16,16,128]{4,3,2,1,0:T(8,128)(2,1)} %param.3), kind=kLoop, calls=%fused_computation.71 | loop fusion | bytes 3145728 | tf_op jit(solution)/shard_map/slice | solution.py:11
  2.3 4.9 %collective-permute-start = (bf16[8,3,16,8,128]{4,3,2,1,0:T(8,128)(2,1)S(1)}, bf16[8,3,16,8,128]{4,3,2,1,0:T(8,128)(2,1)S(1)}, u32[]{:S(2)}, u32[]{:S(2)}) collective-permute-start(bf16[8,3,16,8,128]{4,3,2,1,0:T(8,128)(2,1)S(1)} %get-tuple-element.28), channel_id=1, source_target_pairs={{0,2},{2,4},{4,6},{6,8},{8,10},{10,12},{12,14},{1,3},{3,5},{5,7},{... | collective-permute-start | bytes 2359304 | tf_op jit(solution)/shard_map/ppermute | solution.py:15
  7.2 1.3 collective-permute-start.1
  8.5 32.3 %collective-permute-done = bf16[8,3,16,8,128]{4,3,2,1,0:T(8,128)(2,1)S(1)} collective-permute-done((bf16[8,3,16,8,128]{4,3,2,1,0:T(8,128)(2,1)S(1)}, bf16[8,3,16,8,128]{4,3,2,1,0:T(8,128)(2,1)S(1)}, u32[]{:S(2)}, u32[]{:S(2)}) %collective-permute-start) | collective-permute-done | bytes 786464 | tf_op jit(solution)/shard_map/ppermute | solution.py:15
  40.8 0.1 constant_dynamic-update-slice_fusion.2
  40.9 0.0 copy-done
  40.9 0.4 constant_dynamic-update-slice_fusion.1
  41.3 0.0 collective-permute-done.1
  41.3 0.2 constant_dynamic-update-slice_fusion
  41.6 0.0 copy-start.1
  41.6 0.0 copy-start.4
  41.6 0.0 copy-start.2
  41.6 1.7 %fusion.31 = (bf16[8,3,8,32,128]{4,3,2,1,0:T(8,128)(2,1)}, bf16[8,3,8,32,128]{4,3,2,1,0:T(8,128)(2,1)S(1)}) fusion(bf16[8,3,16,32,128]{4,3,2,1,0:T(8,128)(2,1)S(1)} %constant_dynamic-update-slice_fusion), kind=kLoop, calls=%fused_computation.70 | loop fusion | bytes 6291456 | tf_op jit(solution)/shard_map/slice | solution.py:12
  43.3 0.4 copy-done.1
  43.7 2.5 %collective-permute-start.2 = (bf16[8,3,8,32,128]{4,3,2,1,0:T(8,128)(2,1)}, bf16[8,3,8,32,128]{4,3,2,1,0:T(8,128)(2,1)}, u32[]{:S(2)}, u32[]{:S(2)}) collective-permute-start(bf16[8,3,8,32,128]{4,3,2,1,0:T(8,128)(2,1)} %get-tuple-element.25), channel_id=1, source_target_pairs={{0,1},{2,3},{4,5},{6,7},{8,9},{10,11},{12,13},{14,15},{16,17},{18,... | collective-permute-start | bytes 4718600 | tf_op jit(solution)/shard_map/ppermute | solution.py:15
  46.2 1.3 collective-permute-start.3
  47.5 0.1 iota_subtract_fusion
  47.6 0.0 copy-done.4
  47.6 0.1 select_reduce_fusion.4
  47.7 0.1 subtract_add_fusion
  47.8 0.1 select_reduce_fusion
  47.9 0.0 copy-done.2
  47.9 0.1 constant_dynamic-update-slice_fusion.4
  47.9 0.4 collective-permute-done.2
  48.4 3.2 %collective-permute-done.3 = bf16[8,3,8,32,128]{4,3,2,1,0:T(8,128)(2,1)} collective-permute-done((bf16[8,3,8,32,128]{4,3,2,1,0:T(8,128)(2,1)S(1)}, bf16[8,3,8,32,128]{4,3,2,1,0:T(8,128)(2,1)}, u32[]{:S(2)}, u32[]{:S(2)}) %collective-permute-start.3) | collective-permute-done | bytes 1572896 | tf_op jit(solution)/shard_map/ppermute | solution.py:17
  51.6 7.1 %fusion.2 = f32[8,3,32,32,32]{4,3,2,1,0:T(8,128)S(1)} fusion(bf16[8,3,8,32,128]{4,3,2,1,0:T(8,128)(2,1)} %collective-permute-done.3, bf16[8,3,16,32,128]{4,3,2,1,0:T(8,128)(2,1)} %copy-done.1, bf16[8,3,8,32,128]{4,3,2,1,0:T(8,128)(2,1)} %collective-permute-done.2, f32[128,32]{0,1:T(8,128)S(1)} %select_reduce_fusion), kind=kOutput, calls=%fused_computation.4 | convolution fusion | flops 1214251008 | bytes 9453568 | tf_op jit(solution)/shard_map/ncyzx,xj->ncyzj/dot_general | solution.py:34
  58.7 13.1 %fusion = f32[4,8,3,32,32]{4,0,3,2,1:T(4,128)S(1)} fusion(f32[8,3,32,32,32]{4,3,2,1,0:T(8,128)S(1)} %fusion.2, f32[32,4]{0,1:T(4,128)S(1)} %get-tuple-element.12), kind=kOutput, calls=%fused_computation.2 | convolution fusion | flops 37748736 | bytes 3539456 | tf_op jit(solution)/shard_map/ncyzj,yk->nckzj/dot_general | solution.py:34
  71.8 0.9 fusion.14
  72.7 0.1 reshape.80
  72.8 0.0 copy-start.3
  72.9 0.4 convolution_multiply_fusion
  73.3 0.2 collective-permute-start.4
  73.5 1.2 collective-permute-done.4
  74.7 2.5 %collective-permute-start.5 = (f32[128,256]{0,1:T(8,128)S(1)}, f32[128,256]{0,1:T(8,128)S(1)}, u32[]{:S(2)}, u32[]{:S(2)}) collective-permute-start(f32[128,256]{0,1:T(8,128)S(1)} %dynamic-slice_add_fusion), channel_id=1, source_target_pairs={{0,2},{2,0},{4,6},{6,4},{8,10},{10,8},{12,14},{14,12},{1,3},{3,1},... | collective-permute-start | bytes 393224 | tf_op jit(solution)/shard_map/ppermute | solution.py:41
  77.3 3.8 %collective-permute-done.5 = f32[128,256]{0,1:T(8,128)S(1)} collective-permute-done((f32[128,256]{0,1:T(8,128)S(1)}, f32[128,256]{0,1:T(8,128)S(1)}, u32[]{:S(2)}, u32[]{:S(2)}) %collective-permute-start.5) | collective-permute-done | bytes 131104 | tf_op jit(solution)/shard_map/ppermute | solution.py:41
  81.1 2.8 %collective-permute-start.6 = (f32[128,256]{0,1:T(8,128)S(1)}, f32[128,256]{0,1:T(8,128)S(1)}, u32[]{:S(2)}, u32[]{:S(2)}) collective-permute-start(f32[128,256]{0,1:T(8,128)S(1)} %add.56), channel_id=1, source_target_pairs={{0,4},{2,6},{4,0},{6,2},{8,12},{10,14},{12,8},{14,10},{1,5},{3,7},... | collective-permute-start | bytes 393224 | tf_op jit(solution)/shard_map/ppermute | solution.py:41
  83.9 3.0 %collective-permute-done.6 = f32[128,256]{0,1:T(8,128)S(1)} collective-permute-done((f32[128,256]{0,1:T(8,128)S(1)}, f32[128,256]{0,1:T(8,128)S(1)}, u32[]{:S(2)}, u32[]{:S(2)}) %collective-permute-start.6) | collective-permute-done | bytes 131104 | tf_op jit(solution)/shard_map/ppermute | solution.py:41
  86.9 3.1 %collective-permute-start.7 = (f32[128,256]{0,1:T(8,128)S(1)}, f32[128,256]{0,1:T(8,128)S(1)}, u32[]{:S(2)}, u32[]{:S(2)}) collective-permute-start(f32[128,256]{0,1:T(8,128)S(1)} %add.57), channel_id=1, source_target_pairs={{0,8},{2,10},{4,12},{6,14},{8,0},{10,2},{12,4},{14,6},{1,9},{3,11}... | collective-permute-start | bytes 393224 | tf_op jit(solution)/shard_map/ppermute | solution.py:41
  90.0 4.6 %collective-permute-done.7 = f32[128,256]{0,1:T(8,128)S(1)} collective-permute-done((f32[128,256]{0,1:T(8,128)S(1)}, f32[128,256]{0,1:T(8,128)S(1)}, u32[]{:S(2)}, u32[]{:S(2)}) %collective-permute-start.7) | collective-permute-done | bytes 131104 | tf_op jit(solution)/shard_map/ppermute | solution.py:41
  94.7 0.1 collective-permute-start.8
  94.8 1.3 collective-permute-done.8
  96.1 0.1 copy.9
  96.3 11.7 %cholesky.50 = f32[128,128]{1,0:T(8,128)S(1)} custom-call(f32[128,128]{1,0:T(8,128)S(1)} %cholesky.118), custom_call_target="Cholesky" | custom-call | tf_op jit(solution)/shard_map/jit(cholesky)/cholesky | solution.py:82
  108.1 0.0 copy-done.3
  108.1 9.8 %custom-call.15 = f32[1,128,128]{1,2,0:T(8,128)S(1)} custom-call(f32[1,128,128]{2,1,0:T(8,128)S(1)} %get-tuple-element.34), custom_call_target="InvertDiagBlocksLowerTriangular" | custom-call | tf_op jit(solution)/shard_map/jit(cholesky)/cholesky | solution.py:82
  117.9 0.2 constant_dynamic-update-slice_fusion.5
  118.1 0.3 convolution_subtract_fusion.1
  118.4 12.0 %cholesky.105 = f32[128,128]{1,0:T(8,128)S(1)} custom-call(f32[128,128]{1,0:T(8,128)S(1)} %convolution_subtract_fusion.1), custom_call_target="Cholesky" | custom-call | tf_op jit(solution)/shard_map/jit(cholesky)/cholesky | solution.py:82
  130.4 0.6 compare_reduce_fusion
  132.3 0.7 fusion.20
  133.1 0.1 triangular_solve.44
  133.2 3.8 %while.1 = (s32[]{:T(128)}, f32[256,256]{1,0:T(8,128)S(1)}, s32[2,2]{1,0:T(2,128)S(1)}, f32[2,128,128]{2,1,0:T(8,128)S(1)}, s32[]{:T(128)}) while((s32[]{:T(128)}, f32[256,256]{1,0:T(8,128)S(1)}, s32[2,2]{1,0:T(2,128)S(1)}, f32[2,128,128]{2,1,0:T(8,128)S(1)}, s32[]{:T(128)}) %tuple.34), condition=%wide.while_cond, body=%wide.while_body.sunk | while | flops 2 | bytes 131181 | solution.py:83
  133.2 0.6 fusion.40
  133.7 1.3 bitcast_dynamic-update-slice_fusion.2
  135.1 0.6 fusion.40
  135.7 1.3 bitcast_dynamic-update-slice_fusion.2
  137.0 19.7 %custom-call.16 = f32[2,128,128]{1,2,0:T(8,128)S(1)} custom-call(f32[2,128,128]{2,1,0:T(8,128)S(1)} %get-tuple-element.10), custom_call_target="InvertDiagBlocksLowerTriangular" | custom-call | tf_op jit(solution)/shard_map/jit(_solve_triangular)/triangular_solve | solution.py:83
  156.7 0.5 fusion.17
  157.2 0.8 convolution_subtract_fusion
  158.0 0.8 fusion.22
  158.8 1.3 pad_maximum_fusion
  (20 shorter events, 0.3 us)
Async XLA Ops:
  0.6 40.3 %copy-start = (bf16[8,3,16,16,128]{4,3,2,1,0:T(8,128)(2,1)S(1)}, bf16[8,3,16,16,128]{4,3,2,1,0:T(8,128)(2,1)}, u32[]{:S(2)}) copy-start(bf16[8,3,16,16,128]{4,3,2,1,0:T(8,128)(2,1)} %param.3) | copy-start | bytes 4718596
  2.3 38.5 %collective-permute-start = (bf16[8,3,16,8,128]{4,3,2,1,0:T(8,128)(2,1)S(1)}, bf16[8,3,16,8,128]{4,3,2,1,0:T(8,128)(2,1)S(1)}, u32[]{:S(2)}, u32[]{:S(2)}) collective-permute-start(bf16[8,3,16,8,128]{4,3,2,1,0:T(8,128)(2,1)S(1)} %get-tuple-element.28), channel_id=1, source_target_pairs={{0,2},{2,4},{4,6},{6,8},{8,10},{10,12},{12,14},{1,3},{3,5},{5,7},{... | collective-permute-start | bytes 2359304 | tf_op jit(solution)/shard_map/ppermute | solution.py:15
  7.2 34.2 %collective-permute-start.1 = (bf16[8,3,16,8,128]{4,3,2,1,0:T(8,128)(2,1)S(1)}, bf16[8,3,16,8,128]{4,3,2,1,0:T(8,128)(2,1)S(1)}, u32[]{:S(2)}, u32[]{:S(2)}) collective-permute-start(bf16[8,3,16,8,128]{4,3,2,1,0:T(8,128)(2,1)S(1)} %get-tuple-element.27), channel_id=1, source_target_pairs={{2,0},{4,2},{6,4},{8,6},{10,8},{12,10},{14,12},{3,1},{5,3},{7,5},{... | collective-permute-start | bytes 2359304 | tf_op jit(solution)/shard_map/ppermute | solution.py:17
  41.6 2.2 %copy-start.1 = (bf16[8,3,16,32,128]{4,3,2,1,0:T(8,128)(2,1)}, bf16[8,3,16,32,128]{4,3,2,1,0:T(8,128)(2,1)S(1)}, u32[]{:S(2)}) copy-start(bf16[8,3,16,32,128]{4,3,2,1,0:T(8,128)(2,1)S(1)} %constant_dynamic-update-slice_fusion) | copy-start | bytes 9437188
  41.6 6.0 %copy-start.4 = (f32[3,17]{1,0:T(4,128)S(1)}, f32[3,17]{1,0:T(4,128)}, u32[]{:S(2)}) copy-start(f32[3,17]{1,0:T(4,128)} %param.5) | copy-start | bytes 616
  41.6 6.3 %copy-start.2 = (bf16[248,1536]{1,0:T(8,128)(2,1)S(1)}, bf16[248,1536]{1,0:T(8,128)(2,1)}, u32[]{:S(2)}) copy-start(bf16[248,1536]{1,0:T(8,128)(2,1)} %param.4) | copy-start | bytes 2285572
  43.7 4.6 %collective-permute-start.2 = (bf16[8,3,8,32,128]{4,3,2,1,0:T(8,128)(2,1)}, bf16[8,3,8,32,128]{4,3,2,1,0:T(8,128)(2,1)}, u32[]{:S(2)}, u32[]{:S(2)}) collective-permute-start(bf16[8,3,8,32,128]{4,3,2,1,0:T(8,128)(2,1)} %get-tuple-element.25), channel_id=1, source_target_pairs={{0,1},{2,3},{4,5},{6,7},{8,9},{10,11},{12,13},{14,15},{16,17},{18,... | collective-permute-start | bytes 4718600 | tf_op jit(solution)/shard_map/ppermute | solution.py:15
  46.2 5.4 %collective-permute-start.3 = (bf16[8,3,8,32,128]{4,3,2,1,0:T(8,128)(2,1)S(1)}, bf16[8,3,8,32,128]{4,3,2,1,0:T(8,128)(2,1)}, u32[]{:S(2)}, u32[]{:S(2)}) collective-permute-start(bf16[8,3,8,32,128]{4,3,2,1,0:T(8,128)(2,1)S(1)} %get-tuple-element.26), channel_id=1, source_target_pairs={{1,0},{3,2},{5,4},{7,6},{9,8},{11,10},{13,12},{15,14},{17,16},{19,... | collective-permute-start | bytes 4718600 | tf_op jit(solution)/shard_map/ppermute | solution.py:17
  72.8 35.2 %copy-start.3 = (bf16[8,1536]{1,0:T(8,128)(2,1)}, bf16[8,1536]{1,0:T(8,128)(2,1)S(1)}, u32[]{:S(2)}) copy-start(bf16[8,1536]{1,0:T(8,128)(2,1)S(1)} %reshape.80) | copy-start | bytes 73732
  73.3 1.4 collective-permute-start.4
  74.7 6.4 %collective-permute-start.5 = (f32[128,256]{0,1:T(8,128)S(1)}, f32[128,256]{0,1:T(8,128)S(1)}, u32[]{:S(2)}, u32[]{:S(2)}) collective-permute-start(f32[128,256]{0,1:T(8,128)S(1)} %dynamic-slice_add_fusion), channel_id=1, source_target_pairs={{0,2},{2,0},{4,6},{6,4},{8,10},{10,8},{12,14},{14,12},{1,3},{3,1},... | collective-permute-start | bytes 393224 | tf_op jit(solution)/shard_map/ppermute | solution.py:41
  81.1 5.8 %collective-permute-start.6 = (f32[128,256]{0,1:T(8,128)S(1)}, f32[128,256]{0,1:T(8,128)S(1)}, u32[]{:S(2)}, u32[]{:S(2)}) collective-permute-start(f32[128,256]{0,1:T(8,128)S(1)} %add.56), channel_id=1, source_target_pairs={{0,4},{2,6},{4,0},{6,2},{8,12},{10,14},{12,8},{14,10},{1,5},{3,7},... | collective-permute-start | bytes 393224 | tf_op jit(solution)/shard_map/ppermute | solution.py:41
  86.9 7.7 %collective-permute-start.7 = (f32[128,256]{0,1:T(8,128)S(1)}, f32[128,256]{0,1:T(8,128)S(1)}, u32[]{:S(2)}, u32[]{:S(2)}) collective-permute-start(f32[128,256]{0,1:T(8,128)S(1)} %add.57), channel_id=1, source_target_pairs={{0,8},{2,10},{4,12},{6,14},{8,0},{10,2},{12,4},{14,6},{1,9},{3,11}... | collective-permute-start | bytes 393224 | tf_op jit(solution)/shard_map/ppermute | solution.py:41
  94.7 1.4 collective-permute-start.8

commit v2 on v0

v2 whole, which is shorter than its diff:
```python
import functools

import jax
import jax.numpy as jnp
from jax import lax
from jax.experimental import pallas as pl
from jax.experimental.pallas import tpu as pltpu
from jax.sharding import PartitionSpec as P

F32 = jnp.float32
BF16 = jnp.bfloat16
TAPS = 17
LANES = 128
PANEL = 64


def iota(shape, dim):
    return lax.broadcasted_iota(jnp.int32, shape, dim)


def split2(values):
    high = values.astype(BF16)
    return high, (values - high.astype(F32)).astype(BF16)


def split3(values):
    high = values.astype(BF16)
    rest = values - high.astype(F32)
    middle = rest.astype(BF16)
    return high, middle, (rest - middle.astype(F32)).astype(BF16)


def weights_at(offset, taps_ref, row):
    total = jnp.zeros(offset.shape, F32)
    for tap in range(TAPS):
        total = jnp.where(offset == tap, taps_ref[row, tap], total)
    return total


def filter_kernel(place_ref, fine_ref, taps_ref, own_ref, ext_ref, send_ref, plane_ref, row_ref):
    first = place_ref[0] == 0
    fields = fine_ref.shape[0]
    slot, cell = iota((64, 256), 0), iota((64, 256), 1)
    span_slot, sect_slot = slot // 8, slot % 8
    span_cell = jnp.where(span_slot < 6, span_slot, span_slot - 8)
    sect_cell = jnp.where((sect_slot < 4) | first, sect_slot, sect_slot - 6)
    span_tap = cell % 16 - 4 * span_cell + 8
    sect_tap = jnp.where(sect_slot < 6, cell // 16 - 4 * sect_cell + 8, -1)
    plane = weights_at(span_tap, taps_ref, 1) * weights_at(sect_tap, taps_ref, 0)
    plane = jnp.concatenate(split2(plane), axis=0)
    for field in range(fields):
        both = jnp.dot(plane, fine_ref[field], preferred_element_type=F32)
        summed = both[:64] + both[64:]
        for s in range(8):
            plane_ref[s, 8 * field : 8 * field + 8, :] = summed[8 * s : 8 * s + 8]
    cell, lane = iota((LANES, LANES), 0), iota((LANES, LANES), 1)
    stream = weights_at(cell - 4 * (lane % 32) + 8, taps_ref, 2)
    parts = [
        jnp.concatenate([jnp.where(lane // 32 == s, part, 0.0) for s in range(4)], axis=0).astype(BF16)
        for part in (stream.astype(BF16).astype(F32), stream - stream.astype(BF16).astype(F32))
    ]
    matrix = jnp.concatenate([parts[0], parts[0], parts[1]], axis=0)
    for half in range(2):
        values = jnp.concatenate([plane_ref[4 * half + s] for s in range(4)], axis=1)
        high, low = split2(values)
        row_ref[half] = jnp.dot(
            jnp.concatenate([high, low, high], axis=1), matrix, preferred_element_type=F32
        )
    for comp in range(3):
        for k in range(4):
            rows = pl.ds(8 * comp + k, 8, stride=24)
            own_ref[4 * comp + k] = row_ref[0, rows, :]
            ext_ref[4 * comp + k] = row_ref[1, rows, :]
        for k in range(2):
            rows = pl.ds(8 * comp + 4 + k, 8, stride=24)
            for half in range(2):
                send_ref[6 * half + 2 * comp + k] = row_ref[half, rows, :]


def gram_kernel(
    total, place_ref, stored_ref, own_ref, partner_ref, left_ref, right_ref, coarse_ref, window_ref, kept_ref, sent_ref
):
    first = place_ref[0] == 0
    old = stored_ref.shape[0]
    lane = iota((8, LANES), 1)
    cells = []
    for comp in range(3):
        for k in range(4):
            at = 4 * comp + k
            value = own_ref[at] + jnp.where(lane < 64, left_ref[at], right_ref[at])
            here = first if k >= 2 else jnp.logical_not(first)
            cells.append(value + jnp.where(here, partner_ref[2 * comp + k % 2], 0.0))
    coarse = jnp.concatenate(cells, axis=1).astype(BF16)
    coarse_ref[...] = coarse
    window_ref[: old - 8, :] = stored_ref[: old - 8, :]
    window_ref[old - 8 :, :] = jnp.concatenate(
        [stored_ref[old - 8 :, :].astype(F32), coarse.astype(F32)], axis=0
    ).astype(BF16)
    window = window_ref[...]
    gram = lax.dot_general(window, window, (((1,), (1,)), ((), ())), preferred_element_type=F32) / total
    row, col = iota((LANES, LANES), 0), iota((LANES, LANES), 1)
    upper, lower = gram[:LANES, :LANES], gram[LANES:, LANES:]
    packed = jnp.where(row >= col, upper, lower)
    corner = jnp.sum(jnp.where(row == col, lower, 0.0), axis=0, keepdims=True)
    corner = jnp.broadcast_to(corner, (8, LANES))
    across = gram[:LANES, LANES:]
    kept_ref[:LANES] = jnp.where(first, packed, across)
    kept_ref[LANES:] = corner
    sent_ref[:LANES] = jnp.where(first, across, packed)
    sent_ref[LANES:] = corner


def eliminate(groups, at, lane):
    count = len(groups)
    width = groups[at].shape[1]
    wide = lambda column: jnp.concatenate([column] * (width // LANES), axis=1)
    spread = lambda row: jnp.broadcast_to(row, (8, row.shape[1]))
    sub = iota((8, LANES), 0)
    sub_wide = iota((8, width), 0)
    cols = {
        (j, g): jnp.broadcast_to(groups[g][:, lane + j : lane + j + 1], (8, LANES))
        for j in range(8)
        for g in range(at, count)
    }
    for k in range(8):
        scale = lax.rsqrt(spread(cols[k, at][k : k + 1, :]))
        row = spread(groups[at][k : k + 1, :]) * wide(scale)
        heads = {j: spread(cols[j, at][k : k + 1, :]) * scale for j in range(k + 1, 8)}
        for g in range(at, count):
            share = cols[k, g] * scale
            if g == at:
                share = jnp.where(sub > k, share, 0.0)
            for j in range(k + 1, 8):
                cols[j, g] = cols[j, g] - share * heads[j]
            updated = groups[g] - wide(share) * row
            groups[g] = jnp.where(sub_wide == k, row, updated) if g == at else updated
    return groups


def factor_kernel(place_ref, kept_ref, other_ref, window_ref, factor_ref, basis_ref, left_ref, inverse_ref, upper_ref):
    first = place_ref[0] == 0
    size = left_ref.shape[0]
    row, col = iota((LANES, LANES), 0), iota((LANES, LANES), 1)
    packed = jnp.where(first, kept_ref[:LANES], other_ref[:LANES])
    across = jnp.where(first, other_ref[:LANES], kept_ref[:LANES])
    corner = jnp.where(first, kept_ref[LANES : LANES + 1], other_ref[LANES : LANES + 1])
    turned = packed.T
    left_ref[:LANES, :LANES] = jnp.where(row >= col, packed, turned)
    left_ref[:LANES, LANES:] = across
    left_ref[LANES:, :LANES] = jnp.zeros((LANES, LANES), F32)
    left_ref[LANES:, LANES:] = jnp.where(
        row == col, jnp.broadcast_to(corner, (LANES, LANES)), jnp.where(row > col, turned, packed)
    )
    row, col = iota((size, size), 0), iota((size, size), 1)
    inverse_ref[...] = jnp.where(row == col, 1.0, 0.0)
    upper_ref[...] = jnp.zeros((size, size), F32)
    for begin in range(0, size, PANEL):
        end = begin + PANEL
        skip = 0 if begin < LANES else LANES
        reach = LANES if end <= LANES else size
        groups = [
            jnp.concatenate([left_ref[g : g + 8, skip:], inverse_ref[g : g + 8, :reach]], axis=1)
            for g in range(begin, end, 8)
        ]
        for g in range(PANEL // 8):
            groups = eliminate(groups, g, begin + 8 * g - skip)
        panel = jnp.concatenate(groups, axis=0)
        upper_ref[begin:end, skip:] = panel[:, : size - skip]
        inverse_ref[begin:end, :reach] = panel[:, size - skip :]
        if end < size:
            high, middle, low = split3(panel)
            right = jnp.concatenate([high, middle, high, low, high, middle], axis=0)
            high, middle, low = split3(panel[:, : size - skip].T[end - skip :, :])
            left = jnp.concatenate([high, high, middle, high, low, middle], axis=1)
            share = jnp.dot(left, right, preferred_element_type=F32)
            left_ref[end:, skip:] = left_ref[end:, skip:] - share[:, : size - skip]
            inverse_ref[end:, :reach] = inverse_ref[end:, :reach] - share[:, size - skip :]
    factor_ref[...] = jnp.where(row >= col, upper_ref[...].T, 0.0)
    high, low = split2(jnp.where(row >= col, inverse_ref[...], 0.0))
    left = jnp.concatenate([high, low], axis=1)
    wide = 512
    for at in range(0, window_ref.shape[1], wide):
        cells = window_ref[:, at : at + wide]
        basis_ref[:, at : at + wide] = jnp.dot(
            left, jnp.concatenate([cells, cells], axis=0), preferred_element_type=F32
        )


VMEM = pl.BlockSpec(memory_space=pltpu.VMEM)
SMEM = pl.BlockSpec(memory_space=pltpu.SMEM)
LIMIT = pltpu.CompilerParams(vmem_limit_bytes=48 * 2**20)


def shaped(shape, dtype=F32):
    return jax.ShapeDtypeStruct(shape, dtype)


def swap(values, axis, bit):
    count = lax.axis_size(axis)
    return lax.ppermute(values, axis, [(i, i ^ bit) for i in range(count)])


def shift(values, axis, step):
    count = lax.axis_size(axis)
    return lax.ppermute(values, axis, [(i, i + step) for i in range(count) if 0 <= i + step < count])


def sum_over_span(values):
    count = lax.axis_size("span")
    if count & (count - 1):
        return lax.psum(values, "span")
    bit = 1
    while bit < count:
        values = values + swap(values, "span", bit)
        bit *= 2
    return values


def local(fine_field, stored, filter_taps):
    snapshots, comps, cells_y, cells_z, cells_x = fine_field.shape
    assert (snapshots, comps, cells_y, cells_z, cells_x) == (8, 3, 16, 16, 128)
    assert lax.axis_size("sect") == 2
    old, rows_dev = stored.shape
    size = old + snapshots
    total = rows_dev * lax.axis_size("span") * lax.axis_size("sect")
    place = lax.axis_index("sect").astype(jnp.int32).reshape(1)
    fields = snapshots * comps
    own, ext, send = pl.pallas_call(
        filter_kernel,
        out_shape=[shaped((12, 8, LANES))] * 3,
        in_specs=[SMEM, VMEM, SMEM],
        out_specs=[VMEM] * 3,
        scratch_shapes=[pltpu.VMEM((8, 8 * fields, LANES), F32), pltpu.VMEM((2, 8 * fields, LANES), F32)],
        compiler_params=LIMIT,
        name="filter",
    )(place, fine_field.reshape(fields, cells_y * cells_z, cells_x), filter_taps)
    partner = swap(send, "sect", 1)
    own_share, ext_share = partner[:6], partner[6:].reshape(3, 2, 8, LANES)
    none = jnp.zeros_like(ext_share)
    ext_share = jnp.where(
        place[0] == 0,
        jnp.concatenate([none, ext_share], axis=1),
        jnp.concatenate([ext_share, none], axis=1),
    )
    ext = ext + ext_share.reshape(12, 8, LANES)
    from_left = shift(ext, "span", 1)
    from_right = shift(ext, "span", -1)
    coarse_new, window, kept, sent = pl.pallas_call(
        functools.partial(gram_kernel, total),
        out_shape=[
            shaped((snapshots, rows_dev), BF16),
            shaped((size, rows_dev), BF16),
            shaped((LANES + 8, LANES)),
            shaped((LANES + 8, LANES)),
        ],
        in_specs=[SMEM] + [VMEM] * 5,
        out_specs=[VMEM] * 4,
        compiler_params=LIMIT,
        name="gram",
    )(place, stored, own, own_share, from_left, from_right)
    kept = sum_over_span(kept + swap(sent, "sect", 1))
    other = swap(kept, "sect", 1)
    factor, basis = pl.pallas_call(
        factor_kernel,
        out_shape=[shaped((size, size)), shaped((size, rows_dev))],
        in_specs=[SMEM] + [VMEM] * 3,
        out_specs=[VMEM] * 2,
        scratch_shapes=[pltpu.VMEM((size, size), F32)] * 3,
        compiler_params=LIMIT,
        name="factor",
    )(place, kept, other, window)
    return (coarse_new, factor, basis)


def solution(mesh):
    in_specs = (P("case", None, "sect", "span", None), P(None, ("case", "span", "sect")), P())
    out_specs = (
        P(None, ("case", "span", "sect")),
        P("case", None),
        P(None, ("case", "span", "sect")),
    )
    return jax.shard_map(local, mesh=mesh, in_specs=in_specs, out_specs=out_specs, check_vma=False)
```

time: 243 us -> 44.5 us (0.18); the launches traced: 240 us -> 44.3 us
  waiting for transfers between devices: 127 us -> 12.2 us
  other arithmetic: 57.2 us -> 0.06 us
  matrix products: 22.8 us -> 0 us
  between operations: 16 us -> 0.7 us
  Pallas kernels: 0 us -> 12.3 us
  starting transfers between devices: 9.08 us -> 17 us
  local copies, waits for them, and re-layouts: 8.3 us -> 2.09 us
    psum x1 -> x0, waiting for transfers between devices: 91.1 us -> none  [local(): gram = lax.psum(local_gram, ('span', 'sect'))]
    another operation x10 -> x0, other arithmetic: 55.9 us -> none  [the longest x6 34.2 us: local(): lower = jnp.linalg.cholesky(gram)]
    ppermute x4 -> x8, waiting for transfers between devices: 35.7 us -> 12.2 us  [the longest x6 10.5 us: swap(): return lax.ppermute(values, axis, [(i, i ^ bit) for i in range(count)])]
    dot_general x4 -> x0, matrix products: 20.2 us -> none  [the longest x3 19.1 us: contract(): jnp.einsum(form, values, matrix, precision=lax.Precision.HIGHEST, preferr...]
    pallas_call x0 -> x3, Pallas kernels: none -> 12.3 us  [the longest x1 9.78 us: local(): pl.pallas_call(factor_kernel, out_shape=[shaped((size, size)), shaped((si...]
    ppermute x4 -> x8, starting transfers between devices: 9.04 us -> 17 us  [the longest x6 10.3 us: swap(): return lax.ppermute(values, axis, [(i, i ^ bit) for i in range(count)])]
    another operation x9 -> x0, local copies, waits for them, and re-layouts: 4.15 us -> none
    another operation x5 -> x0, matrix products: 2.63 us -> none  [the longest x3 2.16 us: local(): jax.scipy.linalg.solve_triangular(lower, window.astype(jnp.float32), lowe...]
  transfers between devices with their start and end apart: 5 -> 8, of which waited for: 4 -> 8; matrix products, arithmetic and copies ran while one was open for 0% -> 0% of each run, Pallas kernels for 0% -> 0%
where the time goes in v2:
time: 44.5 us; the launch traced here: 44.3 us
  starting transfers between devices  17 us (38%)
  Pallas kernels  12.3 us (28%)
  waiting for transfers between devices  12.2 us (27%)
  local copies, waits for them, and re-layouts  2.09 us (5%)
  between operations  0.7 us (2%)
    ppermute x6, waiting for transfers between devices, swap(): return lax.ppermute(values, axis, [(i, i ^ bit) for i in range(count)])  10.5 us
    ppermute x6, starting transfers between devices, swap(): return lax.ppermute(values, axis, [(i, i ^ bit) for i in range(count)])  10.3 us
    pallas_call x1, Pallas kernels, local(): pl.pallas_call(factor_kernel, out_shape=[shaped((size, size)), shaped((si...  9.78 us
    ppermute x2, starting transfers between devices, shift(): lax.ppermute(values, axis, [(i, i + step) for i in range(count) if 0 <= i...  6.66 us
    unnamed x6, local copies, waits for them, and re-layouts  2.09 us
    ppermute x2, waiting for transfers between devices, shift(): lax.ppermute(values, axis, [(i, i + step) for i in range(count) if 0 <= i...  1.73 us
    pallas_call x1, Pallas kernels, local(): pl.pallas_call(filter_kernel, out_shape=[shaped((12, 8, LANES))] * 3, in_...  1.72 us
  transfers between devices with their start and end apart: 8, of which 8 were waited for; matrix products, arithmetic and copies ran while one was open for 0% of the time, Pallas kernels for 0%

profile of v2, /device:TPU:0, one launch (start us, length us, event | category | flops | bytes accessed | tf_op | source)
XLA Modules:
  0.0 44.3 jit_solution(17717798660325594232)
XLA Ops:
  0.6 0.0 copy-start
  0.6 1.4 %copy-done = bf16[8,3,16,16,128]{4,3,2,1,0:T(8,128)(2,1)S(1)} copy-done((bf16[8,3,16,16,128]{4,3,2,1,0:T(8,128)(2,1)S(1)}, bf16[8,3,16,16,128]{4,3,2,1,0:T(8,128)(2,1)}, u32[]{:S(2)}) %copy-start) | copy-done | bytes 1572888
  2.0 0.0 copy-start.2
  2.0 0.7 %copy-done.2 = f32[3,17]{1,0:T(4,128)S(1)} copy-done((f32[3,17]{1,0:T(4,128)S(1)}, f32[3,17]{1,0:T(4,128)}, u32[]{:S(2)}) %copy-start.2) | copy-done | bytes 228
  2.7 0.0 copy-start.1
  2.7 1.7 %filter.1 = (f32[12,8,128]{2,1,0:T(8,128)S(1)}, f32[12,8,128]{2,1,0:T(8,128)S(1)}, f32[12,8,128]{2,1,0:T(8,128)S(1)}) custom-call(s32[1]{0:T(128)} %bitcast.place_ref, bf16[24,256,128]{2,1,0:T(8,128)(2,1)S(1)} %bitcast.5, f32[3,17]{1,0:T(4,128)S(1)} %copy-done.2), custom_call_target="tpu_custom_call" | custom-call | tf_op jit(solution)/shard_map/filter/pallas_call | solution.py:228
  4.5 0.5 %collective-permute-start = (f32[12,8,128]{2,1,0:T(8,128)S(1)}, f32[12,8,128]{2,1,0:T(8,128)S(1)}, u32[]{:S(2)}, u32[]{:S(2)}) collective-permute-start(f32[12,8,128]{2,1,0:T(8,128)S(1)} %get-tuple-element.13), channel_id=1, source_target_pairs={{0,1},{1,0},{2,3},{3,2},{4,5},{5,4},{6,7},{7,6},{8,9},{9,8},{10,11... | collective-permute-start | bytes 147464 | tf_op jit(solution)/shard_map/ppermute | solution.py:200
  5.0 0.9 %collective-permute-done = f32[12,8,128]{2,1,0:T(8,128)S(1)} collective-permute-done((f32[12,8,128]{2,1,0:T(8,128)S(1)}, f32[12,8,128]{2,1,0:T(8,128)S(1)}, u32[]{:S(2)}, u32[]{:S(2)}) %collective-permute-start) | collective-permute-done | bytes 49184 | tf_op jit(solution)/shard_map/ppermute | solution.py:200
  5.9 1.3 %collective-permute-start.2 = (f32[12,8,128]{2,1,0:T(8,128)S(1)}, f32[12,8,128]{2,1,0:T(8,128)S(1)}, u32[]{:S(2)}, u32[]{:S(2)}) collective-permute-start(f32[12,8,128]{2,1,0:T(8,128)S(1)} %bitcast_add_fusion), channel_id=1, source_target_pairs={{2,0},{4,2},{6,4},{8,6},{10,8},{12,10},{14,12},{3,1},{5,3},{7,5},{... | collective-permute-start | bytes 147464 | tf_op jit(solution)/shard_map/ppermute | solution.py:205
  7.2 5.4 %collective-permute-start.1 = (f32[12,8,128]{2,1,0:T(8,128)S(1)}, f32[12,8,128]{2,1,0:T(8,128)S(1)}, u32[]{:S(2)}, u32[]{:S(2)}) collective-permute-start(f32[12,8,128]{2,1,0:T(8,128)S(1)} %bitcast_add_fusion), channel_id=1, source_target_pairs={{0,2},{2,4},{4,6},{6,8},{8,10},{10,12},{12,14},{1,3},{3,5},{5,7},{... | collective-permute-start | bytes 147464 | tf_op jit(solution)/shard_map/ppermute | solution.py:205
  12.6 0.1 collective-permute-done.2.right_ref
  12.7 1.6 %collective-permute-done.1.left_ref = f32[12,8,128]{2,1,0:T(8,128)S(1)} collective-permute-done((f32[12,8,128]{2,1,0:T(8,128)S(1)}, f32[12,8,128]{2,1,0:T(8,128)S(1)}, u32[]{:S(2)}, u32[]{:S(2)}) %collective-permute-start.1) | collective-permute-done | bytes 49184 | tf_op jit(solution)/shard_map/ppermute | solution.py:205
  14.3 0.0 copy-done.1
  14.3 0.8 %gram.1 = (bf16[8,1536]{1,0:T(8,128)(2,1)}, bf16[256,1536]{1,0:T(8,128)(2,1)S(1)}, f32[136,128]{1,0:T(8,128)S(1)}, f32[136,128]{1,0:T(8,128)S(1)}) custom-call(s32[1]{0:T(128)} %bitcast.place_ref, bf16[248,1536]{1,0:T(8,128)(2,1)S(1)} %copy-done.1, f32[12,8,128]{2,1,0:T(8,128)S(1)} %get-tuple-element.12.own_ref, ...), custom_call_target="tpu_custom_call" | custom-call | tf_op jit(solution)/shard_map/gram/pallas_call | solution.py:248
  15.1 0.0 collective-permute-start.3
  15.1 1.3 %collective-permute-done.3 = f32[136,128]{1,0:T(8,128)S(1)} collective-permute-done((f32[136,128]{1,0:T(8,128)S(1)}, f32[136,128]{1,0:T(8,128)S(1)}, u32[]{:S(2)}, u32[]{:S(2)}) %collective-permute-start.3) | collective-permute-done | bytes 69664 | tf_op jit(solution)/shard_map/ppermute | solution.py:200
  16.4 3.0 %collective-permute-start.4 = (f32[136,128]{1,0:T(8,128)S(1)}, f32[136,128]{1,0:T(8,128)S(1)}, u32[]{:S(2)}, u32[]{:S(2)}) collective-permute-start(f32[136,128]{1,0:T(8,128)S(1)} %add.20), channel_id=1, source_target_pairs={{0,2},{2,0},{4,6},{6,4},{8,10},{10,8},{12,14},{14,12},{1,3},{3,1},... | collective-permute-start | bytes 208904 | tf_op jit(solution)/shard_map/ppermute | solution.py:200
  19.3 2.5 %collective-permute-done.4 = f32[136,128]{1,0:T(8,128)S(1)} collective-permute-done((f32[136,128]{1,0:T(8,128)S(1)}, f32[136,128]{1,0:T(8,128)S(1)}, u32[]{:S(2)}, u32[]{:S(2)}) %collective-permute-start.4) | collective-permute-done | bytes 69664 | tf_op jit(solution)/shard_map/ppermute | solution.py:200
  21.9 3.6 %collective-permute-start.5 = (f32[136,128]{1,0:T(8,128)S(1)}, f32[136,128]{1,0:T(8,128)S(1)}, u32[]{:S(2)}, u32[]{:S(2)}) collective-permute-start(f32[136,128]{1,0:T(8,128)S(1)} %add.21), channel_id=1, source_target_pairs={{0,4},{2,6},{4,0},{6,2},{8,12},{10,14},{12,8},{14,10},{1,5},{3,7},... | collective-permute-start | bytes 208904 | tf_op jit(solution)/shard_map/ppermute | solution.py:200
  25.5 2.3 %collective-permute-done.5 = f32[136,128]{1,0:T(8,128)S(1)} collective-permute-done((f32[136,128]{1,0:T(8,128)S(1)}, f32[136,128]{1,0:T(8,128)S(1)}, u32[]{:S(2)}, u32[]{:S(2)}) %collective-permute-start.5) | collective-permute-done | bytes 69664 | tf_op jit(solution)/shard_map/ppermute | solution.py:200
  27.8 3.1 %collective-permute-start.6 = (f32[136,128]{1,0:T(8,128)S(1)}, f32[136,128]{1,0:T(8,128)S(1)}, u32[]{:S(2)}, u32[]{:S(2)}) collective-permute-start(f32[136,128]{1,0:T(8,128)S(1)} %add.22), channel_id=1, source_target_pairs={{0,8},{2,10},{4,12},{6,14},{8,0},{10,2},{12,4},{14,6},{1,9},{3,11}... | collective-permute-start | bytes 208904 | tf_op jit(solution)/shard_map/ppermute | solution.py:200
  30.9 2.3 %collective-permute-done.6 = f32[136,128]{1,0:T(8,128)S(1)} collective-permute-done((f32[136,128]{1,0:T(8,128)S(1)}, f32[136,128]{1,0:T(8,128)S(1)}, u32[]{:S(2)}, u32[]{:S(2)}) %collective-permute-start.6) | collective-permute-done | bytes 69664 | tf_op jit(solution)/shard_map/ppermute | solution.py:200
  33.2 0.1 collective-permute-start.7
  33.3 1.2 %collective-permute-done.7.other_ref = f32[136,128]{1,0:T(8,128)S(1)} collective-permute-done((f32[136,128]{1,0:T(8,128)S(1)}, f32[136,128]{1,0:T(8,128)S(1)}, u32[]{:S(2)}, u32[]{:S(2)}) %collective-permute-start.7) | collective-permute-done | bytes 69664 | tf_op jit(solution)/shard_map/ppermute | solution.py:200
  34.5 9.8 %factor.1 = (f32[256,256]{1,0:T(8,128)}, f32[256,1536]{1,0:T(8,128)}) custom-call(s32[1]{0:T(128)} %bitcast.place_ref, f32[136,128]{1,0:T(8,128)S(1)} %add.23.kept_ref, f32[136,128]{1,0:T(8,128)S(1)} %collective-permute-done.7.other_ref, bf16[256,1536]{1,0:T(8,128)(2,1)S(1)} %get-tuple-element.18.window_ref), custom_call_target="tpu_custom_call" | custom-call | tf_op jit(solution)/shard_map/factor/pallas_call | solution.py:263
  (7 shorter events, 0.1 us)
Async XLA Ops:
  0.6 1.4 %copy-start = (bf16[8,3,16,16,128]{4,3,2,1,0:T(8,128)(2,1)S(1)}, bf16[8,3,16,16,128]{4,3,2,1,0:T(8,128)(2,1)}, u32[]{:S(2)}) copy-start(bf16[8,3,16,16,128]{4,3,2,1,0:T(8,128)(2,1)} %param.3) | copy-start | bytes 4718596
  2.0 0.7 %copy-start.2 = (f32[3,17]{1,0:T(4,128)S(1)}, f32[3,17]{1,0:T(4,128)}, u32[]{:S(2)}) copy-start(f32[3,17]{1,0:T(4,128)} %taps_ref.1) | copy-start | bytes 616
  2.7 11.6 %copy-start.1 = (bf16[248,1536]{1,0:T(8,128)(2,1)S(1)}, bf16[248,1536]{1,0:T(8,128)(2,1)}, u32[]{:S(2)}) copy-start(bf16[248,1536]{1,0:T(8,128)(2,1)} %stored_ref.1) | copy-start | bytes 2285572
  4.5 1.4 %collective-permute-start = (f32[12,8,128]{2,1,0:T(8,128)S(1)}, f32[12,8,128]{2,1,0:T(8,128)S(1)}, u32[]{:S(2)}, u32[]{:S(2)}) collective-permute-start(f32[12,8,128]{2,1,0:T(8,128)S(1)} %get-tuple-element.13), channel_id=1, source_target_pairs={{0,1},{1,0},{2,3},{3,2},{4,5},{5,4},{6,7},{7,6},{8,9},{9,8},{10,11... | collective-permute-start | bytes 147464 | tf_op jit(solution)/shard_map/ppermute | solution.py:200
  5.9 6.8 %collective-permute-start.2 = (f32[12,8,128]{2,1,0:T(8,128)S(1)}, f32[12,8,128]{2,1,0:T(8,128)S(1)}, u32[]{:S(2)}, u32[]{:S(2)}) collective-permute-start(f32[12,8,128]{2,1,0:T(8,128)S(1)} %bitcast_add_fusion), channel_id=1, source_target_pairs={{2,0},{4,2},{6,4},{8,6},{10,8},{12,10},{14,12},{3,1},{5,3},{7,5},{... | collective-permute-start | bytes 147464 | tf_op jit(solution)/shard_map/ppermute | solution.py:205
  7.2 7.1 %collective-permute-start.1 = (f32[12,8,128]{2,1,0:T(8,128)S(1)}, f32[12,8,128]{2,1,0:T(8,128)S(1)}, u32[]{:S(2)}, u32[]{:S(2)}) collective-permute-start(f32[12,8,128]{2,1,0:T(8,128)S(1)} %bitcast_add_fusion), channel_id=1, source_target_pairs={{0,2},{2,4},{4,6},{6,8},{8,10},{10,12},{12,14},{1,3},{3,5},{5,7},{... | collective-permute-start | bytes 147464 | tf_op jit(solution)/shard_map/ppermute | solution.py:205
  15.1 1.3 %collective-permute-start.3 = (f32[136,128]{1,0:T(8,128)S(1)}, f32[136,128]{1,0:T(8,128)S(1)}, u32[]{:S(2)}, u32[]{:S(2)}) collective-permute-start(f32[136,128]{1,0:T(8,128)S(1)} %get-tuple-element.17), channel_id=1, source_target_pairs={{0,1},{1,0},{2,3},{3,2},{4,5},{5,4},{6,7},{7,6},{8,9},{9,8},{10,11... | collective-permute-start | bytes 208904 | tf_op jit(solution)/shard_map/ppermute | solution.py:200
  16.4 5.5 %collective-permute-start.4 = (f32[136,128]{1,0:T(8,128)S(1)}, f32[136,128]{1,0:T(8,128)S(1)}, u32[]{:S(2)}, u32[]{:S(2)}) collective-permute-start(f32[136,128]{1,0:T(8,128)S(1)} %add.20), channel_id=1, source_target_pairs={{0,2},{2,0},{4,6},{6,4},{8,10},{10,8},{12,14},{14,12},{1,3},{3,1},... | collective-permute-start | bytes 208904 | tf_op jit(solution)/shard_map/ppermute | solution.py:200
  21.9 5.9 %collective-permute-start.5 = (f32[136,128]{1,0:T(8,128)S(1)}, f32[136,128]{1,0:T(8,128)S(1)}, u32[]{:S(2)}, u32[]{:S(2)}) collective-permute-start(f32[136,128]{1,0:T(8,128)S(1)} %add.21), channel_id=1, source_target_pairs={{0,4},{2,6},{4,0},{6,2},{8,12},{10,14},{12,8},{14,10},{1,5},{3,7},... | collective-permute-start | bytes 208904 | tf_op jit(solution)/shard_map/ppermute | solution.py:200
  27.8 5.4 %collective-permute-start.6 = (f32[136,128]{1,0:T(8,128)S(1)}, f32[136,128]{1,0:T(8,128)S(1)}, u32[]{:S(2)}, u32[]{:S(2)}) collective-permute-start(f32[136,128]{1,0:T(8,128)S(1)} %add.22), channel_id=1, source_target_pairs={{0,8},{2,10},{4,12},{6,14},{8,0},{10,2},{12,4},{14,6},{1,9},{3,11}... | collective-permute-start | bytes 208904 | tf_op jit(solution)/shard_map/ppermute | solution.py:200
  33.2 1.3 %collective-permute-start.7 = (f32[136,128]{1,0:T(8,128)S(1)}, f32[136,128]{1,0:T(8,128)S(1)}, u32[]{:S(2)}, u32[]{:S(2)}) collective-permute-start(f32[136,128]{1,0:T(8,128)S(1)} %add.23.kept_ref), channel_id=1, source_target_pairs={{0,1},{1,0},{2,3},{3,2},{4,5},{5,4},{6,7},{7,6},{8,9},{9,8},{10,11... | collective-permute-start | bytes 208904 | tf_op jit(solution)/shard_map/ppermute | solution.py:200

commit v3 on v2

--- a/solution.py
+++ b/solution.py
@@ -12,6 +12,8 @@
 TAPS = 17
 LANES = 128
 PANEL = 64
+NEAR = 8
+FAR = 8
 
 
 def iota(shape, dim):
@@ -110,35 +112,52 @@
     sent_ref[LANES:] = corner
 
 
-def eliminate(groups, at, lane):
+def eliminate(groups, at, lane, none, scale_ref):
     count = len(groups)
     width = groups[at].shape[1]
     wide = lambda column: jnp.concatenate([column] * (width // LANES), axis=1)
-    spread = lambda row: jnp.broadcast_to(row, (8, row.shape[1]))
+    spread = lambda values, k: jnp.broadcast_to(values[k : k + 1, :], (8, values.shape[1]))
+    column = lambda g, j: jnp.broadcast_to(groups[g][:, lane + j : lane + j + 1], (8, LANES))
     sub = iota((8, LANES), 0)
-    sub_wide = iota((8, width), 0)
-    cols = {
-        (j, g): jnp.broadcast_to(groups[g][:, lane + j : lane + j + 1], (8, LANES))
-        for j in range(8)
-        for g in range(at, count)
-    }
-    for k in range(8):
-        scale = lax.rsqrt(spread(cols[k, at][k : k + 1, :]))
-        row = spread(groups[at][k : k + 1, :]) * wide(scale)
-        heads = {j: spread(cols[j, at][k : k + 1, :]) * scale for j in range(k + 1, 8)}
-        for g in range(at, count):
-            share = cols[k, g] * scale
-            if g == at:
-                share = jnp.where(sub > k, share, 0.0)
-            for j in range(k + 1, 8):
-                cols[j, g] = cols[j, g] - share * heads[j]
-            updated = groups[g] - wide(share) * row
-            groups[g] = jnp.where(sub_wide == k, row, updated) if g == at else updated
+    cols = {(j, g): column(g, j) for g in (at, at + 1) for j in range(8 * (g - at) + 8)}
+    for g in (at, at + 1):
+        cols[0, g] = cols[0, g] + none
+    for k in range(16):
+        home, k_sub = at + k // 8, k % 8
+        for g in range(at + 2, count):
+            step = NEAR if g < at + 4 else FAR
+            if k % step == 0:
+                for j in range(k, k + step):
+                    cols[j, g] = column(g, j)
+        scale = lax.rsqrt(spread(cols[k, home], k_sub))
+        square = scale * scale
+        scale_ref[8 * home + k_sub : 8 * home + k_sub + 1, :] = scale[k_sub : k_sub + 1, :]
+        share = {g: cols[k, g] * square for g in range(home, count)}
+        share[home] = jnp.where(sub > k_sub, share[home], 0.0)
+        for j in range(k + 1, 16):
+            j_home, j_sub = at + j // 8, j % 8
+            head = spread(cols[k, j_home], j_sub)
+            for g in range(j_home, count):
+                step = 16 if g < at + 2 else NEAR if g < at + 4 else FAR
+                if j // step == k // step:
+                    if j == k + 1 and g == j_home:
+                        cols[j, g] = cols[j, g] - (cols[k, g] * head) * square
+                    else:
+                        cols[j, g] = cols[j, g] - share[g] * head
+        row = spread(groups[home], k_sub)
+        for g in range(home, count):
+            groups[g] = groups[g] - wide(share[g]) * row
+    for g in (at, at + 1):
+        groups[g] = groups[g] * wide(scale_ref[8 * g : 8 * g + 8, :])
     return groups
 
 
-def factor_kernel(place_ref, kept_ref, other_ref, window_ref, factor_ref, basis_ref, left_ref, inverse_ref, upper_ref):
+def factor_kernel(
+    place_ref, kept_ref, other_ref, window_ref, factor_hbm, basis_hbm,
+    left_ref, inverse_ref, upper_ref, factor_ref, basis_ref, scale_ref, sems,
+):
     first = place_ref[0] == 0
+    none = jnp.full((8, LANES), jnp.minimum(place_ref[0], 0).astype(F32))
     size = left_ref.shape[0]
     row, col = iota((LANES, LANES), 0), iota((LANES, LANES), 1)
     packed = jnp.where(first, kept_ref[:LANES], other_ref[:LANES])
@@ -151,9 +170,14 @@
     left_ref[LANES:, LANES:] = jnp.where(
         row == col, jnp.broadcast_to(corner, (LANES, LANES)), jnp.where(row > col, turned, packed)
     )
-    row, col = iota((size, size), 0), iota((size, size), 1)
-    inverse_ref[...] = jnp.where(row == col, 1.0, 0.0)
+    inverse_ref[...] = jnp.where(iota((size, size), 0) == iota((size, size), 1), 1.0, 0.0)
     upper_ref[...] = jnp.zeros((size, size), F32)
+    copies = []
+
+    def send(source, target, begin, end):
+        copies.append(pltpu.make_async_copy(source.at[begin:end], target.at[begin:end], sems.at[len(copies)]))
+        copies[-1].start()
+
     for begin in range(0, size, PANEL):
         end = begin + PANEL
         skip = 0 if begin < LANES else LANES
@@ -162,28 +186,64 @@
             jnp.concatenate([left_ref[g : g + 8, skip:], inverse_ref[g : g + 8, :reach]], axis=1)
             for g in range(begin, end, 8)
         ]
-        for g in range(PANEL // 8):
-            groups = eliminate(groups, g, begin + 8 * g - skip)
+        for g in range(0, PANEL // 8, 2):
+            groups = eliminate(groups, g, begin + 8 * g - skip, none, scale_ref)
         panel = jnp.concatenate(groups, axis=0)
         upper_ref[begin:end, skip:] = panel[:, : size - skip]
-        inverse_ref[begin:end, :reach] = panel[:, size - skip :]
         if end < size:
             high, middle, low = split3(panel)
             right = jnp.concatenate([high, middle, high, low, high, middle], axis=0)
-            high, middle, low = split3(panel[:, : size - skip].T[end - skip :, :])
-            left = jnp.concatenate([high, high, middle, high, low, middle], axis=1)
-            share = jnp.dot(left, right, preferred_element_type=F32)
-            left_ref[end:, skip:] = left_ref[end:, skip:] - share[:, : size - skip]
-            inverse_ref[end:, :reach] = inverse_ref[end:, :reach] - share[:, size - skip :]
-    factor_ref[...] = jnp.where(row >= col, upper_ref[...].T, 0.0)
-    high, low = split2(jnp.where(row >= col, inverse_ref[...], 0.0))
-    left = jnp.concatenate([high, low], axis=1)
-    wide = 512
-    for at in range(0, window_ref.shape[1], wide):
-        cells = window_ref[:, at : at + wide]
-        basis_ref[:, at : at + wide] = jnp.dot(
-            left, jnp.concatenate([cells, cells], axis=0), preferred_element_type=F32
+            lost = LANES if end == LANES else skip
+            turned = panel[:, lost - skip : size - skip]
+            turned = jnp.concatenate([turned, turned], axis=0).T[end - lost :, :]
+            high = turned.astype(BF16).astype(F32)
+            rest = turned - high
+            middle = rest.astype(BF16).astype(F32)
+            low = rest - middle
+            early = iota(turned.shape, 1) < PANEL
+            left = jnp.concatenate(
+                [high, jnp.where(early, middle, high), jnp.where(early, low, middle)], axis=1
+            ).astype(BF16)
+            apart = lost - skip
+            near = jnp.dot(left[:PANEL], right[:, apart : size - skip], preferred_element_type=F32)
+            left_ref[end : end + PANEL, lost:] = left_ref[end : end + PANEL, lost:] - near
+            near = jnp.dot(left[:PANEL], right[:, size - skip :], preferred_element_type=F32)
+            inverse_ref[end : end + PANEL, :reach] = inverse_ref[end : end + PANEL, :reach] - near
+            if end + PANEL < size:
+                far = jnp.dot(left[PANEL:], right[:, apart:], preferred_element_type=F32)
+                left_ref[end + PANEL :, lost:] = left_ref[end + PANEL :, lost:] - far[:, : size - lost]
+                inverse_ref[end + PANEL :, :reach] = inverse_ref[end + PANEL :, :reach] - far[:, size - lost :]
+        inverse = panel[:, size - skip :]
+        inverse = jnp.where(iota(inverse.shape, 0) + begin >= iota(inverse.shape, 1), inverse, 0.0)
+        high, low = split2(inverse)
+        cells = window_ref[:reach, :]
+        basis_ref[begin:end, :] = jnp.dot(
+            jnp.concatenate([high, low], axis=1), jnp.concatenate([cells, cells], axis=0), preferred_element_type=F32
         )
+        send(basis_ref, basis_hbm, begin, end)
+        if end == LANES:
+            factor_ref[:LANES, :LANES] = jnp.where(row >= col, upper_ref[:LANES, :LANES].T, 0.0)
+            factor_ref[:LANES, LANES:] = jnp.zeros((LANES, LANES), F32)
+            factor_ref[LANES:, :LANES] = upper_ref[:LANES, LANES:].T
+            send(factor_ref, factor_hbm, 0, LANES)
+    factor_ref[LANES:, LANES:] = jnp.where(row >= col, upper_ref[LANES:, LANES:].T, 0.0)
+    send(factor_ref, factor_hbm, LANES, size)
+    for copy in copies:
+        copy.wait()
+
+
+def factorise(place, kept, other, window):
+    size, rows_dev = window.shape
+    return pl.pallas_call(
+        factor_kernel,
+        out_shape=[shaped((size, size)), shaped((size, rows_dev))],
+        in_specs=[SMEM] + [VMEM] * 3,
+        out_specs=[pl.BlockSpec(memory_space=pl.ANY)] * 2,
+        scratch_shapes=[pltpu.VMEM((size, size), F32)] * 4
+        + [pltpu.VMEM((size, rows_dev), F32), pltpu.VMEM((PANEL, LANES), F32), pltpu.SemaphoreType.DMA((size // PANEL + 2,))],
+        compiler_params=LIMIT,
+        name="factor",
+    )(place, kept, other, window)
 
 
 VMEM = pl.BlockSpec(memory_space=pltpu.VMEM)
@@ -260,15 +320,7 @@
     )(place, stored, own, own_share, from_left, from_right)
     kept = sum_over_span(kept + swap(sent, "sect", 1))
     other = swap(kept, "sect", 1)
-    factor, basis = pl.pallas_call(
-        factor_kernel,
-        out_shape=[shaped((size, size)), shaped((size, rows_dev))],
-        in_specs=[SMEM] + [VMEM] * 3,
-        out_specs=[VMEM] * 2,
-        scratch_shapes=[pltpu.VMEM((size, size), F32)] * 3,
-        compiler_params=LIMIT,
-        name="factor",
-    )(place, kept, other, window)
+    factor, basis = factorise(place, kept, other, window)
     return (coarse_new, factor, basis)
 
 

time: 44.5 us -> 41.8 us (0.939)
  Pallas kernels: 12.3 us -> 9.58 us
    pallas_call x1, Pallas kernels: 9.78 us -> 7.07 us  [factorise(): pl.pallas_call(factor_kernel, out_shape=[shaped((size, size)), shaped((si...]
where the time goes in v3:
time: 41.8 us; the launch traced here: 41.6 us
  starting transfers between devices  17 us (41%)
  waiting for transfers between devices  12.2 us (29%)
  Pallas kernels  9.58 us (23%)
  local copies, waits for them, and re-layouts  2.09 us (5%)
  between operations  0.7 us (2%)
    ppermute x6, waiting for transfers between devices, swap(): return lax.ppermute(values, axis, [(i, i ^ bit) for i in range(count)])  10.5 us
    ppermute x6, starting transfers between devices, swap(): return lax.ppermute(values, axis, [(i, i ^ bit) for i in range(count)])  10.3 us
    pallas_call x1, Pallas kernels, factorise(): pl.pallas_call(factor_kernel, out_shape=[shaped((size, size)), shaped((si...  7.07 us
    ppermute x2, starting transfers between devices, shift(): lax.ppermute(values, axis, [(i, i + step) for i in range(count) if 0 <= i...  6.66 us
    unnamed x6, local copies, waits for them, and re-layouts  2.09 us
    ppermute x2, waiting for transfers between devices, shift(): lax.ppermute(values, axis, [(i, i + step) for i in range(count) if 0 <= i...  1.73 us
    pallas_call x1, Pallas kernels, local(): pl.pallas_call(filter_kernel, out_shape=[shaped((12, 8, LANES))] * 3, in_...  1.72 us
  transfers between devices with their start and end apart: 8, of which 8 were waited for; matrix products, arithmetic and copies ran while one was open for 0% of the time, Pallas kernels for 0%

profile of v3, /device:TPU:0, one launch (start us, length us, event | category | flops | bytes accessed | tf_op | source)
XLA Modules:
  0.0 41.6 jit_solution(10515817438978986909)
XLA Ops:
  0.6 0.0 copy-start
  0.6 1.4 %copy-done = bf16[8,3,16,16,128]{4,3,2,1,0:T(8,128)(2,1)S(1)} copy-done((bf16[8,3,16,16,128]{4,3,2,1,0:T(8,128)(2,1)S(1)}, bf16[8,3,16,16,128]{4,3,2,1,0:T(8,128)(2,1)}, u32[]{:S(2)}) %copy-start) | copy-done | bytes 1572888
  2.0 0.0 copy-start.2
  2.0 0.7 %copy-done.2 = f32[3,17]{1,0:T(4,128)S(1)} copy-done((f32[3,17]{1,0:T(4,128)S(1)}, f32[3,17]{1,0:T(4,128)}, u32[]{:S(2)}) %copy-start.2) | copy-done | bytes 228
  2.7 0.0 copy-start.1
  2.7 1.7 %filter.1 = (f32[12,8,128]{2,1,0:T(8,128)S(1)}, f32[12,8,128]{2,1,0:T(8,128)S(1)}, f32[12,8,128]{2,1,0:T(8,128)S(1)}) custom-call(s32[1]{0:T(128)} %bitcast.place_ref, bf16[24,256,128]{2,1,0:T(8,128)(2,1)S(1)} %bitcast.5, f32[3,17]{1,0:T(4,128)S(1)} %copy-done.2), custom_call_target="tpu_custom_call" | custom-call | tf_op jit(solution)/shard_map/filter/pallas_call | solution.py:288
  4.5 0.5 %collective-permute-start = (f32[12,8,128]{2,1,0:T(8,128)S(1)}, f32[12,8,128]{2,1,0:T(8,128)S(1)}, u32[]{:S(2)}, u32[]{:S(2)}) collective-permute-start(f32[12,8,128]{2,1,0:T(8,128)S(1)} %get-tuple-element.13), channel_id=1, source_target_pairs={{0,1},{1,0},{2,3},{3,2},{4,5},{5,4},{6,7},{7,6},{8,9},{9,8},{10,11... | collective-permute-start | bytes 147464 | tf_op jit(solution)/shard_map/ppermute | solution.py:260
  5.0 0.9 %collective-permute-done = f32[12,8,128]{2,1,0:T(8,128)S(1)} collective-permute-done((f32[12,8,128]{2,1,0:T(8,128)S(1)}, f32[12,8,128]{2,1,0:T(8,128)S(1)}, u32[]{:S(2)}, u32[]{:S(2)}) %collective-permute-start) | collective-permute-done | bytes 49184 | tf_op jit(solution)/shard_map/ppermute | solution.py:260
  5.9 1.3 %collective-permute-start.2 = (f32[12,8,128]{2,1,0:T(8,128)S(1)}, f32[12,8,128]{2,1,0:T(8,128)S(1)}, u32[]{:S(2)}, u32[]{:S(2)}) collective-permute-start(f32[12,8,128]{2,1,0:T(8,128)S(1)} %bitcast_add_fusion), channel_id=1, source_target_pairs={{2,0},{4,2},{6,4},{8,6},{10,8},{12,10},{14,12},{3,1},{5,3},{7,5},{... | collective-permute-start | bytes 147464 | tf_op jit(solution)/shard_map/ppermute | solution.py:265
  7.2 5.4 %collective-permute-start.1 = (f32[12,8,128]{2,1,0:T(8,128)S(1)}, f32[12,8,128]{2,1,0:T(8,128)S(1)}, u32[]{:S(2)}, u32[]{:S(2)}) collective-permute-start(f32[12,8,128]{2,1,0:T(8,128)S(1)} %bitcast_add_fusion), channel_id=1, source_target_pairs={{0,2},{2,4},{4,6},{6,8},{8,10},{10,12},{12,14},{1,3},{3,5},{5,7},{... | collective-permute-start | bytes 147464 | tf_op jit(solution)/shard_map/ppermute | solution.py:265
  12.6 0.1 collective-permute-done.2.right_ref
  12.7 1.6 %collective-permute-done.1.left_ref = f32[12,8,128]{2,1,0:T(8,128)S(1)} collective-permute-done((f32[12,8,128]{2,1,0:T(8,128)S(1)}, f32[12,8,128]{2,1,0:T(8,128)S(1)}, u32[]{:S(2)}, u32[]{:S(2)}) %collective-permute-start.1) | collective-permute-done | bytes 49184 | tf_op jit(solution)/shard_map/ppermute | solution.py:265
  14.3 0.0 copy-done.1
  14.3 0.8 %gram.1 = (bf16[8,1536]{1,0:T(8,128)(2,1)}, bf16[256,1536]{1,0:T(8,128)(2,1)S(1)}, f32[136,128]{1,0:T(8,128)S(1)}, f32[136,128]{1,0:T(8,128)S(1)}) custom-call(s32[1]{0:T(128)} %bitcast.place_ref, bf16[248,1536]{1,0:T(8,128)(2,1)S(1)} %copy-done.1, f32[12,8,128]{2,1,0:T(8,128)S(1)} %get-tuple-element.12.own_ref, ...), custom_call_target="tpu_custom_call" | custom-call | tf_op jit(solution)/shard_map/gram/pallas_call | solution.py:308
  15.1 0.0 collective-permute-start.3
  15.1 1.3 %collective-permute-done.3 = f32[136,128]{1,0:T(8,128)S(1)} collective-permute-done((f32[136,128]{1,0:T(8,128)S(1)}, f32[136,128]{1,0:T(8,128)S(1)}, u32[]{:S(2)}, u32[]{:S(2)}) %collective-permute-start.3) | collective-permute-done | bytes 69664 | tf_op jit(solution)/shard_map/ppermute | solution.py:260
  16.4 3.0 %collective-permute-start.4 = (f32[136,128]{1,0:T(8,128)S(1)}, f32[136,128]{1,0:T(8,128)S(1)}, u32[]{:S(2)}, u32[]{:S(2)}) collective-permute-start(f32[136,128]{1,0:T(8,128)S(1)} %add.20), channel_id=1, source_target_pairs={{0,2},{2,0},{4,6},{6,4},{8,10},{10,8},{12,14},{14,12},{1,3},{3,1},... | collective-permute-start | bytes 208904 | tf_op jit(solution)/shard_map/ppermute | solution.py:260
  19.3 2.5 %collective-permute-done.4 = f32[136,128]{1,0:T(8,128)S(1)} collective-permute-done((f32[136,128]{1,0:T(8,128)S(1)}, f32[136,128]{1,0:T(8,128)S(1)}, u32[]{:S(2)}, u32[]{:S(2)}) %collective-permute-start.4) | collective-permute-done | bytes 69664 | tf_op jit(solution)/shard_map/ppermute | solution.py:260
  21.9 3.6 %collective-permute-start.5 = (f32[136,128]{1,0:T(8,128)S(1)}, f32[136,128]{1,0:T(8,128)S(1)}, u32[]{:S(2)}, u32[]{:S(2)}) collective-permute-start(f32[136,128]{1,0:T(8,128)S(1)} %add.21), channel_id=1, source_target_pairs={{0,4},{2,6},{4,0},{6,2},{8,12},{10,14},{12,8},{14,10},{1,5},{3,7},... | collective-permute-start | bytes 208904 | tf_op jit(solution)/shard_map/ppermute | solution.py:260
  25.5 2.3 %collective-permute-done.5 = f32[136,128]{1,0:T(8,128)S(1)} collective-permute-done((f32[136,128]{1,0:T(8,128)S(1)}, f32[136,128]{1,0:T(8,128)S(1)}, u32[]{:S(2)}, u32[]{:S(2)}) %collective-permute-start.5) | collective-permute-done | bytes 69664 | tf_op jit(solution)/shard_map/ppermute | solution.py:260
  27.8 3.1 %collective-permute-start.6 = (f32[136,128]{1,0:T(8,128)S(1)}, f32[136,128]{1,0:T(8,128)S(1)}, u32[]{:S(2)}, u32[]{:S(2)}) collective-permute-start(f32[136,128]{1,0:T(8,128)S(1)} %add.22), channel_id=1, source_target_pairs={{0,8},{2,10},{4,12},{6,14},{8,0},{10,2},{12,4},{14,6},{1,9},{3,11}... | collective-permute-start | bytes 208904 | tf_op jit(solution)/shard_map/ppermute | solution.py:260
  30.9 2.3 %collective-permute-done.6 = f32[136,128]{1,0:T(8,128)S(1)} collective-permute-done((f32[136,128]{1,0:T(8,128)S(1)}, f32[136,128]{1,0:T(8,128)S(1)}, u32[]{:S(2)}, u32[]{:S(2)}) %collective-permute-start.6) | collective-permute-done | bytes 69664 | tf_op jit(solution)/shard_map/ppermute | solution.py:260
  33.2 0.1 collective-permute-start.7
  33.3 1.2 %collective-permute-done.7.other_ref = f32[136,128]{1,0:T(8,128)S(1)} collective-permute-done((f32[136,128]{1,0:T(8,128)S(1)}, f32[136,128]{1,0:T(8,128)S(1)}, u32[]{:S(2)}, u32[]{:S(2)}) %collective-permute-start.7) | collective-permute-done | bytes 69664 | tf_op jit(solution)/shard_map/ppermute | solution.py:260
  34.5 7.1 %factor.1 = (f32[256,256]{1,0:T(8,128)}, f32[256,1536]{1,0:T(8,128)}) custom-call(s32[1]{0:T(128)} %bitcast.place_ref, f32[136,128]{1,0:T(8,128)S(1)} %add.23.kept_ref, f32[136,128]{1,0:T(8,128)S(1)} %collective-permute-done.7.other_ref, bf16[256,1536]{1,0:T(8,128)(2,1)S(1)} %get-tuple-element.18.window_ref), custom_call_target="tpu_custom_call" | custom-call | tf_op jit(solution)/shard_map/factor/pallas_call | solution.py:237
  (7 shorter events, 0.1 us)
Async XLA Ops:
  0.6 1.4 %copy-start = (bf16[8,3,16,16,128]{4,3,2,1,0:T(8,128)(2,1)S(1)}, bf16[8,3,16,16,128]{4,3,2,1,0:T(8,128)(2,1)}, u32[]{:S(2)}) copy-start(bf16[8,3,16,16,128]{4,3,2,1,0:T(8,128)(2,1)} %param.3) | copy-start | bytes 4718596
  2.0 0.7 %copy-start.2 = (f32[3,17]{1,0:T(4,128)S(1)}, f32[3,17]{1,0:T(4,128)}, u32[]{:S(2)}) copy-start(f32[3,17]{1,0:T(4,128)} %taps_ref.1) | copy-start | bytes 616
  2.7 11.6 %copy-start.1 = (bf16[248,1536]{1,0:T(8,128)(2,1)S(1)}, bf16[248,1536]{1,0:T(8,128)(2,1)}, u32[]{:S(2)}) copy-start(bf16[248,1536]{1,0:T(8,128)(2,1)} %stored_ref.1) | copy-start | bytes 2285572
  4.5 1.4 %collective-permute-start = (f32[12,8,128]{2,1,0:T(8,128)S(1)}, f32[12,8,128]{2,1,0:T(8,128)S(1)}, u32[]{:S(2)}, u32[]{:S(2)}) collective-permute-start(f32[12,8,128]{2,1,0:T(8,128)S(1)} %get-tuple-element.13), channel_id=1, source_target_pairs={{0,1},{1,0},{2,3},{3,2},{4,5},{5,4},{6,7},{7,6},{8,9},{9,8},{10,11... | collective-permute-start | bytes 147464 | tf_op jit(solution)/shard_map/ppermute | solution.py:260
  5.9 6.8 %collective-permute-start.2 = (f32[12,8,128]{2,1,0:T(8,128)S(1)}, f32[12,8,128]{2,1,0:T(8,128)S(1)}, u32[]{:S(2)}, u32[]{:S(2)}) collective-permute-start(f32[12,8,128]{2,1,0:T(8,128)S(1)} %bitcast_add_fusion), channel_id=1, source_target_pairs={{2,0},{4,2},{6,4},{8,6},{10,8},{12,10},{14,12},{3,1},{5,3},{7,5},{... | collective-permute-start | bytes 147464 | tf_op jit(solution)/shard_map/ppermute | solution.py:265
  7.2 7.1 %collective-permute-start.1 = (f32[12,8,128]{2,1,0:T(8,128)S(1)}, f32[12,8,128]{2,1,0:T(8,128)S(1)}, u32[]{:S(2)}, u32[]{:S(2)}) collective-permute-start(f32[12,8,128]{2,1,0:T(8,128)S(1)} %bitcast_add_fusion), channel_id=1, source_target_pairs={{0,2},{2,4},{4,6},{6,8},{8,10},{10,12},{12,14},{1,3},{3,5},{5,7},{... | collective-permute-start | bytes 147464 | tf_op jit(solution)/shard_map/ppermute | solution.py:265
  15.1 1.3 %collective-permute-start.3 = (f32[136,128]{1,0:T(8,128)S(1)}, f32[136,128]{1,0:T(8,128)S(1)}, u32[]{:S(2)}, u32[]{:S(2)}) collective-permute-start(f32[136,128]{1,0:T(8,128)S(1)} %get-tuple-element.17), channel_id=1, source_target_pairs={{0,1},{1,0},{2,3},{3,2},{4,5},{5,4},{6,7},{7,6},{8,9},{9,8},{10,11... | collective-permute-start | bytes 208904 | tf_op jit(solution)/shard_map/ppermute | solution.py:260
  16.4 5.5 %collective-permute-start.4 = (f32[136,128]{1,0:T(8,128)S(1)}, f32[136,128]{1,0:T(8,128)S(1)}, u32[]{:S(2)}, u32[]{:S(2)}) collective-permute-start(f32[136,128]{1,0:T(8,128)S(1)} %add.20), channel_id=1, source_target_pairs={{0,2},{2,0},{4,6},{6,4},{8,10},{10,8},{12,14},{14,12},{1,3},{3,1},... | collective-permute-start | bytes 208904 | tf_op jit(solution)/shard_map/ppermute | solution.py:260
  21.9 5.9 %collective-permute-start.5 = (f32[136,128]{1,0:T(8,128)S(1)}, f32[136,128]{1,0:T(8,128)S(1)}, u32[]{:S(2)}, u32[]{:S(2)}) collective-permute-start(f32[136,128]{1,0:T(8,128)S(1)} %add.21), channel_id=1, source_target_pairs={{0,4},{2,6},{4,0},{6,2},{8,12},{10,14},{12,8},{14,10},{1,5},{3,7},... | collective-permute-start | bytes 208904 | tf_op jit(solution)/shard_map/ppermute | solution.py:260
  27.8 5.4 %collective-permute-start.6 = (f32[136,128]{1,0:T(8,128)S(1)}, f32[136,128]{1,0:T(8,128)S(1)}, u32[]{:S(2)}, u32[]{:S(2)}) collective-permute-start(f32[136,128]{1,0:T(8,128)S(1)} %add.22), channel_id=1, source_target_pairs={{0,8},{2,10},{4,12},{6,14},{8,0},{10,2},{12,4},{14,6},{1,9},{3,11}... | collective-permute-start | bytes 208904 | tf_op jit(solution)/shard_map/ppermute | solution.py:260
  33.2 1.3 %collective-permute-start.7 = (f32[136,128]{1,0:T(8,128)S(1)}, f32[136,128]{1,0:T(8,128)S(1)}, u32[]{:S(2)}, u32[]{:S(2)}) collective-permute-start(f32[136,128]{1,0:T(8,128)S(1)} %add.23.kept_ref), channel_id=1, source_target_pairs={{0,1},{1,0},{2,3},{3,2},{4,5},{5,4},{6,7},{7,6},{8,9},{9,8},{10,11... | collective-permute-start | bytes 208904 | tf_op jit(solution)/shard_map/ppermute | solution.py:260

commit v4 on v3

--- a/solution.py
+++ b/solution.py
@@ -14,6 +14,8 @@
 PANEL = 64
 NEAR = 8
 FAR = 8
+PARTS = 6
+HALF = LANES + 8
 
 
 def iota(shape, dim):
@@ -39,77 +41,93 @@
     return total
 
 
-def filter_kernel(place_ref, fine_ref, taps_ref, own_ref, ext_ref, send_ref, plane_ref, row_ref):
+def filter_kernel(
+    place_ref, fine_hbm, taps_hbm, own_ref, ext_ref, fine_ref, taps_ref, plane_ref, row_ref, sems
+):
+    fields = fine_ref.shape[0]
+    part = fields // PARTS
+    taps_copy = pltpu.make_async_copy(taps_hbm, taps_ref, sems.at[PARTS])
+    taps_copy.start()
+    copies = [
+        pltpu.make_async_copy(fine_hbm.at[p * part : (p + 1) * part], fine_ref.at[p * part : (p + 1) * part], sems.at[p])
+        for p in range(PARTS)
+    ]
+    for copy in copies:
+        copy.start()
     first = place_ref[0] == 0
-    fields = fine_ref.shape[0]
     slot, cell = iota((64, 256), 0), iota((64, 256), 1)
     span_slot, sect_slot = slot // 8, slot % 8
     span_cell = jnp.where(span_slot < 6, span_slot, span_slot - 8)
     sect_cell = jnp.where((sect_slot < 4) | first, sect_slot, sect_slot - 6)
     span_tap = cell % 16 - 4 * span_cell + 8
     sect_tap = jnp.where(sect_slot < 6, cell // 16 - 4 * sect_cell + 8, -1)
+    taps_copy.wait()
     plane = weights_at(span_tap, taps_ref, 1) * weights_at(sect_tap, taps_ref, 0)
     plane = jnp.concatenate(split2(plane), axis=0)
-    for field in range(fields):
-        both = jnp.dot(plane, fine_ref[field], preferred_element_type=F32)
-        summed = both[:64] + both[64:]
-        for s in range(8):
-            plane_ref[s, 8 * field : 8 * field + 8, :] = summed[8 * s : 8 * s + 8]
     cell, lane = iota((LANES, LANES), 0), iota((LANES, LANES), 1)
     stream = weights_at(cell - 4 * (lane % 32) + 8, taps_ref, 2)
     parts = [
-        jnp.concatenate([jnp.where(lane // 32 == s, part, 0.0) for s in range(4)], axis=0).astype(BF16)
-        for part in (stream.astype(BF16).astype(F32), stream - stream.astype(BF16).astype(F32))
+        jnp.concatenate([jnp.where(lane // 32 == s, term, 0.0) for s in range(4)], axis=0).astype(BF16)
+        for term in (stream.astype(BF16).astype(F32), stream - stream.astype(BF16).astype(F32))
     ]
     matrix = jnp.concatenate([parts[0], parts[0], parts[1]], axis=0)
-    for half in range(2):
+    for p in range(PARTS):
+        copies[p].wait()
+        for field in range(p * part, (p + 1) * part):
+            both = jnp.dot(plane, fine_ref[field], preferred_element_type=F32)
+            summed = both[:64] + both[64:]
+            for s in range(8):
+                plane_ref[s, 8 * field : 8 * field + 8, :] = summed[8 * s : 8 * s + 8]
+    for half, out_ref in enumerate((own_ref, ext_ref)):
         values = jnp.concatenate([plane_ref[4 * half + s] for s in range(4)], axis=1)
         high, low = split2(values)
         row_ref[half] = jnp.dot(
             jnp.concatenate([high, low, high], axis=1), matrix, preferred_element_type=F32
         )
-    for comp in range(3):
-        for k in range(4):
-            rows = pl.ds(8 * comp + k, 8, stride=24)
-            own_ref[4 * comp + k] = row_ref[0, rows, :]
-            ext_ref[4 * comp + k] = row_ref[1, rows, :]
-        for k in range(2):
-            rows = pl.ds(8 * comp + 4 + k, 8, stride=24)
-            for half in range(2):
-                send_ref[6 * half + 2 * comp + k] = row_ref[half, rows, :]
-
-
-def gram_kernel(
-    total, place_ref, stored_ref, own_ref, partner_ref, left_ref, right_ref, coarse_ref, window_ref, kept_ref, sent_ref
+        for comp in range(3):
+            for k in range(6):
+                out_ref[comp, k] = row_ref[half, pl.ds(8 * comp + k, 8, stride=24), :]
+
+
+def fold(gram, kept_ref, sent_ref, first):
+    row, col = iota((LANES, LANES), 0), iota((LANES, LANES), 1)
+    across, lower = gram[LANES:, :LANES], gram[LANES:, LANES:]
+    packed = jnp.where(row <= col, gram[:LANES, :LANES], lower)
+    corner = jnp.sum(jnp.where(row == col, lower, 0.0), axis=0, keepdims=True)
+    corner = jnp.broadcast_to(corner, (8, LANES))
+    kept_ref[:LANES] = jnp.where(first, packed, across)
+    kept_ref[LANES:] = corner
+    sent_ref[:LANES] = jnp.where(first, across, packed)
+    sent_ref[LANES:] = corner
+
+
+def old_kernel(total, place_ref, stored_ref, after_ref, kept_ref, sent_ref):
+    old, cells = stored_ref.shape
+    rows = jnp.concatenate([stored_ref[...], jnp.zeros((8, cells), BF16)], axis=0)
+    gram = lax.dot_general(rows, rows, (((1,), (1,)), ((), ())), preferred_element_type=F32) / total
+    fold(gram, kept_ref, sent_ref, place_ref[0] == 0)
+
+
+def new_kernel(
+    total, place_ref, stored_ref, own_ref, left_ref, right_ref, partner_ref, kept_ref, coarse_ref, sums_ref
 ):
     first = place_ref[0] == 0
-    old = stored_ref.shape[0]
+    half = kept_ref.shape[0]
     lane = iota((8, LANES), 1)
     cells = []
     for comp in range(3):
         for k in range(4):
-            at = 4 * comp + k
-            value = own_ref[at] + jnp.where(lane < 64, left_ref[at], right_ref[at])
+            value = own_ref[comp, k] + jnp.where(lane < 64, left_ref[comp, k], right_ref[comp, k])
             here = first if k >= 2 else jnp.logical_not(first)
-            cells.append(value + jnp.where(here, partner_ref[2 * comp + k % 2], 0.0))
+            at = half + 8 * (2 * comp + k % 2)
+            cells.append(value + jnp.where(here, partner_ref[at : at + 8, :], 0.0))
     coarse = jnp.concatenate(cells, axis=1).astype(BF16)
     coarse_ref[...] = coarse
-    window_ref[: old - 8, :] = stored_ref[: old - 8, :]
-    window_ref[old - 8 :, :] = jnp.concatenate(
-        [stored_ref[old - 8 :, :].astype(F32), coarse.astype(F32)], axis=0
-    ).astype(BF16)
-    window = window_ref[...]
-    gram = lax.dot_general(window, window, (((1,), (1,)), ((), ())), preferred_element_type=F32) / total
-    row, col = iota((LANES, LANES), 0), iota((LANES, LANES), 1)
-    upper, lower = gram[:LANES, :LANES], gram[LANES:, LANES:]
-    packed = jnp.where(row >= col, upper, lower)
-    corner = jnp.sum(jnp.where(row == col, lower, 0.0), axis=0, keepdims=True)
-    corner = jnp.broadcast_to(corner, (8, LANES))
-    across = gram[:LANES, LANES:]
-    kept_ref[:LANES] = jnp.where(first, packed, across)
-    kept_ref[LANES:] = corner
-    sent_ref[:LANES] = jnp.where(first, across, packed)
-    sent_ref[LANES:] = corner
+    rows = jnp.concatenate([stored_ref[...], coarse], axis=0)
+    gram = lax.dot_general(coarse, rows, (((1,), (1,)), ((), ())), preferred_element_type=F32) / total
+    sums_ref[:half] = kept_ref[...] + partner_ref[:half, :]
+    sums_ref[half : half + 8] = gram[:, :LANES]
+    sums_ref[half + 8 :] = gram[:, LANES:]
 
 
 def eliminate(groups, at, lane, none, scale_ref):
@@ -153,22 +171,30 @@
 
 
 def factor_kernel(
-    place_ref, kept_ref, other_ref, window_ref, factor_hbm, basis_hbm,
-    left_ref, inverse_ref, upper_ref, factor_ref, basis_ref, scale_ref, sems,
+    place_ref, mine_ref, other_ref, stored_ref, coarse_ref, factor_hbm, basis_hbm,
+    left_ref, inverse_ref, upper_ref, factor_ref, basis_ref, scale_ref, window_ref, sems,
 ):
     first = place_ref[0] == 0
     none = jnp.full((8, LANES), jnp.minimum(place_ref[0], 0).astype(F32))
     size = left_ref.shape[0]
     row, col = iota((LANES, LANES), 0), iota((LANES, LANES), 1)
-    packed = jnp.where(first, kept_ref[:LANES], other_ref[:LANES])
-    across = jnp.where(first, other_ref[:LANES], kept_ref[:LANES])
-    corner = jnp.where(first, kept_ref[LANES : LANES + 1], other_ref[LANES : LANES + 1])
+    packed = jnp.where(first, mine_ref[:LANES], other_ref[:LANES])
+    across = jnp.where(first, other_ref[:LANES], mine_ref[:LANES])
+    corner = jnp.where(first, mine_ref[LANES : LANES + 1], other_ref[LANES : LANES + 1])
+    added = mine_ref[HALF : HALF + 8] + other_ref[HALF : HALF + 8]
+    across = jnp.concatenate([across[:-8], across[-8:] + added], axis=0)
+    added = mine_ref[HALF + 8 :] + other_ref[HALF + 8 :]
+    added = jnp.concatenate([jnp.zeros((LANES - 8, LANES), F32), added], axis=0)
+    corner = corner + jnp.sum(jnp.where(row == col, added, 0.0), axis=0, keepdims=True)
+    packed = packed + jnp.where(row > col, added, 0.0)
     turned = packed.T
-    left_ref[:LANES, :LANES] = jnp.where(row >= col, packed, turned)
-    left_ref[:LANES, LANES:] = across
+    window_ref[: size - 8, :] = stored_ref[...]
+    window_ref[size - 8 :, :] = coarse_ref[...]
+    left_ref[:LANES, :LANES] = jnp.where(row <= col, packed, turned)
+    left_ref[:LANES, LANES:] = across.T
     left_ref[LANES:, :LANES] = jnp.zeros((LANES, LANES), F32)
     left_ref[LANES:, LANES:] = jnp.where(
-        row == col, jnp.broadcast_to(corner, (LANES, LANES)), jnp.where(row > col, turned, packed)
+        row == col, jnp.broadcast_to(corner, (LANES, LANES)), jnp.where(row < col, turned, packed)
     )
     inverse_ref[...] = jnp.where(iota((size, size), 0) == iota((size, size), 1), 1.0, 0.0)
     upper_ref[...] = jnp.zeros((size, size), F32)
@@ -232,21 +258,28 @@
         copy.wait()
 
 
-def factorise(place, kept, other, window):
-    size, rows_dev = window.shape
+def factorise(place, mine, other, stored, coarse):
+    old, rows_dev = stored.shape
+    size = old + coarse.shape[0]
     return pl.pallas_call(
         factor_kernel,
         out_shape=[shaped((size, size)), shaped((size, rows_dev))],
-        in_specs=[SMEM] + [VMEM] * 3,
-        out_specs=[pl.BlockSpec(memory_space=pl.ANY)] * 2,
+        in_specs=[SMEM] + [VMEM] * 4,
+        out_specs=[ANY] * 2,
         scratch_shapes=[pltpu.VMEM((size, size), F32)] * 4
-        + [pltpu.VMEM((size, rows_dev), F32), pltpu.VMEM((PANEL, LANES), F32), pltpu.SemaphoreType.DMA((size // PANEL + 2,))],
+        + [
+            pltpu.VMEM((size, rows_dev), F32),
+            pltpu.VMEM((PANEL, LANES), F32),
+            pltpu.VMEM((size, rows_dev), BF16),
+            pltpu.SemaphoreType.DMA((size // PANEL + 2,)),
+        ],
         compiler_params=LIMIT,
         name="factor",
-    )(place, kept, other, window)
+    )(place, mine, other, stored, coarse)
 
 
 VMEM = pl.BlockSpec(memory_space=pltpu.VMEM)
+ANY = pl.BlockSpec(memory_space=pl.ANY)
 SMEM = pl.BlockSpec(memory_space=pltpu.SMEM)
 LIMIT = pltpu.CompilerParams(vmem_limit_bytes=48 * 2**20)
 
@@ -281,46 +314,47 @@
     assert (snapshots, comps, cells_y, cells_z, cells_x) == (8, 3, 16, 16, 128)
     assert lax.axis_size("sect") == 2
     old, rows_dev = stored.shape
-    size = old + snapshots
     total = rows_dev * lax.axis_size("span") * lax.axis_size("sect")
     place = lax.axis_index("sect").astype(jnp.int32).reshape(1)
     fields = snapshots * comps
-    own, ext, send = pl.pallas_call(
+    own, ext = pl.pallas_call(
         filter_kernel,
-        out_shape=[shaped((12, 8, LANES))] * 3,
-        in_specs=[SMEM, VMEM, SMEM],
-        out_specs=[VMEM] * 3,
-        scratch_shapes=[pltpu.VMEM((8, 8 * fields, LANES), F32), pltpu.VMEM((2, 8 * fields, LANES), F32)],
+        out_shape=[shaped((comps, 6, snapshots, LANES))] * 2,
+        in_specs=[SMEM, ANY, ANY],
+        out_specs=[VMEM] * 2,
+        scratch_shapes=[
+            pltpu.VMEM((fields, cells_y * cells_z, cells_x), BF16),
+            pltpu.SMEM(filter_taps.shape, F32),
+            pltpu.VMEM((8, 8 * fields, LANES), F32),
+            pltpu.VMEM((2, 8 * fields, LANES), F32),
+            pltpu.SemaphoreType.DMA((PARTS + 1,)),
+        ],
         compiler_params=LIMIT,
         name="filter",
     )(place, fine_field.reshape(fields, cells_y * cells_z, cells_x), filter_taps)
-    partner = swap(send, "sect", 1)
-    own_share, ext_share = partner[:6], partner[6:].reshape(3, 2, 8, LANES)
-    none = jnp.zeros_like(ext_share)
-    ext_share = jnp.where(
-        place[0] == 0,
-        jnp.concatenate([none, ext_share], axis=1),
-        jnp.concatenate([ext_share, none], axis=1),
-    )
-    ext = ext + ext_share.reshape(12, 8, LANES)
-    from_left = shift(ext, "span", 1)
-    from_right = shift(ext, "span", -1)
-    coarse_new, window, kept, sent = pl.pallas_call(
-        functools.partial(gram_kernel, total),
-        out_shape=[
-            shaped((snapshots, rows_dev), BF16),
-            shaped((size, rows_dev), BF16),
-            shaped((LANES + 8, LANES)),
-            shaped((LANES + 8, LANES)),
-        ],
-        in_specs=[SMEM] + [VMEM] * 5,
-        out_specs=[VMEM] * 4,
+    left = shift(ext, "span", 1)
+    right = shift(ext, "span", -1)
+    kept, sent = pl.pallas_call(
+        functools.partial(old_kernel, total),
+        out_shape=[shaped((HALF, LANES))] * 2,
+        in_specs=[SMEM, VMEM, VMEM],
+        out_specs=[VMEM] * 2,
         compiler_params=LIMIT,
-        name="gram",
-    )(place, stored, own, own_share, from_left, from_right)
-    kept = sum_over_span(kept + swap(sent, "sect", 1))
-    other = swap(kept, "sect", 1)
-    factor, basis = factorise(place, kept, other, window)
+        name="gram_stored",
+    )(place, stored, own)
+    lanes = lax.broadcasted_iota(jnp.int32, (1, 1, 1, LANES), 3)
+    halo = own[:, 4:] + jnp.where(lanes < 64, left[:, 4:], right[:, 4:])
+    partner = swap(jnp.concatenate([sent, halo.reshape(-1, LANES)], axis=0), "sect", 1)
+    coarse_new, sums = pl.pallas_call(
+        functools.partial(new_kernel, total),
+        out_shape=[shaped((snapshots, rows_dev), BF16), shaped((HALF + 2 * snapshots, LANES))],
+        in_specs=[SMEM] + [VMEM] * 6,
+        out_specs=[VMEM] * 2,
+        compiler_params=LIMIT,
+        name="gram_new",
+    )(place, stored, own, left, right, partner, kept)
+    sums = sum_over_span(sums)
+    factor, basis = factorise(place, sums, swap(sums, "sect", 1), stored, coarse_new)
     return (coarse_new, factor, basis)
 
 

time: 41.8 us -> 42.8 us (1.024)
  Pallas kernels: 9.58 us -> 10.8 us
  starting transfers between devices: 17 us -> 16.2 us
  local copies, waits for them, and re-layouts: 2.09 us -> 2.89 us
    pallas_call x2 -> x3, Pallas kernels: 2.5 us -> 3.8 us  [the longest x1 2.65 us: local(): pl.pallas_call(filter_kernel, out_shape=[shaped((comps, 6, snapshots, LAN...]
    ppermute x6 -> x5, starting transfers between devices: 10.3 us -> 9.43 us  [swap(): return lax.ppermute(values, axis, [(i, i ^ bit) for i in range(count)])]
    unnamed x6 -> x8, local copies, waits for them, and re-layouts: 2.09 us -> 2.89 us
    ppermute x6 -> x5, waiting for transfers between devices: 10.5 us -> 9.96 us  [swap(): return lax.ppermute(values, axis, [(i, i ^ bit) for i in range(count)])]
  transfers between devices with their start and end apart: 8 -> 7, of which waited for: 8 -> 6; matrix products, arithmetic and copies ran while one was open for 0% -> 0% of each run, Pallas kernels for 0% -> 1%
where the time goes in v4:
time: 42.8 us; the launch traced here: 42.5 us
  starting transfers between devices  16.2 us (38%)
  waiting for transfers between devices  11.8 us (28%)
  Pallas kernels  10.8 us (25%)
  local copies, waits for them, and re-layouts  2.89 us (7%)
  between operations  0.74 us (2%)
    ppermute x5, waiting for transfers between devices, swap(): return lax.ppermute(values, axis, [(i, i ^ bit) for i in range(count)])  9.96 us
    ppermute x5, starting transfers between devices, swap(): return lax.ppermute(values, axis, [(i, i ^ bit) for i in range(count)])  9.43 us
    pallas_call x1, Pallas kernels, factorise(): pl.pallas_call(factor_kernel, out_shape=[shaped((size, size)), shaped((si...  7.05 us
    ppermute x2, starting transfers between devices, shift(): lax.ppermute(values, axis, [(i, i + step) for i in range(count) if 0 <= i...  6.77 us
    unnamed x8, local copies, waits for them, and re-layouts  2.89 us
    pallas_call x1, Pallas kernels, local(): pl.pallas_call(filter_kernel, out_shape=[shaped((comps, 6, snapshots, LAN...  2.65 us
    ppermute x2, waiting for transfers between devices, shift(): lax.ppermute(values, axis, [(i, i + step) for i in range(count) if 0 <= i...  1.84 us
  transfers between devices with their start and end apart: 7, of which 6 were waited for; matrix products, arithmetic and copies ran while one was open for 0% of the time, Pallas kernels for 1%

profile of v4, /device:TPU:0, one launch (start us, length us, event | category | flops | bytes accessed | tf_op | source)
XLA Modules:
  0.0 42.5 jit_solution(14396773432713802022)
XLA Ops:
  0.6 0.0 copy-start
  0.6 0.0 copy-start.1
  0.7 1.5 %copy-done.1 = bf16[8,3,16,16,128]{4,3,2,1,0:T(8,128)(2,1)S(1)} copy-done((bf16[8,3,16,16,128]{4,3,2,1,0:T(8,128)(2,1)S(1)}, bf16[8,3,16,16,128]{4,3,2,1,0:T(8,128)(2,1)}, u32[]{:S(2)}) %copy-start.1) | copy-done | bytes 1572888
  2.1 0.0 copy-start.3
  2.1 0.7 %copy-done.3 = f32[3,17]{1,0:T(4,128)S(1)} copy-done((f32[3,17]{1,0:T(4,128)S(1)}, f32[3,17]{1,0:T(4,128)}, u32[]{:S(2)}) %copy-start.3) | copy-done | bytes 228
  2.8 2.7 %filter.1 = (f32[3,6,8,128]{3,2,1,0:T(8,128)S(1)}, f32[3,6,8,128]{3,2,1,0:T(8,128)S(1)}) custom-call(s32[1]{0:T(128)} %bitcast.place_ref, bf16[24,256,128]{2,1,0:T(8,128)(2,1)S(1)} %bitcast.3, f32[3,17]{1,0:T(4,128)S(1)} %copy-done.3), custom_call_target="tpu_custom_call" | custom-call | tf_op jit(solution)/shard_map/filter/pallas_call | solution.py:320
  5.5 1.3 %collective-permute-start.1 = (f32[3,6,8,128]{3,2,1,0:T(8,128)S(1)}, f32[3,6,8,128]{3,2,1,0:T(8,128)S(1)}, u32[]{:S(2)}, u32[]{:S(2)}) collective-permute-start(f32[3,6,8,128]{3,2,1,0:T(8,128)S(1)} %get-tuple-element.12), channel_id=1, source_target_pairs={{2,0},{4,2},{6,4},{8,6},{10,8},{12,10},{14,12},{3,1},{5,3},{7,5},{... | collective-permute-start | bytes 221192 | tf_op jit(solution)/shard_map/ppermute | solution.py:298
  6.8 5.5 %collective-permute-start = (f32[3,6,8,128]{3,2,1,0:T(8,128)S(1)}, f32[3,6,8,128]{3,2,1,0:T(8,128)S(1)}, u32[]{:S(2)}, u32[]{:S(2)}) collective-permute-start(f32[3,6,8,128]{3,2,1,0:T(8,128)S(1)} %get-tuple-element.12), channel_id=1, source_target_pairs={{0,2},{2,4},{4,6},{6,8},{8,10},{10,12},{12,14},{1,3},{3,5},{5,7},{... | collective-permute-start | bytes 221192 | tf_op jit(solution)/shard_map/ppermute | solution.py:298
  12.2 0.0 copy-done
  12.3 0.4 gram_stored.1
  12.7 0.0 collective-permute-done.1.right_ref
  12.7 1.8 %collective-permute-done.left_ref = f32[3,6,8,128]{3,2,1,0:T(8,128)S(1)} collective-permute-done((f32[3,6,8,128]{3,2,1,0:T(8,128)S(1)}, f32[3,6,8,128]{3,2,1,0:T(8,128)S(1)}, u32[]{:S(2)}, u32[]{:S(2)}) %collective-permute-start) | collective-permute-done | bytes 73760 | tf_op jit(solution)/shard_map/ppermute | solution.py:298
  14.6 0.1 collective-permute-start.2
  14.6 1.3 %collective-permute-done.2.partner_ref = f32[184,128]{1,0:T(8,128)S(1)} collective-permute-done((f32[184,128]{1,0:T(8,128)S(1)}, f32[184,128]{1,0:T(8,128)S(1)}, u32[]{:S(2)}, u32[]{:S(2)}) %collective-permute-start.2) | collective-permute-done | bytes 94240 | tf_op jit(solution)/shard_map/ppermute | solution.py:293
  15.9 0.7 %gram_new.1 = (bf16[8,1536]{1,0:T(8,128)(2,1)}, f32[152,128]{1,0:T(8,128)S(1)}) custom-call(s32[1]{0:T(128)} %bitcast.place_ref, bf16[248,1536]{1,0:T(8,128)(2,1)S(1)} %copy-done, f32[3,6,8,128]{3,2,1,0:T(8,128)S(1)} %get-tuple-element.11.after_ref.own_ref, f32[3,6,8,128]{3,2,1,0:T(8,128)S(1)} %collective-permute-done.left_ref, ...), custom_call_target="tpu_custom_call" | custom-call | tf_op jit(solution)/shard_map/gram_new/pallas_call | solution.py:348
  16.6 2.6 %collective-permute-start.3 = (f32[152,128]{1,0:T(8,128)S(1)}, f32[152,128]{1,0:T(8,128)S(1)}, u32[]{:S(2)}, u32[]{:S(2)}) collective-permute-start(f32[152,128]{1,0:T(8,128)S(1)} %get-tuple-element.16), channel_id=1, source_target_pairs={{0,2},{2,0},{4,6},{6,4},{8,10},{10,8},{12,14},{14,12},{1,3},{3,1},... | collective-permute-start | bytes 233480 | tf_op jit(solution)/shard_map/ppermute | solution.py:293
  19.2 2.7 %collective-permute-done.3 = f32[152,128]{1,0:T(8,128)S(1)} collective-permute-done((f32[152,128]{1,0:T(8,128)S(1)}, f32[152,128]{1,0:T(8,128)S(1)}, u32[]{:S(2)}, u32[]{:S(2)}) %collective-permute-start.3) | collective-permute-done | bytes 77856 | tf_op jit(solution)/shard_map/ppermute | solution.py:293
  21.9 3.6 %collective-permute-start.4 = (f32[152,128]{1,0:T(8,128)S(1)}, f32[152,128]{1,0:T(8,128)S(1)}, u32[]{:S(2)}, u32[]{:S(2)}) collective-permute-start(f32[152,128]{1,0:T(8,128)S(1)} %add.13), channel_id=1, source_target_pairs={{0,4},{2,6},{4,0},{6,2},{8,12},{10,14},{12,8},{14,10},{1,5},{3,7},... | collective-permute-start | bytes 233480 | tf_op jit(solution)/shard_map/ppermute | solution.py:293
  25.5 2.4 %collective-permute-done.4 = f32[152,128]{1,0:T(8,128)S(1)} collective-permute-done((f32[152,128]{1,0:T(8,128)S(1)}, f32[152,128]{1,0:T(8,128)S(1)}, u32[]{:S(2)}, u32[]{:S(2)}) %collective-permute-start.4) | collective-permute-done | bytes 77856 | tf_op jit(solution)/shard_map/ppermute | solution.py:293
  27.9 3.1 %collective-permute-start.5 = (f32[152,128]{1,0:T(8,128)S(1)}, f32[152,128]{1,0:T(8,128)S(1)}, u32[]{:S(2)}, u32[]{:S(2)}) collective-permute-start(f32[152,128]{1,0:T(8,128)S(1)} %add.14), channel_id=1, source_target_pairs={{0,8},{2,10},{4,12},{6,14},{8,0},{10,2},{12,4},{14,6},{1,9},{3,11}... | collective-permute-start | bytes 233480 | tf_op jit(solution)/shard_map/ppermute | solution.py:293
  31.0 2.4 %collective-permute-done.5 = f32[152,128]{1,0:T(8,128)S(1)} collective-permute-done((f32[152,128]{1,0:T(8,128)S(1)}, f32[152,128]{1,0:T(8,128)S(1)}, u32[]{:S(2)}, u32[]{:S(2)}) %collective-permute-start.5) | collective-permute-done | bytes 77856 | tf_op jit(solution)/shard_map/ppermute | solution.py:293
  33.4 0.1 collective-permute-start.6
  33.5 1.3 %collective-permute-done.6.other_ref = f32[152,128]{1,0:T(8,128)S(1)} collective-permute-done((f32[152,128]{1,0:T(8,128)S(1)}, f32[152,128]{1,0:T(8,128)S(1)}, u32[]{:S(2)}, u32[]{:S(2)}) %collective-permute-start.6) | collective-permute-done | bytes 77856 | tf_op jit(solution)/shard_map/ppermute | solution.py:293
  34.7 0.0 copy-start.2
  34.7 0.7 %copy-done.2 = bf16[8,1536]{1,0:T(8,128)(2,1)S(1)} copy-done((bf16[8,1536]{1,0:T(8,128)(2,1)S(1)}, bf16[8,1536]{1,0:T(8,128)(2,1)}, u32[]{:S(2)}) %copy-start.2) | copy-done | bytes 24600
  35.5 7.0 %factor.1 = (f32[256,256]{1,0:T(8,128)}, f32[256,1536]{1,0:T(8,128)}) custom-call(s32[1]{0:T(128)} %bitcast.place_ref, f32[152,128]{1,0:T(8,128)S(1)} %add.15.mine_ref, f32[152,128]{1,0:T(8,128)S(1)} %collective-permute-done.6.other_ref, bf16[248,1536]{1,0:T(8,128)(2,1)S(1)} %copy-done, bf16[8,1536]{1,0:T(8,128)(2,1)S(1)} %copy-done.2), custom_call_target="tpu_custom_call" | custom-call | tf_op jit(solution)/shard_map/factor/pallas_call | solution.py:264
  (6 shorter events, 0.1 us)
Async XLA Ops:
  0.6 11.6 %copy-start = (bf16[248,1536]{1,0:T(8,128)(2,1)S(1)}, bf16[248,1536]{1,0:T(8,128)(2,1)}, u32[]{:S(2)}) copy-start(bf16[248,1536]{1,0:T(8,128)(2,1)} %stored_ref.5) | copy-start | bytes 2285572
  0.6 1.5 %copy-start.1 = (bf16[8,3,16,16,128]{4,3,2,1,0:T(8,128)(2,1)S(1)}, bf16[8,3,16,16,128]{4,3,2,1,0:T(8,128)(2,1)}, u32[]{:S(2)}) copy-start(bf16[8,3,16,16,128]{4,3,2,1,0:T(8,128)(2,1)} %param.3) | copy-start | bytes 4718596
  2.1 0.7 %copy-start.3 = (f32[3,17]{1,0:T(4,128)S(1)}, f32[3,17]{1,0:T(4,128)}, u32[]{:S(2)}) copy-start(f32[3,17]{1,0:T(4,128)} %taps_hbm.1) | copy-start | bytes 616
  5.5 7.2 %collective-permute-start.1 = (f32[3,6,8,128]{3,2,1,0:T(8,128)S(1)}, f32[3,6,8,128]{3,2,1,0:T(8,128)S(1)}, u32[]{:S(2)}, u32[]{:S(2)}) collective-permute-start(f32[3,6,8,128]{3,2,1,0:T(8,128)S(1)} %get-tuple-element.12), channel_id=1, source_target_pairs={{2,0},{4,2},{6,4},{8,6},{10,8},{12,10},{14,12},{3,1},{5,3},{7,5},{... | collective-permute-start | bytes 221192 | tf_op jit(solution)/shard_map/ppermute | solution.py:298
  6.8 7.8 %collective-permute-start = (f32[3,6,8,128]{3,2,1,0:T(8,128)S(1)}, f32[3,6,8,128]{3,2,1,0:T(8,128)S(1)}, u32[]{:S(2)}, u32[]{:S(2)}) collective-permute-start(f32[3,6,8,128]{3,2,1,0:T(8,128)S(1)} %get-tuple-element.12), channel_id=1, source_target_pairs={{0,2},{2,4},{4,6},{6,8},{8,10},{10,12},{12,14},{1,3},{3,5},{5,7},{... | collective-permute-start | bytes 221192 | tf_op jit(solution)/shard_map/ppermute | solution.py:298
  14.6 1.4 %collective-permute-start.2 = (f32[184,128]{1,0:T(8,128)S(1)}, f32[184,128]{1,0:T(8,128)S(1)}, u32[]{:S(2)}, u32[]{:S(2)}) collective-permute-start(f32[184,128]{1,0:T(8,128)S(1)} %pad_maximum_fusion), channel_id=1, source_target_pairs={{0,1},{1,0},{2,3},{3,2},{4,5},{5,4},{6,7},{7,6},{8,9},{9,8},{10,11... | collective-permute-start | bytes 282632 | tf_op jit(solution)/shard_map/ppermute | solution.py:293
  16.6 5.2 %collective-permute-start.3 = (f32[152,128]{1,0:T(8,128)S(1)}, f32[152,128]{1,0:T(8,128)S(1)}, u32[]{:S(2)}, u32[]{:S(2)}) collective-permute-start(f32[152,128]{1,0:T(8,128)S(1)} %get-tuple-element.16), channel_id=1, source_target_pairs={{0,2},{2,0},{4,6},{6,4},{8,10},{10,8},{12,14},{14,12},{1,3},{3,1},... | collective-permute-start | bytes 233480 | tf_op jit(solution)/shard_map/ppermute | solution.py:293
  21.9 6.0 %collective-permute-start.4 = (f32[152,128]{1,0:T(8,128)S(1)}, f32[152,128]{1,0:T(8,128)S(1)}, u32[]{:S(2)}, u32[]{:S(2)}) collective-permute-start(f32[152,128]{1,0:T(8,128)S(1)} %add.13), channel_id=1, source_target_pairs={{0,4},{2,6},{4,0},{6,2},{8,12},{10,14},{12,8},{14,10},{1,5},{3,7},... | collective-permute-start | bytes 233480 | tf_op jit(solution)/shard_map/ppermute | solution.py:293
  27.9 5.5 %collective-permute-start.5 = (f32[152,128]{1,0:T(8,128)S(1)}, f32[152,128]{1,0:T(8,128)S(1)}, u32[]{:S(2)}, u32[]{:S(2)}) collective-permute-start(f32[152,128]{1,0:T(8,128)S(1)} %add.14), channel_id=1, source_target_pairs={{0,8},{2,10},{4,12},{6,14},{8,0},{10,2},{12,4},{14,6},{1,9},{3,11}... | collective-permute-start | bytes 233480 | tf_op jit(solution)/shard_map/ppermute | solution.py:293
  33.4 1.3 %collective-permute-start.6 = (f32[152,128]{1,0:T(8,128)S(1)}, f32[152,128]{1,0:T(8,128)S(1)}, u32[]{:S(2)}, u32[]{:S(2)}) collective-permute-start(f32[152,128]{1,0:T(8,128)S(1)} %add.15.mine_ref), channel_id=1, source_target_pairs={{0,1},{1,0},{2,3},{3,2},{4,5},{5,4},{6,7},{7,6},{8,9},{9,8},{10,11... | collective-permute-start | bytes 233480 | tf_op jit(solution)/shard_map/ppermute | solution.py:293
  34.7 0.7 %copy-start.2 = (bf16[8,1536]{1,0:T(8,128)(2,1)S(1)}, bf16[8,1536]{1,0:T(8,128)(2,1)}, u32[]{:S(2)}) copy-start(bf16[8,1536]{1,0:T(8,128)(2,1)} %get-tuple-element.8.coarse_ref) | copy-start | bytes 73732

commit v5 on v4

--- a/solution.py
+++ b/solution.py
@@ -171,7 +171,7 @@
 
 
 def factor_kernel(
-    place_ref, mine_ref, other_ref, stored_ref, coarse_ref, factor_hbm, basis_hbm,
+    place_ref, mine_ref, other_ref, stored_ref, coarse_ref, new_hbm, factor_hbm, basis_hbm,
     left_ref, inverse_ref, upper_ref, factor_ref, basis_ref, scale_ref, window_ref, sems,
 ):
     first = place_ref[0] == 0
@@ -188,6 +188,8 @@
     corner = corner + jnp.sum(jnp.where(row == col, added, 0.0), axis=0, keepdims=True)
     packed = packed + jnp.where(row > col, added, 0.0)
     turned = packed.T
+    copies = [pltpu.make_async_copy(coarse_ref, new_hbm, sems.at[0])]
+    copies[0].start()
     window_ref[: size - 8, :] = stored_ref[...]
     window_ref[size - 8 :, :] = coarse_ref[...]
     left_ref[:LANES, :LANES] = jnp.where(row <= col, packed, turned)
@@ -198,7 +200,6 @@
     )
     inverse_ref[...] = jnp.where(iota((size, size), 0) == iota((size, size), 1), 1.0, 0.0)
     upper_ref[...] = jnp.zeros((size, size), F32)
-    copies = []
 
     def send(source, target, begin, end):
         copies.append(pltpu.make_async_copy(source.at[begin:end], target.at[begin:end], sems.at[len(copies)]))
@@ -263,15 +264,15 @@
     size = old + coarse.shape[0]
     return pl.pallas_call(
         factor_kernel,
-        out_shape=[shaped((size, size)), shaped((size, rows_dev))],
+        out_shape=[shaped(coarse.shape, BF16), shaped((size, size)), shaped((size, rows_dev))],
         in_specs=[SMEM] + [VMEM] * 4,
-        out_specs=[ANY] * 2,
+        out_specs=[HBM] * 3,
         scratch_shapes=[pltpu.VMEM((size, size), F32)] * 4
         + [
             pltpu.VMEM((size, rows_dev), F32),
             pltpu.VMEM((PANEL, LANES), F32),
             pltpu.VMEM((size, rows_dev), BF16),
-            pltpu.SemaphoreType.DMA((size // PANEL + 2,)),
+            pltpu.SemaphoreType.DMA((size // PANEL + 3,)),
         ],
         compiler_params=LIMIT,
         name="factor",
@@ -279,7 +280,7 @@
 
 
 VMEM = pl.BlockSpec(memory_space=pltpu.VMEM)
-ANY = pl.BlockSpec(memory_space=pl.ANY)
+HBM = pl.BlockSpec(memory_space=pltpu.HBM)
 SMEM = pl.BlockSpec(memory_space=pltpu.SMEM)
 LIMIT = pltpu.CompilerParams(vmem_limit_bytes=48 * 2**20)
 
@@ -320,7 +321,7 @@
     own, ext = pl.pallas_call(
         filter_kernel,
         out_shape=[shaped((comps, 6, snapshots, LANES))] * 2,
-        in_specs=[SMEM, ANY, ANY],
+        in_specs=[SMEM, HBM, HBM],
         out_specs=[VMEM] * 2,
         scratch_shapes=[
             pltpu.VMEM((fields, cells_y * cells_z, cells_x), BF16),
@@ -329,7 +330,7 @@
             pltpu.VMEM((2, 8 * fields, LANES), F32),
             pltpu.SemaphoreType.DMA((PARTS + 1,)),
         ],
-        compiler_params=LIMIT,
+        compiler_params=pltpu.CompilerParams(vmem_limit_bytes=55 * 2**20),
         name="filter",
     )(place, fine_field.reshape(fields, cells_y * cells_z, cells_x), filter_taps)
     left = shift(ext, "span", 1)
@@ -345,7 +346,7 @@
     lanes = lax.broadcasted_iota(jnp.int32, (1, 1, 1, LANES), 3)
     halo = own[:, 4:] + jnp.where(lanes < 64, left[:, 4:], right[:, 4:])
     partner = swap(jnp.concatenate([sent, halo.reshape(-1, LANES)], axis=0), "sect", 1)
-    coarse_new, sums = pl.pallas_call(
+    coarse, sums = pl.pallas_call(
         functools.partial(new_kernel, total),
         out_shape=[shaped((snapshots, rows_dev), BF16), shaped((HALF + 2 * snapshots, LANES))],
         in_specs=[SMEM] + [VMEM] * 6,
@@ -354,8 +355,7 @@
         name="gram_new",
     )(place, stored, own, left, right, partner, kept)
     sums = sum_over_span(sums)
-    factor, basis = factorise(place, sums, swap(sums, "sect", 1), stored, coarse_new)
-    return (coarse_new, factor, basis)
+    return tuple(factorise(place, sums, swap(sums, "sect", 1), stored, coarse))
 
 
 def solution(mesh):

time: 42.8 us -> 40.6 us (0.949)
  local copies, waits for them, and re-layouts: 2.89 us -> 0.88 us
  waiting for transfers between devices: 11.8 us -> 11.2 us
  Pallas kernels: 10.8 us -> 11.3 us
    unnamed x8 -> x4, local copies, waits for them, and re-layouts: 2.89 us -> 0.88 us
    pallas_call x1, Pallas kernels: 2.65 us -> 3.55 us  [local(): pl.pallas_call(filter_kernel, out_shape=[shaped((comps, 6, snapshots, LAN...]
    ppermute x2, waiting for transfers between devices: 1.84 us -> 1.27 us  [shift(): lax.ppermute(values, axis, [(i, i + step) for i in range(count) if 0 <= i...]
where the time goes in v5:
time: 40.6 us; the launch traced here: 40.4 us
  starting transfers between devices  16.1 us (40%)
  Pallas kernels  11.3 us (28%)
  waiting for transfers between devices  11.2 us (28%)
  local copies, waits for them, and re-layouts  0.88 us (2%)
  between operations  0.73 us (2%)
    ppermute x5, waiting for transfers between devices, swap(): return lax.ppermute(values, axis, [(i, i ^ bit) for i in range(count)])  9.97 us
    ppermute x5, starting transfers between devices, swap(): return lax.ppermute(values, axis, [(i, i ^ bit) for i in range(count)])  9.35 us
    pallas_call x1, Pallas kernels, factorise(): pl.pallas_call(factor_kernel, out_shape=[shaped(coarse.shape, BF16), shap...  7.06 us
    ppermute x2, starting transfers between devices, shift(): lax.ppermute(values, axis, [(i, i + step) for i in range(count) if 0 <= i...  6.76 us
    pallas_call x1, Pallas kernels, local(): pl.pallas_call(filter_kernel, out_shape=[shaped((comps, 6, snapshots, LAN...  3.55 us
    ppermute x2, waiting for transfers between devices, shift(): lax.ppermute(values, axis, [(i, i + step) for i in range(count) if 0 <= i...  1.27 us
    unnamed x4, local copies, waits for them, and re-layouts  0.88 us
  transfers between devices with their start and end apart: 7, of which 6 were waited for; matrix products, arithmetic and copies ran while one was open for 0% of the time, Pallas kernels for 1%

profile of v5, /device:TPU:0, one launch (start us, length us, event | category | flops | bytes accessed | tf_op | source)
XLA Modules:
  0.0 40.4 jit_solution(10434208917588298325)
XLA Ops:
  0.6 0.0 copy-start
  0.6 3.6 %filter.1 = (f32[3,6,8,128]{3,2,1,0:T(8,128)}, f32[3,6,8,128]{3,2,1,0:T(8,128)}) custom-call(s32[1]{0:T(128)} %bitcast.place_ref, bf16[24,256,128]{2,1,0:T(8,128)(2,1)} %bitcast.3, f32[3,17]{1,0:T(4,128)} %taps_hbm.1), custom_call_target="tpu_custom_call" | custom-call | tf_op jit(solution)/shard_map/filter/pallas_call | solution.py:321
  4.2 1.3 %collective-permute-start.1 = (f32[3,6,8,128]{3,2,1,0:T(8,128)}, f32[3,6,8,128]{3,2,1,0:T(8,128)S(1)}, u32[]{:S(2)}, u32[]{:S(2)}) collective-permute-start(f32[3,6,8,128]{3,2,1,0:T(8,128)} %get-tuple-element.10), channel_id=1, source_target_pairs={{2,0},{4,2},{6,4},{8,6},{10,8},{12,10},{14,12},{3,1},{5,3},{7,5},{... | collective-permute-start | bytes 221192 | tf_op jit(solution)/shard_map/ppermute | solution.py:299
  5.5 5.5 %collective-permute-start = (f32[3,6,8,128]{3,2,1,0:T(8,128)}, f32[3,6,8,128]{3,2,1,0:T(8,128)S(1)}, u32[]{:S(2)}, u32[]{:S(2)}) collective-permute-start(f32[3,6,8,128]{3,2,1,0:T(8,128)} %get-tuple-element.10), channel_id=1, source_target_pairs={{0,2},{2,4},{4,6},{6,8},{8,10},{10,12},{12,14},{1,3},{3,5},{5,7},{... | collective-permute-start | bytes 221192 | tf_op jit(solution)/shard_map/ppermute | solution.py:299
  11.0 0.0 copy-done
  11.0 0.0 copy-start.1
  11.0 0.9 %copy-done.1 = f32[3,6,8,128]{3,2,1,0:T(8,128)S(1)} copy-done((f32[3,6,8,128]{3,2,1,0:T(8,128)S(1)}, f32[3,6,8,128]{3,2,1,0:T(8,128)}, u32[]{:S(2)}) %copy-start.1) | copy-done | bytes 73752
  11.9 0.4 %gram_stored.1 = (f32[136,128]{1,0:T(8,128)S(1)}, f32[136,128]{1,0:T(8,128)S(1)}) custom-call(s32[1]{0:T(128)} %bitcast.place_ref, bf16[248,1536]{1,0:T(8,128)(2,1)S(1)} %copy-done, f32[3,6,8,128]{3,2,1,0:T(8,128)S(1)} %copy-done.1), custom_call_target="tpu_custom_call" | custom-call | tf_op jit(solution)/shard_map/gram_stored/pallas_call | solution.py:338
  12.3 0.0 collective-permute-done.1.right_ref
  12.3 1.3 %collective-permute-done.left_ref = f32[3,6,8,128]{3,2,1,0:T(8,128)S(1)} collective-permute-done((f32[3,6,8,128]{3,2,1,0:T(8,128)}, f32[3,6,8,128]{3,2,1,0:T(8,128)S(1)}, u32[]{:S(2)}, u32[]{:S(2)}) %collective-permute-start) | collective-permute-done | bytes 73760 | tf_op jit(solution)/shard_map/ppermute | solution.py:299
  13.6 0.1 collective-permute-start.2
  13.7 1.3 %collective-permute-done.2.partner_ref = f32[184,128]{1,0:T(8,128)S(1)} collective-permute-done((f32[184,128]{1,0:T(8,128)S(1)}, f32[184,128]{1,0:T(8,128)S(1)}, u32[]{:S(2)}, u32[]{:S(2)}) %collective-permute-start.2) | collective-permute-done | bytes 94240 | tf_op jit(solution)/shard_map/ppermute | solution.py:294
  15.0 0.3 gram_new.1
  15.3 2.6 %collective-permute-start.3 = (f32[152,128]{1,0:T(8,128)S(1)}, f32[152,128]{1,0:T(8,128)S(1)}, u32[]{:S(2)}, u32[]{:S(2)}) collective-permute-start(f32[152,128]{1,0:T(8,128)S(1)} %get-tuple-element.13), channel_id=1, source_target_pairs={{0,2},{2,0},{4,6},{6,4},{8,10},{10,8},{12,14},{14,12},{1,3},{3,1},... | collective-permute-start | bytes 233480 | tf_op jit(solution)/shard_map/ppermute | solution.py:294
  17.9 2.7 %collective-permute-done.3 = f32[152,128]{1,0:T(8,128)S(1)} collective-permute-done((f32[152,128]{1,0:T(8,128)S(1)}, f32[152,128]{1,0:T(8,128)S(1)}, u32[]{:S(2)}, u32[]{:S(2)}) %collective-permute-start.3) | collective-permute-done | bytes 77856 | tf_op jit(solution)/shard_map/ppermute | solution.py:294
  20.6 3.5 %collective-permute-start.4 = (f32[152,128]{1,0:T(8,128)S(1)}, f32[152,128]{1,0:T(8,128)S(1)}, u32[]{:S(2)}, u32[]{:S(2)}) collective-permute-start(f32[152,128]{1,0:T(8,128)S(1)} %add.13), channel_id=1, source_target_pairs={{0,4},{2,6},{4,0},{6,2},{8,12},{10,14},{12,8},{14,10},{1,5},{3,7},... | collective-permute-start | bytes 233480 | tf_op jit(solution)/shard_map/ppermute | solution.py:294
  24.1 2.4 %collective-permute-done.4 = f32[152,128]{1,0:T(8,128)S(1)} collective-permute-done((f32[152,128]{1,0:T(8,128)S(1)}, f32[152,128]{1,0:T(8,128)S(1)}, u32[]{:S(2)}, u32[]{:S(2)}) %collective-permute-start.4) | collective-permute-done | bytes 77856 | tf_op jit(solution)/shard_map/ppermute | solution.py:294
  26.5 3.1 %collective-permute-start.5 = (f32[152,128]{1,0:T(8,128)S(1)}, f32[152,128]{1,0:T(8,128)S(1)}, u32[]{:S(2)}, u32[]{:S(2)}) collective-permute-start(f32[152,128]{1,0:T(8,128)S(1)} %add.14), channel_id=1, source_target_pairs={{0,8},{2,10},{4,12},{6,14},{8,0},{10,2},{12,4},{14,6},{1,9},{3,11}... | collective-permute-start | bytes 233480 | tf_op jit(solution)/shard_map/ppermute | solution.py:294
  29.6 2.4 %collective-permute-done.5 = f32[152,128]{1,0:T(8,128)S(1)} collective-permute-done((f32[152,128]{1,0:T(8,128)S(1)}, f32[152,128]{1,0:T(8,128)S(1)}, u32[]{:S(2)}, u32[]{:S(2)}) %collective-permute-start.5) | collective-permute-done | bytes 77856 | tf_op jit(solution)/shard_map/ppermute | solution.py:294
  32.0 0.1 collective-permute-start.6
  32.0 1.3 %collective-permute-done.6.other_ref = f32[152,128]{1,0:T(8,128)S(1)} collective-permute-done((f32[152,128]{1,0:T(8,128)S(1)}, f32[152,128]{1,0:T(8,128)S(1)}, u32[]{:S(2)}, u32[]{:S(2)}) %collective-permute-start.6) | collective-permute-done | bytes 77856 | tf_op jit(solution)/shard_map/ppermute | solution.py:294
  33.3 7.1 %factor.1 = (bf16[8,1536]{1,0:T(8,128)(2,1)}, f32[256,256]{1,0:T(8,128)}, f32[256,1536]{1,0:T(8,128)}) custom-call(s32[1]{0:T(128)} %bitcast.place_ref, f32[152,128]{1,0:T(8,128)S(1)} %add.15.mine_ref, f32[152,128]{1,0:T(8,128)S(1)} %collective-permute-done.6.other_ref, bf16[248,1536]{1,0:T(8,128)(2,1)S(1)} %copy-done, ...), custom_call_target="tpu_custom_call" | custom-call | tf_op jit(solution)/shard_map/factor/pallas_call | solution.py:265
  (6 shorter events, 0.1 us)
Async XLA Ops:
  0.6 10.4 %copy-start = (bf16[248,1536]{1,0:T(8,128)(2,1)S(1)}, bf16[248,1536]{1,0:T(8,128)(2,1)}, u32[]{:S(2)}) copy-start(bf16[248,1536]{1,0:T(8,128)(2,1)} %stored_ref.5) | copy-start | bytes 2285572
  4.2 8.1 %collective-permute-start.1 = (f32[3,6,8,128]{3,2,1,0:T(8,128)}, f32[3,6,8,128]{3,2,1,0:T(8,128)S(1)}, u32[]{:S(2)}, u32[]{:S(2)}) collective-permute-start(f32[3,6,8,128]{3,2,1,0:T(8,128)} %get-tuple-element.10), channel_id=1, source_target_pairs={{2,0},{4,2},{6,4},{8,6},{10,8},{12,10},{14,12},{3,1},{5,3},{7,5},{... | collective-permute-start | bytes 221192 | tf_op jit(solution)/shard_map/ppermute | solution.py:299
  5.5 8.1 %collective-permute-start = (f32[3,6,8,128]{3,2,1,0:T(8,128)}, f32[3,6,8,128]{3,2,1,0:T(8,128)S(1)}, u32[]{:S(2)}, u32[]{:S(2)}) collective-permute-start(f32[3,6,8,128]{3,2,1,0:T(8,128)} %get-tuple-element.10), channel_id=1, source_target_pairs={{0,2},{2,4},{4,6},{6,8},{8,10},{10,12},{12,14},{1,3},{3,5},{5,7},{... | collective-permute-start | bytes 221192 | tf_op jit(solution)/shard_map/ppermute | solution.py:299
  11.0 0.9 %copy-start.1 = (f32[3,6,8,128]{3,2,1,0:T(8,128)S(1)}, f32[3,6,8,128]{3,2,1,0:T(8,128)}, u32[]{:S(2)}) copy-start(f32[3,6,8,128]{3,2,1,0:T(8,128)} %get-tuple-element.9.after_ref.own_ref) | copy-start | bytes 221188
  13.6 1.4 %collective-permute-start.2 = (f32[184,128]{1,0:T(8,128)S(1)}, f32[184,128]{1,0:T(8,128)S(1)}, u32[]{:S(2)}, u32[]{:S(2)}) collective-permute-start(f32[184,128]{1,0:T(8,128)S(1)} %pad_maximum_fusion), channel_id=1, source_target_pairs={{0,1},{1,0},{2,3},{3,2},{4,5},{5,4},{6,7},{7,6},{8,9},{9,8},{10,11... | collective-permute-start | bytes 282632 | tf_op jit(solution)/shard_map/ppermute | solution.py:294
  15.3 5.3 %collective-permute-start.3 = (f32[152,128]{1,0:T(8,128)S(1)}, f32[152,128]{1,0:T(8,128)S(1)}, u32[]{:S(2)}, u32[]{:S(2)}) collective-permute-start(f32[152,128]{1,0:T(8,128)S(1)} %get-tuple-element.13), channel_id=1, source_target_pairs={{0,2},{2,0},{4,6},{6,4},{8,10},{10,8},{12,14},{14,12},{1,3},{3,1},... | collective-permute-start | bytes 233480 | tf_op jit(solution)/shard_map/ppermute | solution.py:294
  20.6 5.9 %collective-permute-start.4 = (f32[152,128]{1,0:T(8,128)S(1)}, f32[152,128]{1,0:T(8,128)S(1)}, u32[]{:S(2)}, u32[]{:S(2)}) collective-permute-start(f32[152,128]{1,0:T(8,128)S(1)} %add.13), channel_id=1, source_target_pairs={{0,4},{2,6},{4,0},{6,2},{8,12},{10,14},{12,8},{14,10},{1,5},{3,7},... | collective-permute-start | bytes 233480 | tf_op jit(solution)/shard_map/ppermute | solution.py:294
  26.5 5.5 %collective-permute-start.5 = (f32[152,128]{1,0:T(8,128)S(1)}, f32[152,128]{1,0:T(8,128)S(1)}, u32[]{:S(2)}, u32[]{:S(2)}) collective-permute-start(f32[152,128]{1,0:T(8,128)S(1)} %add.14), channel_id=1, source_target_pairs={{0,8},{2,10},{4,12},{6,14},{8,0},{10,2},{12,4},{14,6},{1,9},{3,11}... | collective-permute-start | bytes 233480 | tf_op jit(solution)/shard_map/ppermute | solution.py:294
  32.0 1.3 %collective-permute-start.6 = (f32[152,128]{1,0:T(8,128)S(1)}, f32[152,128]{1,0:T(8,128)S(1)}, u32[]{:S(2)}, u32[]{:S(2)}) collective-permute-start(f32[152,128]{1,0:T(8,128)S(1)} %add.15.mine_ref), channel_id=1, source_target_pairs={{0,1},{1,0},{2,3},{3,2},{4,5},{5,4},{6,7},{7,6},{8,9},{9,8},{10,11... | collective-permute-start | bytes 233480 | tf_op jit(solution)/shard_map/ppermute | solution.py:294

commit v6 on v5

--- a/solution.py
+++ b/solution.py
@@ -15,6 +15,7 @@
 NEAR = 8
 FAR = 8
 PARTS = 6
+OUTSIDE = -64
 HALF = LANES + 8
 
 
@@ -41,52 +42,83 @@
     return total
 
 
-def filter_kernel(
-    place_ref, fine_hbm, taps_hbm, own_ref, ext_ref, fine_ref, taps_ref, plane_ref, row_ref, sems
-):
-    fields = fine_ref.shape[0]
-    part = fields // PARTS
-    taps_copy = pltpu.make_async_copy(taps_hbm, taps_ref, sems.at[PARTS])
-    taps_copy.start()
-    copies = [
-        pltpu.make_async_copy(fine_hbm.at[p * part : (p + 1) * part], fine_ref.at[p * part : (p + 1) * part], sems.at[p])
-        for p in range(PARTS)
-    ]
+def start_copies(pairs, sems):
+    copies = [pltpu.make_async_copy(source, target, sems.at[i]) for i, (source, target) in enumerate(pairs)]
     for copy in copies:
         copy.start()
-    first = place_ref[0] == 0
-    slot, cell = iota((64, 256), 0), iota((64, 256), 1)
-    span_slot, sect_slot = slot // 8, slot % 8
-    span_cell = jnp.where(span_slot < 6, span_slot, span_slot - 8)
-    sect_cell = jnp.where((sect_slot < 4) | first, sect_slot, sect_slot - 6)
-    span_tap = cell % 16 - 4 * span_cell + 8
-    sect_tap = jnp.where(sect_slot < 6, cell // 16 - 4 * sect_cell + 8, -1)
-    taps_copy.wait()
-    plane = weights_at(span_tap, taps_ref, 1) * weights_at(sect_tap, taps_ref, 0)
-    plane = jnp.concatenate(split2(plane), axis=0)
+    return copies
+
+
+def cells_of(fine_hbm, fine_ref):
+    part = fine_ref.shape[0] // PARTS
+    return [
+        (fine_hbm.at[p * part : (p + 1) * part], fine_ref.at[p * part : (p + 1) * part]) for p in range(PARTS)
+    ]
+
+
+def plane_matrix(span_cells, sect_cells, taps_ref):
+    row, cell = iota((8, 256), 0), iota((8, 256), 1)
+    pick = lambda cells: sum(jnp.where(row == s, at, 0) for s, at in enumerate(cells))
+    span = weights_at(cell % 16 - 4 * pick(span_cells) + 8, taps_ref, 1)
+    sect = weights_at(cell // 16 - 4 * pick(sect_cells) + 8, taps_ref, 0)
+    rows = [jnp.broadcast_to(span[s : s + 1], (8, 256)) * sect for s in range(len(span_cells))]
+    return jnp.concatenate(split2(jnp.concatenate(rows, axis=0)), axis=0)
+
+
+def stream_matrix(taps_ref):
     cell, lane = iota((LANES, LANES), 0), iota((LANES, LANES), 1)
     stream = weights_at(cell - 4 * (lane % 32) + 8, taps_ref, 2)
+    high = stream.astype(BF16).astype(F32)
     parts = [
         jnp.concatenate([jnp.where(lane // 32 == s, term, 0.0) for s in range(4)], axis=0).astype(BF16)
-        for term in (stream.astype(BF16).astype(F32), stream - stream.astype(BF16).astype(F32))
+        for term in (high, stream - high)
     ]
-    matrix = jnp.concatenate([parts[0], parts[0], parts[1]], axis=0)
+    return jnp.concatenate([parts[0], parts[0], parts[1]], axis=0)
+
+
+def filter_plane(matrix, fine_ref, plane_ref, copies=None):
+    part = fine_ref.shape[0] // PARTS
+    half = matrix.shape[0] // 2
     for p in range(PARTS):
-        copies[p].wait()
+        if copies:
+            copies[p].wait()
         for field in range(p * part, (p + 1) * part):
-            both = jnp.dot(plane, fine_ref[field], preferred_element_type=F32)
-            summed = both[:64] + both[64:]
-            for s in range(8):
+            both = jnp.dot(matrix, fine_ref[field], preferred_element_type=F32)
+            summed = both[:half] + both[half:]
+            for s in range(half // 8):
                 plane_ref[s, 8 * field : 8 * field + 8, :] = summed[8 * s : 8 * s + 8]
-    for half, out_ref in enumerate((own_ref, ext_ref)):
-        values = jnp.concatenate([plane_ref[4 * half + s] for s in range(4)], axis=1)
-        high, low = split2(values)
-        row_ref[half] = jnp.dot(
-            jnp.concatenate([high, low, high], axis=1), matrix, preferred_element_type=F32
-        )
-        for comp in range(3):
-            for k in range(6):
-                out_ref[comp, k] = row_ref[half, pl.ds(8 * comp + k, 8, stride=24), :]
+
+
+def filter_stream(plane_ref, tiles, matrix):
+    rows = [
+        jnp.concatenate([plane_ref[s, pl.ds(8 * comp + k, 8, stride=24), :] for s, k in slots], axis=1)
+        for comp, slots in tiles
+    ]
+    high, low = split2(jnp.concatenate(rows, axis=0))
+    return jnp.dot(jnp.concatenate([high, low, high], axis=1), matrix, preferred_element_type=F32)
+
+
+def sect_cells(first):
+    return [0, 1, 2, 3, jnp.where(first, 4, -2), jnp.where(first, 5, -1), OUTSIDE, OUTSIDE]
+
+
+def sent_kernel(fine_hbm, taps_hbm, near_ref, far_ref, fine_ref, taps_ref, plane_ref, sems):
+    *copies, taps_copy = start_copies(cells_of(fine_hbm, fine_ref) + [(taps_hbm, taps_ref)], sems)
+    even = lax.axis_index("span") % 2 == 0
+    span_cells = [jnp.where(even, at, at - 6) for at in (4, 5)] + [jnp.where(even, at - 6, at) for at in (4, 5)]
+    taps_copy.wait()
+    matrix = plane_matrix(span_cells, sect_cells(lax.axis_index("sect") == 0), taps_ref)
+    filter_plane(matrix, fine_ref, plane_ref, copies)
+    matrix = stream_matrix(taps_ref)
+    for base, out_ref in ((0, near_ref), (2, far_ref)):
+        tiles = [
+            (comp, [(base + s, 2 * pair + k) for k in range(2) for s in range(2)])
+            for comp in range(3)
+            for pair in range(3)
+        ]
+        result = filter_stream(plane_ref, tiles, matrix)
+        for t in range(len(tiles)):
+            out_ref[t] = result[8 * t : 8 * t + 8]
 
 
 def fold(gram, kept_ref, sent_ref, first):
@@ -101,26 +133,54 @@
     sent_ref[LANES:] = corner
 
 
-def old_kernel(total, place_ref, stored_ref, after_ref, kept_ref, sent_ref):
+def own_kernel(
+    total, stored_ref, fine_ref, taps_hbm, own_ref, kept_ref, sent_ref, taps_ref, plane_ref, sems
+):
+    (taps_copy,) = start_copies([(taps_hbm, taps_ref)], sems)
     old, cells = stored_ref.shape
     rows = jnp.concatenate([stored_ref[...], jnp.zeros((8, cells), BF16)], axis=0)
     gram = lax.dot_general(rows, rows, (((1,), (1,)), ((), ())), preferred_element_type=F32) / total
-    fold(gram, kept_ref, sent_ref, place_ref[0] == 0)
-
-
-def new_kernel(
-    total, place_ref, stored_ref, own_ref, left_ref, right_ref, partner_ref, kept_ref, coarse_ref, sums_ref
-):
-    first = place_ref[0] == 0
+    fold(gram, kept_ref, sent_ref, lax.axis_index("sect") == 0)
+    taps_copy.wait()
+    matrix = plane_matrix([0, 1, 2, 3], sect_cells(lax.axis_index("sect") == 0), taps_ref)
+    filter_plane(matrix, fine_ref, plane_ref)
+    tiles = [(comp, [(s, k) for s in range(4)]) for comp in range(3) for k in range(6)]
+    result = filter_stream(plane_ref, tiles, stream_matrix(taps_ref))
+    for t in range(len(tiles)):
+        own_ref[t] = result[8 * t : 8 * t + 8]
+
+
+def join_kernel(own_ref, near_ref, far_ref, sent_ref, cells_ref, swap_ref):
+    even = lax.axis_index("span") % 2 == 0
+    half = sent_ref.shape[0]
+    lane = iota((8, LANES), 1)
+    swap_ref[:half] = sent_ref[...]
+    for comp in range(3):
+        for pair in range(3):
+            near, far = near_ref[3 * comp + pair], far_ref[3 * comp + pair]
+            before, after = jnp.where(even, far, near), jnp.where(even, near, far)
+            shares = (
+                jnp.where(lane < 64, before, pltpu.roll(after, 64, 1)),
+                jnp.where(lane < 64, pltpu.roll(before, 64, 1), after),
+            )
+            for k in range(2):
+                value = own_ref[6 * comp + 2 * pair + k] + shares[k]
+                if pair < 2:
+                    cells_ref[4 * comp + 2 * pair + k] = value
+                else:
+                    at = half + 8 * (2 * comp + k)
+                    swap_ref[at : at + 8, :] = value
+
+
+def new_kernel(total, stored_ref, cells_ref, partner_ref, kept_ref, coarse_ref, sums_ref):
+    first = lax.axis_index("sect") == 0
     half = kept_ref.shape[0]
-    lane = iota((8, LANES), 1)
     cells = []
     for comp in range(3):
         for k in range(4):
-            value = own_ref[comp, k] + jnp.where(lane < 64, left_ref[comp, k], right_ref[comp, k])
             here = first if k >= 2 else jnp.logical_not(first)
             at = half + 8 * (2 * comp + k % 2)
-            cells.append(value + jnp.where(here, partner_ref[at : at + 8, :], 0.0))
+            cells.append(cells_ref[4 * comp + k] + jnp.where(here, partner_ref[at : at + 8, :], 0.0))
     coarse = jnp.concatenate(cells, axis=1).astype(BF16)
     coarse_ref[...] = coarse
     rows = jnp.concatenate([stored_ref[...], coarse], axis=0)
@@ -171,11 +231,11 @@
 
 
 def factor_kernel(
-    place_ref, mine_ref, other_ref, stored_ref, coarse_ref, new_hbm, factor_hbm, basis_hbm,
+    mine_ref, other_ref, stored_ref, coarse_ref, new_hbm, factor_hbm, basis_hbm,
     left_ref, inverse_ref, upper_ref, factor_ref, basis_ref, scale_ref, window_ref, sems,
 ):
-    first = place_ref[0] == 0
-    none = jnp.full((8, LANES), jnp.minimum(place_ref[0], 0).astype(F32))
+    first = lax.axis_index("sect") == 0
+    none = jnp.full((8, LANES), jnp.minimum(lax.axis_index("sect"), 0).astype(F32))
     size = left_ref.shape[0]
     row, col = iota((LANES, LANES), 0), iota((LANES, LANES), 1)
     packed = jnp.where(first, mine_ref[:LANES], other_ref[:LANES])
@@ -259,13 +319,13 @@
         copy.wait()
 
 
-def factorise(place, mine, other, stored, coarse):
+def factorise(mine, other, stored, coarse):
     old, rows_dev = stored.shape
     size = old + coarse.shape[0]
     return pl.pallas_call(
         factor_kernel,
         out_shape=[shaped(coarse.shape, BF16), shaped((size, size)), shaped((size, rows_dev))],
-        in_specs=[SMEM] + [VMEM] * 4,
+        in_specs=[VMEM] * 4,
         out_specs=[HBM] * 3,
         scratch_shapes=[pltpu.VMEM((size, size), F32)] * 4
         + [
@@ -276,12 +336,11 @@
         ],
         compiler_params=LIMIT,
         name="factor",
-    )(place, mine, other, stored, coarse)
+    )(mine, other, stored, coarse)
 
 
 VMEM = pl.BlockSpec(memory_space=pltpu.VMEM)
 HBM = pl.BlockSpec(memory_space=pltpu.HBM)
-SMEM = pl.BlockSpec(memory_space=pltpu.SMEM)
 LIMIT = pltpu.CompilerParams(vmem_limit_bytes=48 * 2**20)
 
 
@@ -294,9 +353,10 @@
     return lax.ppermute(values, axis, [(i, i ^ bit) for i in range(count)])
 
 
-def shift(values, axis, step):
+def swap_pairs(values, axis, begin):
     count = lax.axis_size(axis)
-    return lax.ppermute(values, axis, [(i, i + step) for i in range(count) if 0 <= i + step < count])
+    pairs = [(i, i + 1) for i in range(begin, count - 1, 2)]
+    return lax.ppermute(values, axis, pairs + [(j, i) for i, j in pairs])
 
 
 def sum_over_span(values):
@@ -316,46 +376,49 @@
     assert lax.axis_size("sect") == 2
     old, rows_dev = stored.shape
     total = rows_dev * lax.axis_size("span") * lax.axis_size("sect")
-    place = lax.axis_index("sect").astype(jnp.int32).reshape(1)
     fields = snapshots * comps
-    own, ext = pl.pallas_call(
-        filter_kernel,
-        out_shape=[shaped((comps, 6, snapshots, LANES))] * 2,
-        in_specs=[SMEM, HBM, HBM],
-        out_specs=[VMEM] * 2,
-        scratch_shapes=[
-            pltpu.VMEM((fields, cells_y * cells_z, cells_x), BF16),
-            pltpu.SMEM(filter_taps.shape, F32),
-            pltpu.VMEM((8, 8 * fields, LANES), F32),
-            pltpu.VMEM((2, 8 * fields, LANES), F32),
-            pltpu.SemaphoreType.DMA((PARTS + 1,)),
-        ],
-        compiler_params=pltpu.CompilerParams(vmem_limit_bytes=55 * 2**20),
-        name="filter",
-    )(place, fine_field.reshape(fields, cells_y * cells_z, cells_x), filter_taps)
-    left = shift(ext, "span", 1)
-    right = shift(ext, "span", -1)
-    kept, sent = pl.pallas_call(
-        functools.partial(old_kernel, total),
-        out_shape=[shaped((HALF, LANES))] * 2,
-        in_specs=[SMEM, VMEM, VMEM],
+    fine = fine_field.reshape(fields, cells_y * cells_z, cells_x)
+    fine = pltpu.with_memory_space_constraint(fine, pltpu.HBM)
+    taps = pltpu.with_memory_space_constraint(filter_taps, pltpu.HBM)
+    room = [pltpu.SMEM(taps.shape, F32), pltpu.VMEM((4, 8 * fields, LANES), F32)]
+    near, far, fine = pl.pallas_call(
+        sent_kernel,
+        out_shape=[pltpu.VMEM((9, snapshots, LANES), F32)] * 2 + [pltpu.VMEM(fine.shape, BF16)],
+        in_specs=[HBM, HBM],
+        out_specs=[VMEM] * 3,
+        scratch_shapes=room + [pltpu.SemaphoreType.DMA((PARTS + 1,))],
+        compiler_params=LIMIT,
+        name="filter_sent",
+    )(fine, taps)
+    from_far = swap_pairs(far, "span", 1)
+    from_near = swap_pairs(near, "span", 0)
+    own, kept, sent = pl.pallas_call(
+        functools.partial(own_kernel, total),
+        out_shape=[shaped((18, snapshots, LANES))] + [shaped((HALF, LANES))] * 2,
+        in_specs=[VMEM, VMEM, HBM],
+        out_specs=[VMEM] * 3,
+        scratch_shapes=room + [pltpu.SemaphoreType.DMA((1,))],
+        compiler_params=LIMIT,
+        name="filter_own",
+    )(stored, fine, taps)
+    cells, crossing = pl.pallas_call(
+        join_kernel,
+        out_shape=[shaped((12, snapshots, LANES)), shaped((HALF + 6 * snapshots, LANES))],
+        in_specs=[VMEM] * 4,
         out_specs=[VMEM] * 2,
         compiler_params=LIMIT,
-        name="gram_stored",
-    )(place, stored, own)
-    lanes = lax.broadcasted_iota(jnp.int32, (1, 1, 1, LANES), 3)
-    halo = own[:, 4:] + jnp.where(lanes < 64, left[:, 4:], right[:, 4:])
-    partner = swap(jnp.concatenate([sent, halo.reshape(-1, LANES)], axis=0), "sect", 1)
+        name="join",
+    )(own, from_near, from_far, sent)
     coarse, sums = pl.pallas_call(
         functools.partial(new_kernel, total),
         out_shape=[shaped((snapshots, rows_dev), BF16), shaped((HALF + 2 * snapshots, LANES))],
-        in_specs=[SMEM] + [VMEM] * 6,
+        in_specs=[VMEM] * 4,
         out_specs=[VMEM] * 2,
         compiler_params=LIMIT,
         name="gram_new",
-    )(place, stored, own, left, right, partner, kept)
+    )(stored, cells, swap(crossing, "sect", 1), kept)
     sums = sum_over_span(sums)
-    return tuple(factorise(place, sums, swap(sums, "sect", 1), stored, coarse))
+    return tuple(factorise(sums, swap(sums, "sect", 1), stored, coarse))
 
 
 def solution(mesh):

time: 40.6 us -> 37.1 us (0.914)
  starting transfers between devices: 16.1 us -> 14.5 us
  waiting for transfers between devices: 11.2 us -> 9.97 us
  local copies, waits for them, and re-layouts: 0.88 us -> 0.01 us
  Pallas kernels: 11.3 us -> 11.8 us
    ppermute x2, starting transfers between devices: 6.76 us -> 3.66 us  [swap_pairs(): return lax.ppermute(values, axis, pairs + [(j, i) for i, j in pairs])]
    ppermute x5, starting transfers between devices: 9.35 us -> 10.8 us  [swap(): return lax.ppermute(values, axis, [(i, i ^ bit) for i in range(count)])]
    ppermute x2, waiting for transfers between devices: 1.27 us -> 0.01 us  [swap_pairs(): return lax.ppermute(values, axis, pairs + [(j, i) for i, j in pairs])]
    unnamed x4 -> x2, local copies, waits for them, and re-layouts: 0.88 us -> 0.01 us
    pallas_call x2 -> x3, Pallas kernels: 3.97 us -> 4.39 us  [the longest x1 2.42 us: local(): pl.pallas_call(sent_kernel, out_shape=[pltpu.VMEM((9, snapshots, LANES),...]
  transfers between devices with their start and end apart: 7 -> 7, of which waited for: 6 -> 5; matrix products, arithmetic and copies ran while one was open for 0% -> 0% of each run, Pallas kernels for 1% -> 5%
where the time goes in v6:
time: 37.1 us; the launch traced here: 36.9 us
  starting transfers between devices  14.5 us (39%)
  Pallas kernels  11.8 us (32%)
  waiting for transfers between devices  9.97 us (27%)
  between operations  0.72 us (2%)
    ppermute x5, starting transfers between devices, swap(): return lax.ppermute(values, axis, [(i, i ^ bit) for i in range(count)])  10.8 us
    ppermute x5, waiting for transfers between devices, swap(): return lax.ppermute(values, axis, [(i, i ^ bit) for i in range(count)])  9.97 us
    pallas_call x1, Pallas kernels, factorise(): pl.pallas_call(factor_kernel, out_shape=[shaped(coarse.shape, BF16), shap...  7.06 us
    ppermute x2, starting transfers between devices, swap_pairs(): return lax.ppermute(values, axis, pairs + [(j, i) for i, j in pairs])  3.66 us
    pallas_call x1, Pallas kernels, local(): pl.pallas_call(sent_kernel, out_shape=[pltpu.VMEM((9, snapshots, LANES),...  2.42 us
    pallas_call x1, Pallas kernels, local(): pl.pallas_call(functools.partial(own_kernel, total), out_shape=[shaped((1...  1.88 us
  transfers between devices with their start and end apart: 7, of which 5 were waited for; matrix products, arithmetic and copies ran while one was open for 0% of the time, Pallas kernels for 5%

profile of v6, /device:TPU:0, one launch (start us, length us, event | category | flops | bytes accessed | tf_op | source)
XLA Modules:
  0.0 36.9 jit_solution(17535551908160029925)
XLA Ops:
  0.6 0.0 copy-start
  0.6 2.4 %filter_sent.1 = (f32[9,8,128]{2,1,0:T(8,128)S(1)}, f32[9,8,128]{2,1,0:T(8,128)S(1)}, bf16[24,256,128]{2,1,0:T(8,128)(2,1)S(1)}) custom-call(bf16[24,256,128]{2,1,0:T(8,128)(2,1)} %bitcast.1, f32[3,17]{1,0:T(4,128)} %taps_hbm.3), custom_call_target="tpu_custom_call" | custom-call | tf_op jit(solution)/shard_map/filter_sent/pallas_call | solution.py:384
  3.1 3.0 %collective-permute-start = (f32[9,8,128]{2,1,0:T(8,128)S(1)}, f32[9,8,128]{2,1,0:T(8,128)S(1)}, u32[]{:S(2)}, u32[]{:S(2)}) collective-permute-start(f32[9,8,128]{2,1,0:T(8,128)S(1)} %get-tuple-element.15), channel_id=1, source_target_pairs={{0,2},{4,6},{8,10},{12,14},{2,0},{6,4},{10,8},{14,12},{1,3},{5,7},... | collective-permute-start | bytes 110600 | tf_op jit(solution)/shard_map/ppermute | solution.py:359
  6.1 0.7 %collective-permute-start.1 = (f32[9,8,128]{2,1,0:T(8,128)S(1)}, f32[9,8,128]{2,1,0:T(8,128)S(1)}, u32[]{:S(2)}, u32[]{:S(2)}) collective-permute-start(f32[9,8,128]{2,1,0:T(8,128)S(1)} %get-tuple-element.16), channel_id=1, source_target_pairs={{2,4},{6,8},{10,12},{4,2},{8,6},{12,10},{3,5},{7,9},{11,13},{5,3},... | collective-permute-start | bytes 110600 | tf_op jit(solution)/shard_map/ppermute | solution.py:359
  6.7 0.0 copy-done
  6.7 1.9 %filter_own.1 = (f32[18,8,128]{2,1,0:T(8,128)S(1)}, f32[136,128]{1,0:T(8,128)S(1)}, f32[136,128]{1,0:T(8,128)S(1)}) custom-call(bf16[248,1536]{1,0:T(8,128)(2,1)S(1)} %copy-done, bf16[24,256,128]{2,1,0:T(8,128)(2,1)S(1)} %get-tuple-element.13.fine_ref, f32[3,17]{1,0:T(4,128)} %taps_hbm.3), custom_call_target="tpu_custom_call" | custom-call | tf_op jit(solution)/shard_map/filter_own/pallas_call | solution.py:395
  8.6 0.0 collective-permute-done.near_ref
  8.6 0.0 collective-permute-done.1.far_ref
  8.6 0.1 join.1
  8.7 0.1 collective-permute-start.2
  8.8 1.3 %collective-permute-done.2.partner_ref = f32[184,128]{1,0:T(8,128)S(1)} collective-permute-done((f32[184,128]{1,0:T(8,128)S(1)}, f32[184,128]{1,0:T(8,128)S(1)}, u32[]{:S(2)}, u32[]{:S(2)}) %collective-permute-start.2) | collective-permute-done | bytes 94240 | tf_op jit(solution)/shard_map/ppermute | solution.py:353
  10.1 0.3 gram_new.1
  10.4 4.3 %collective-permute-start.3 = (f32[152,128]{1,0:T(8,128)S(1)}, f32[152,128]{1,0:T(8,128)S(1)}, u32[]{:S(2)}, u32[]{:S(2)}) collective-permute-start(f32[152,128]{1,0:T(8,128)S(1)} %get-tuple-element.21), channel_id=1, source_target_pairs={{0,2},{2,0},{4,6},{6,4},{8,10},{10,8},{12,14},{14,12},{1,3},{3,1},... | collective-permute-start | bytes 233480 | tf_op jit(solution)/shard_map/ppermute | solution.py:353
  14.7 2.7 %collective-permute-done.3 = f32[152,128]{1,0:T(8,128)S(1)} collective-permute-done((f32[152,128]{1,0:T(8,128)S(1)}, f32[152,128]{1,0:T(8,128)S(1)}, u32[]{:S(2)}, u32[]{:S(2)}) %collective-permute-start.3) | collective-permute-done | bytes 77856 | tf_op jit(solution)/shard_map/ppermute | solution.py:353
  17.4 3.3 %collective-permute-start.4 = (f32[152,128]{1,0:T(8,128)S(1)}, f32[152,128]{1,0:T(8,128)S(1)}, u32[]{:S(2)}, u32[]{:S(2)}) collective-permute-start(f32[152,128]{1,0:T(8,128)S(1)} %add.9), channel_id=1, source_target_pairs={{0,4},{2,6},{4,0},{6,2},{8,12},{10,14},{12,8},{14,10},{1,5},{3,7},... | collective-permute-start | bytes 233480 | tf_op jit(solution)/shard_map/ppermute | solution.py:353
  20.7 2.4 %collective-permute-done.4 = f32[152,128]{1,0:T(8,128)S(1)} collective-permute-done((f32[152,128]{1,0:T(8,128)S(1)}, f32[152,128]{1,0:T(8,128)S(1)}, u32[]{:S(2)}, u32[]{:S(2)}) %collective-permute-start.4) | collective-permute-done | bytes 77856 | tf_op jit(solution)/shard_map/ppermute | solution.py:353
  23.1 3.1 %collective-permute-start.5 = (f32[152,128]{1,0:T(8,128)S(1)}, f32[152,128]{1,0:T(8,128)S(1)}, u32[]{:S(2)}, u32[]{:S(2)}) collective-permute-start(f32[152,128]{1,0:T(8,128)S(1)} %add.10), channel_id=1, source_target_pairs={{0,8},{2,10},{4,12},{6,14},{8,0},{10,2},{12,4},{14,6},{1,9},{3,11}... | collective-permute-start | bytes 233480 | tf_op jit(solution)/shard_map/ppermute | solution.py:353
  26.2 2.4 %collective-permute-done.5 = f32[152,128]{1,0:T(8,128)S(1)} collective-permute-done((f32[152,128]{1,0:T(8,128)S(1)}, f32[152,128]{1,0:T(8,128)S(1)}, u32[]{:S(2)}, u32[]{:S(2)}) %collective-permute-start.5) | collective-permute-done | bytes 77856 | tf_op jit(solution)/shard_map/ppermute | solution.py:353
  28.5 0.1 collective-permute-start.6
  28.6 1.3 %collective-permute-done.6.other_ref = f32[152,128]{1,0:T(8,128)S(1)} collective-permute-done((f32[152,128]{1,0:T(8,128)S(1)}, f32[152,128]{1,0:T(8,128)S(1)}, u32[]{:S(2)}, u32[]{:S(2)}) %collective-permute-start.6) | collective-permute-done | bytes 77856 | tf_op jit(solution)/shard_map/ppermute | solution.py:353
  29.9 7.1 %factor.1 = (bf16[8,1536]{1,0:T(8,128)(2,1)}, f32[256,256]{1,0:T(8,128)}, f32[256,1536]{1,0:T(8,128)}) custom-call(f32[152,128]{1,0:T(8,128)S(1)} %add.11.mine_ref, f32[152,128]{1,0:T(8,128)S(1)} %collective-permute-done.6.other_ref, bf16[248,1536]{1,0:T(8,128)(2,1)S(1)} %copy-done, bf16[8,1536]{1,0:T(8,128)(2,1)S(1)} %get-tuple-element.22.coarse_ref), custom_call_target="tpu_custom_call" | custom-call | tf_op jit(solution)/shard_map/factor/pallas_call | solution.py:325
  (3 shorter events, 0.0 us)
Async XLA Ops:
  0.6 6.1 %copy-start = (bf16[248,1536]{1,0:T(8,128)(2,1)S(1)}, bf16[248,1536]{1,0:T(8,128)(2,1)}, u32[]{:S(2)}) copy-start(bf16[248,1536]{1,0:T(8,128)(2,1)} %stored_ref.5) | copy-start | bytes 2285572
  3.1 5.6 %collective-permute-start = (f32[9,8,128]{2,1,0:T(8,128)S(1)}, f32[9,8,128]{2,1,0:T(8,128)S(1)}, u32[]{:S(2)}, u32[]{:S(2)}) collective-permute-start(f32[9,8,128]{2,1,0:T(8,128)S(1)} %get-tuple-element.15), channel_id=1, source_target_pairs={{0,2},{4,6},{8,10},{12,14},{2,0},{6,4},{10,8},{14,12},{1,3},{5,7},... | collective-permute-start | bytes 110600 | tf_op jit(solution)/shard_map/ppermute | solution.py:359
  6.1 2.6 %collective-permute-start.1 = (f32[9,8,128]{2,1,0:T(8,128)S(1)}, f32[9,8,128]{2,1,0:T(8,128)S(1)}, u32[]{:S(2)}, u32[]{:S(2)}) collective-permute-start(f32[9,8,128]{2,1,0:T(8,128)S(1)} %get-tuple-element.16), channel_id=1, source_target_pairs={{2,4},{6,8},{10,12},{4,2},{8,6},{12,10},{3,5},{7,9},{11,13},{5,3},... | collective-permute-start | bytes 110600 | tf_op jit(solution)/shard_map/ppermute | solution.py:359
  8.7 1.4 %collective-permute-start.2 = (f32[184,128]{1,0:T(8,128)S(1)}, f32[184,128]{1,0:T(8,128)S(1)}, u32[]{:S(2)}, u32[]{:S(2)}) collective-permute-start(f32[184,128]{1,0:T(8,128)S(1)} %get-tuple-element.19), channel_id=1, source_target_pairs={{0,1},{1,0},{2,3},{3,2},{4,5},{5,4},{6,7},{7,6},{8,9},{9,8},{10,11... | collective-permute-start | bytes 282632 | tf_op jit(solution)/shard_map/ppermute | solution.py:353
  10.4 7.0 %collective-permute-start.3 = (f32[152,128]{1,0:T(8,128)S(1)}, f32[152,128]{1,0:T(8,128)S(1)}, u32[]{:S(2)}, u32[]{:S(2)}) collective-permute-start(f32[152,128]{1,0:T(8,128)S(1)} %get-tuple-element.21), channel_id=1, source_target_pairs={{0,2},{2,0},{4,6},{6,4},{8,10},{10,8},{12,14},{14,12},{1,3},{3,1},... | collective-permute-start | bytes 233480 | tf_op jit(solution)/shard_map/ppermute | solution.py:353
  17.4 5.6 %collective-permute-start.4 = (f32[152,128]{1,0:T(8,128)S(1)}, f32[152,128]{1,0:T(8,128)S(1)}, u32[]{:S(2)}, u32[]{:S(2)}) collective-permute-start(f32[152,128]{1,0:T(8,128)S(1)} %add.9), channel_id=1, source_target_pairs={{0,4},{2,6},{4,0},{6,2},{8,12},{10,14},{12,8},{14,10},{1,5},{3,7},... | collective-permute-start | bytes 233480 | tf_op jit(solution)/shard_map/ppermute | solution.py:353
  23.1 5.5 %collective-permute-start.5 = (f32[152,128]{1,0:T(8,128)S(1)}, f32[152,128]{1,0:T(8,128)S(1)}, u32[]{:S(2)}, u32[]{:S(2)}) collective-permute-start(f32[152,128]{1,0:T(8,128)S(1)} %add.10), channel_id=1, source_target_pairs={{0,8},{2,10},{4,12},{6,14},{8,0},{10,2},{12,4},{14,6},{1,9},{3,11}... | collective-permute-start | bytes 233480 | tf_op jit(solution)/shard_map/ppermute | solution.py:353
  28.5 1.3 %collective-permute-start.6 = (f32[152,128]{1,0:T(8,128)S(1)}, f32[152,128]{1,0:T(8,128)S(1)}, u32[]{:S(2)}, u32[]{:S(2)}) collective-permute-start(f32[152,128]{1,0:T(8,128)S(1)} %add.11.mine_ref), channel_id=1, source_target_pairs={{0,1},{1,0},{2,3},{3,2},{4,5},{5,4},{6,7},{7,6},{8,9},{9,8},{10,11... | collective-permute-start | bytes 233480 | tf_op jit(solution)/shard_map/ppermute | solution.py:353

commit v7 on v6

--- a/solution.py
+++ b/solution.py
@@ -14,7 +14,7 @@
 PANEL = 64
 NEAR = 8
 FAR = 8
-PARTS = 6
+PARTS = 2
 OUTSIDE = -64
 HALF = LANES + 8
 
@@ -102,14 +102,19 @@
     return [0, 1, 2, 3, jnp.where(first, 4, -2), jnp.where(first, 5, -1), OUTSIDE, OUTSIDE]
 
 
-def sent_kernel(fine_hbm, taps_hbm, near_ref, far_ref, fine_ref, taps_ref, plane_ref, sems):
-    *copies, taps_copy = start_copies(cells_of(fine_hbm, fine_ref) + [(taps_hbm, taps_ref)], sems)
+def sent_kernel(
+    fine_hbm, taps_hbm, near_ref, far_ref, fine_ref, own_matrix_ref, stream_ref, taps_ref, plane_ref, sems
+):
+    taps_copy, *copies = start_copies([(taps_hbm, taps_ref)] + cells_of(fine_hbm, fine_ref), sems)
     even = lax.axis_index("span") % 2 == 0
     span_cells = [jnp.where(even, at, at - 6) for at in (4, 5)] + [jnp.where(even, at - 6, at) for at in (4, 5)]
     taps_copy.wait()
-    matrix = plane_matrix(span_cells, sect_cells(lax.axis_index("sect") == 0), taps_ref)
+    sect = sect_cells(lax.axis_index("sect") == 0)
+    matrix = plane_matrix(span_cells, sect, taps_ref)
+    stream_ref[...] = stream_matrix(taps_ref)
+    own_matrix_ref[...] = plane_matrix([0, 1, 2, 3], sect, taps_ref)
     filter_plane(matrix, fine_ref, plane_ref, copies)
-    matrix = stream_matrix(taps_ref)
+    matrix = stream_ref[...]
     for base, out_ref in ((0, near_ref), (2, far_ref)):
         tiles = [
             (comp, [(base + s, 2 * pair + k) for k in range(2) for s in range(2)])
@@ -134,35 +139,45 @@
 
 
 def own_kernel(
-    total, stored_ref, fine_ref, taps_hbm, own_ref, kept_ref, sent_ref, taps_ref, plane_ref, sems
+    total, stored_hbm, fine_ref, matrix_ref, stream_ref, own_ref, kept_ref, sent_ref, stored_ref, plane_ref, sems
 ):
-    (taps_copy,) = start_copies([(taps_hbm, taps_ref)], sems)
+    (copy,) = start_copies([(stored_hbm, stored_ref)], sems)
+    filter_plane(matrix_ref[...], fine_ref, plane_ref)
+    tiles = [(comp, [(s, k) for s in range(4)]) for comp in range(3) for k in range(6)]
+    result = filter_stream(plane_ref, tiles, stream_ref[...])
+    for t in range(len(tiles)):
+        own_ref[t] = result[8 * t : 8 * t + 8]
+    copy.wait()
     old, cells = stored_ref.shape
     rows = jnp.concatenate([stored_ref[...], jnp.zeros((8, cells), BF16)], axis=0)
     gram = lax.dot_general(rows, rows, (((1,), (1,)), ((), ())), preferred_element_type=F32) / total
     fold(gram, kept_ref, sent_ref, lax.axis_index("sect") == 0)
-    taps_copy.wait()
-    matrix = plane_matrix([0, 1, 2, 3], sect_cells(lax.axis_index("sect") == 0), taps_ref)
-    filter_plane(matrix, fine_ref, plane_ref)
-    tiles = [(comp, [(s, k) for s in range(4)]) for comp in range(3) for k in range(6)]
-    result = filter_stream(plane_ref, tiles, stream_matrix(taps_ref))
-    for t in range(len(tiles)):
-        own_ref[t] = result[8 * t : 8 * t + 8]
-
-
-def join_kernel(own_ref, near_ref, far_ref, sent_ref, cells_ref, swap_ref):
-    even = lax.axis_index("span") % 2 == 0
+
+
+def place_shares(shares, before):
+    lane = iota((8, LANES), 1)
+    turned = pltpu.roll(shares, 64, 1)
+    here = jnp.where(before, lane, LANES - 1 - lane) < 64
+    return [jnp.where(here, jnp.where(before == (k == 0), shares, turned), 0.0) for k in range(2)]
+
+
+def join_far_kernel(own_ref, far_ref, cells_ref):
+    before = lax.axis_index("span") % 2 == 0
+    for comp in range(3):
+        for pair in range(3):
+            shares = place_shares(far_ref[3 * comp + pair], before)
+            for k in range(2):
+                at = 6 * comp + 2 * pair + k
+                cells_ref[at] = own_ref[at] + shares[k]
+
+
+def join_near_kernel(own_ref, near_ref, sent_ref, cells_ref, swap_ref):
+    before = lax.axis_index("span") % 2 == 1
     half = sent_ref.shape[0]
-    lane = iota((8, LANES), 1)
     swap_ref[:half] = sent_ref[...]
     for comp in range(3):
         for pair in range(3):
-            near, far = near_ref[3 * comp + pair], far_ref[3 * comp + pair]
-            before, after = jnp.where(even, far, near), jnp.where(even, near, far)
-            shares = (
-                jnp.where(lane < 64, before, pltpu.roll(after, 64, 1)),
-                jnp.where(lane < 64, pltpu.roll(before, 64, 1), after),
-            )
+            shares = place_shares(near_ref[3 * comp + pair], before)
             for k in range(2):
                 value = own_ref[6 * comp + 2 * pair + k] + shares[k]
                 if pair < 2:
@@ -380,35 +395,46 @@
     fine = fine_field.reshape(fields, cells_y * cells_z, cells_x)
     fine = pltpu.with_memory_space_constraint(fine, pltpu.HBM)
     taps = pltpu.with_memory_space_constraint(filter_taps, pltpu.HBM)
-    room = [pltpu.SMEM(taps.shape, F32), pltpu.VMEM((4, 8 * fields, LANES), F32)]
-    near, far, fine = pl.pallas_call(
+    plane = pltpu.VMEM((4, 8 * fields, LANES), F32)
+    near, far, fine, matrix, stream = pl.pallas_call(
         sent_kernel,
-        out_shape=[pltpu.VMEM((9, snapshots, LANES), F32)] * 2 + [pltpu.VMEM(fine.shape, BF16)],
-        in_specs=[HBM, HBM],
-        out_specs=[VMEM] * 3,
-        scratch_shapes=room + [pltpu.SemaphoreType.DMA((PARTS + 1,))],
+        out_shape=[pltpu.VMEM((9, snapshots, LANES), F32)] * 2
+        + [pltpu.VMEM(fine.shape, BF16), pltpu.VMEM((64, 256), BF16), pltpu.VMEM((12 * LANES, LANES), BF16)],
+        in_specs=[HBM] * 2,
+        out_specs=[VMEM] * 5,
+        scratch_shapes=[pltpu.SMEM(taps.shape, F32), plane, pltpu.SemaphoreType.DMA((PARTS + 1,))],
         compiler_params=LIMIT,
         name="filter_sent",
     )(fine, taps)
     from_far = swap_pairs(far, "span", 1)
     from_near = swap_pairs(near, "span", 0)
-    own, kept, sent = pl.pallas_call(
+    own, kept, sent, stored = pl.pallas_call(
         functools.partial(own_kernel, total),
-        out_shape=[shaped((18, snapshots, LANES))] + [shaped((HALF, LANES))] * 2,
-        in_specs=[VMEM, VMEM, HBM],
-        out_specs=[VMEM] * 3,
-        scratch_shapes=room + [pltpu.SemaphoreType.DMA((1,))],
+        out_shape=[shaped((18, snapshots, LANES))]
+        + [shaped((HALF, LANES))] * 2
+        + [pltpu.VMEM(stored.shape, BF16)],
+        in_specs=[HBM] + [VMEM] * 3,
+        out_specs=[VMEM] * 4,
+        scratch_shapes=[plane, pltpu.SemaphoreType.DMA((1,))],
         compiler_params=LIMIT,
         name="filter_own",
-    )(stored, fine, taps)
+    )(pltpu.with_memory_space_constraint(stored, pltpu.HBM), fine, matrix, stream)
+    own = pl.pallas_call(
+        join_far_kernel,
+        out_shape=shaped((18, snapshots, LANES)),
+        in_specs=[VMEM] * 2,
+        out_specs=VMEM,
+        compiler_params=LIMIT,
+        name="join_far",
+    )(own, from_far)
     cells, crossing = pl.pallas_call(
-        join_kernel,
+        join_near_kernel,
         out_shape=[shaped((12, snapshots, LANES)), shaped((HALF + 6 * snapshots, LANES))],
-        in_specs=[VMEM] * 4,
+        in_specs=[VMEM] * 3,
         out_specs=[VMEM] * 2,
         compiler_params=LIMIT,
-        name="join",
-    )(own, from_near, from_far, sent)
+        name="join_near",
+    )(own, from_near, sent)
     coarse, sums = pl.pallas_call(
         functools.partial(new_kernel, total),
         out_shape=[shaped((snapshots, rows_dev), BF16), shaped((HALF + 2 * snapshots, LANES))],

time: 37.1 us -> 35.9 us (0.968)
  starting transfers between devices: 14.5 us -> 13.1 us
  waiting for transfers between devices: 9.97 us -> 10.9 us
  Pallas kernels: 11.8 us -> 11 us
    ppermute x5, starting transfers between devices: 10.8 us -> 6.63 us  [swap(): return lax.ppermute(values, axis, [(i, i ^ bit) for i in range(count)])]
    ppermute x2, starting transfers between devices: 3.66 us -> 6.46 us  [swap_pairs(): return lax.ppermute(values, axis, pairs + [(j, i) for i, j in pairs])]
    ppermute x5, waiting for transfers between devices: 9.97 us -> 10.6 us  [swap(): return lax.ppermute(values, axis, [(i, i ^ bit) for i in range(count)])]
    pallas_call x1, Pallas kernels: 2.42 us -> 1.96 us  [local(): pl.pallas_call(sent_kernel, out_shape=[pltpu.VMEM((9, snapshots, LANES),...]
  transfers between devices with their start and end apart: 7 -> 7, of which waited for: 5 -> 6; matrix products, arithmetic and copies ran while one was open for 0% -> 0% of each run, Pallas kernels for 5% -> 5%
where the time goes in v7:
time: 35.9 us; the launch traced here: 35.7 us
  starting transfers between devices  13.1 us (36%)
  Pallas kernels  11 us (31%)
  waiting for transfers between devices  10.9 us (30%)
  between operations  0.7 us (2%)
    ppermute x5, waiting for transfers between devices, swap(): return lax.ppermute(values, axis, [(i, i ^ bit) for i in range(count)])  10.6 us
    pallas_call x1, Pallas kernels, factorise(): pl.pallas_call(factor_kernel, out_shape=[shaped(coarse.shape, BF16), shap...  7.06 us
    ppermute x5, starting transfers between devices, swap(): return lax.ppermute(values, axis, [(i, i ^ bit) for i in range(count)])  6.63 us
    ppermute x2, starting transfers between devices, swap_pairs(): return lax.ppermute(values, axis, pairs + [(j, i) for i, j in pairs])  6.46 us
    pallas_call x1, Pallas kernels, local(): pl.pallas_call(sent_kernel, out_shape=[pltpu.VMEM((9, snapshots, LANES),...  1.96 us
    pallas_call x1, Pallas kernels, local(): pl.pallas_call(functools.partial(own_kernel, total), out_shape=[shaped((1...  1.55 us
  transfers between devices with their start and end apart: 7, of which 6 were waited for; matrix products, arithmetic and copies ran while one was open for 0% of the time, Pallas kernels for 5%

profile of v7, /device:TPU:0, one launch (start us, length us, event | category | flops | bytes accessed | tf_op | source)
XLA Modules:
  0.0 35.7 jit_solution(1662715689867294621)
XLA Ops:
  0.6 2.0 %filter_sent.1 = (f32[9,8,128]{2,1,0:T(8,128)S(1)}, f32[9,8,128]{2,1,0:T(8,128)S(1)}, bf16[24,256,128]{2,1,0:T(8,128)(2,1)S(1)}, bf16[64,256]{1,0:T(8,128)(2,1)S(1)}, bf16[1536,128]{1,0:T(8,128)(2,1)S(1)}) custom-call(bf16[24,256,128]{2,1,0:T(8,128)(2,1)} %bitcast.1, f32[3,17]{1,0:T(4,128)} %taps_hbm.1), custom_call_target="tpu_custom_call" | custom-call | tf_op jit(solution)/shard_map/filter_sent/pallas_call | solution.py:399
  2.6 0.7 %collective-permute-start = (f32[9,8,128]{2,1,0:T(8,128)S(1)}, f32[9,8,128]{2,1,0:T(8,128)S(1)}, u32[]{:S(2)}, u32[]{:S(2)}) collective-permute-start(f32[9,8,128]{2,1,0:T(8,128)S(1)} %get-tuple-element.21), channel_id=1, source_target_pairs={{2,4},{6,8},{10,12},{4,2},{8,6},{12,10},{3,5},{7,9},{11,13},{5,3},... | collective-permute-start | bytes 110600 | tf_op jit(solution)/shard_map/ppermute | solution.py:374
  3.3 5.8 %collective-permute-start.1 = (f32[9,8,128]{2,1,0:T(8,128)S(1)}, f32[9,8,128]{2,1,0:T(8,128)S(1)}, u32[]{:S(2)}, u32[]{:S(2)}) collective-permute-start(f32[9,8,128]{2,1,0:T(8,128)S(1)} %get-tuple-element.22), channel_id=1, source_target_pairs={{0,2},{4,6},{8,10},{12,14},{2,0},{6,4},{10,8},{14,12},{1,3},{5,7},... | collective-permute-start | bytes 110600 | tf_op jit(solution)/shard_map/ppermute | solution.py:374
  9.1 1.5 %filter_own.1 = (f32[18,8,128]{2,1,0:T(8,128)S(1)}, f32[136,128]{1,0:T(8,128)S(1)}, f32[136,128]{1,0:T(8,128)S(1)}, bf16[248,1536]{1,0:T(8,128)(2,1)S(1)}) custom-call(bf16[248,1536]{1,0:T(8,128)(2,1)} %stored_hbm.1, bf16[24,256,128]{2,1,0:T(8,128)(2,1)S(1)} %get-tuple-element.16.fine_ref, bf16[64,256]{1,0:T(8,128)(2,1)S(1)} %get-tuple-element.17.matrix_ref, ...), custom_call_target="tpu_custom_call" | custom-call | tf_op jit(solution)/shard_map/filter_own/pallas_call | solution.py:411
  10.6 0.0 collective-permute-done.far_ref
  10.6 0.1 join_far.1.own_ref
  10.7 0.3 collective-permute-done.1.near_ref
  11.0 0.1 join_near.1
  11.1 0.1 collective-permute-start.2
  11.2 1.3 %collective-permute-done.2.partner_ref = f32[184,128]{1,0:T(8,128)S(1)} collective-permute-done((f32[184,128]{1,0:T(8,128)S(1)}, f32[184,128]{1,0:T(8,128)S(1)}, u32[]{:S(2)}, u32[]{:S(2)}) %collective-permute-start.2) | collective-permute-done | bytes 94240 | tf_op jit(solution)/shard_map/ppermute | solution.py:368
  12.4 0.3 gram_new.1
  12.7 2.0 %collective-permute-start.3 = (f32[152,128]{1,0:T(8,128)S(1)}, f32[152,128]{1,0:T(8,128)S(1)}, u32[]{:S(2)}, u32[]{:S(2)}) collective-permute-start(f32[152,128]{1,0:T(8,128)S(1)} %get-tuple-element.27), channel_id=1, source_target_pairs={{0,2},{2,0},{4,6},{6,4},{8,10},{10,8},{12,14},{14,12},{1,3},{3,1},... | collective-permute-start | bytes 233480 | tf_op jit(solution)/shard_map/ppermute | solution.py:368
  14.8 2.7 %collective-permute-done.3 = f32[152,128]{1,0:T(8,128)S(1)} collective-permute-done((f32[152,128]{1,0:T(8,128)S(1)}, f32[152,128]{1,0:T(8,128)S(1)}, u32[]{:S(2)}, u32[]{:S(2)}) %collective-permute-start.3) | collective-permute-done | bytes 77856 | tf_op jit(solution)/shard_map/ppermute | solution.py:368
  17.5 1.7 %collective-permute-start.4 = (f32[152,128]{1,0:T(8,128)S(1)}, f32[152,128]{1,0:T(8,128)S(1)}, u32[]{:S(2)}, u32[]{:S(2)}) collective-permute-start(f32[152,128]{1,0:T(8,128)S(1)} %add.9), channel_id=1, source_target_pairs={{0,4},{2,6},{4,0},{6,2},{8,12},{10,14},{12,8},{14,10},{1,5},{3,7},... | collective-permute-start | bytes 233480 | tf_op jit(solution)/shard_map/ppermute | solution.py:368
  19.2 2.7 %collective-permute-done.4 = f32[152,128]{1,0:T(8,128)S(1)} collective-permute-done((f32[152,128]{1,0:T(8,128)S(1)}, f32[152,128]{1,0:T(8,128)S(1)}, u32[]{:S(2)}, u32[]{:S(2)}) %collective-permute-start.4) | collective-permute-done | bytes 77856 | tf_op jit(solution)/shard_map/ppermute | solution.py:368
  22.0 2.7 %collective-permute-start.5 = (f32[152,128]{1,0:T(8,128)S(1)}, f32[152,128]{1,0:T(8,128)S(1)}, u32[]{:S(2)}, u32[]{:S(2)}) collective-permute-start(f32[152,128]{1,0:T(8,128)S(1)} %add.10), channel_id=1, source_target_pairs={{0,8},{2,10},{4,12},{6,14},{8,0},{10,2},{12,4},{14,6},{1,9},{3,11}... | collective-permute-start | bytes 233480 | tf_op jit(solution)/shard_map/ppermute | solution.py:368
  24.7 2.6 %collective-permute-done.5 = f32[152,128]{1,0:T(8,128)S(1)} collective-permute-done((f32[152,128]{1,0:T(8,128)S(1)}, f32[152,128]{1,0:T(8,128)S(1)}, u32[]{:S(2)}, u32[]{:S(2)}) %collective-permute-start.5) | collective-permute-done | bytes 77856 | tf_op jit(solution)/shard_map/ppermute | solution.py:368
  27.3 0.1 collective-permute-start.6
  27.4 1.3 %collective-permute-done.6.other_ref = f32[152,128]{1,0:T(8,128)S(1)} collective-permute-done((f32[152,128]{1,0:T(8,128)S(1)}, f32[152,128]{1,0:T(8,128)S(1)}, u32[]{:S(2)}, u32[]{:S(2)}) %collective-permute-start.6) | collective-permute-done | bytes 77856 | tf_op jit(solution)/shard_map/ppermute | solution.py:368
  28.7 7.1 %factor.1 = (bf16[8,1536]{1,0:T(8,128)(2,1)}, f32[256,256]{1,0:T(8,128)}, f32[256,1536]{1,0:T(8,128)}) custom-call(f32[152,128]{1,0:T(8,128)S(1)} %add.11.mine_ref, f32[152,128]{1,0:T(8,128)S(1)} %collective-permute-done.6.other_ref, bf16[248,1536]{1,0:T(8,128)(2,1)S(1)} %get-tuple-element.19.stored_ref, bf16[8,1536]{1,0:T(8,128)(2,1)S(1)} %get-tuple-element.28.coarse_ref), custom_call_target="tpu_custom_call" | custom-call | tf_op jit(solution)/shard_map/factor/pallas_call | solution.py:340
  (3 shorter events, 0.0 us)
Async XLA Ops:
  2.6 8.0 %collective-permute-start = (f32[9,8,128]{2,1,0:T(8,128)S(1)}, f32[9,8,128]{2,1,0:T(8,128)S(1)}, u32[]{:S(2)}, u32[]{:S(2)}) collective-permute-start(f32[9,8,128]{2,1,0:T(8,128)S(1)} %get-tuple-element.21), channel_id=1, source_target_pairs={{2,4},{6,8},{10,12},{4,2},{8,6},{12,10},{3,5},{7,9},{11,13},{5,3},... | collective-permute-start | bytes 110600 | tf_op jit(solution)/shard_map/ppermute | solution.py:374
  3.3 7.7 %collective-permute-start.1 = (f32[9,8,128]{2,1,0:T(8,128)S(1)}, f32[9,8,128]{2,1,0:T(8,128)S(1)}, u32[]{:S(2)}, u32[]{:S(2)}) collective-permute-start(f32[9,8,128]{2,1,0:T(8,128)S(1)} %get-tuple-element.22), channel_id=1, source_target_pairs={{0,2},{4,6},{8,10},{12,14},{2,0},{6,4},{10,8},{14,12},{1,3},{5,7},... | collective-permute-start | bytes 110600 | tf_op jit(solution)/shard_map/ppermute | solution.py:374
  11.1 1.4 %collective-permute-start.2 = (f32[184,128]{1,0:T(8,128)S(1)}, f32[184,128]{1,0:T(8,128)S(1)}, u32[]{:S(2)}, u32[]{:S(2)}) collective-permute-start(f32[184,128]{1,0:T(8,128)S(1)} %get-tuple-element.25), channel_id=1, source_target_pairs={{0,1},{1,0},{2,3},{3,2},{4,5},{5,4},{6,7},{7,6},{8,9},{9,8},{10,11... | collective-permute-start | bytes 282632 | tf_op jit(solution)/shard_map/ppermute | solution.py:368
  12.7 4.7 %collective-permute-start.3 = (f32[152,128]{1,0:T(8,128)S(1)}, f32[152,128]{1,0:T(8,128)S(1)}, u32[]{:S(2)}, u32[]{:S(2)}) collective-permute-start(f32[152,128]{1,0:T(8,128)S(1)} %get-tuple-element.27), channel_id=1, source_target_pairs={{0,2},{2,0},{4,6},{6,4},{8,10},{10,8},{12,14},{14,12},{1,3},{3,1},... | collective-permute-start | bytes 233480 | tf_op jit(solution)/shard_map/ppermute | solution.py:368
  17.5 4.5 %collective-permute-start.4 = (f32[152,128]{1,0:T(8,128)S(1)}, f32[152,128]{1,0:T(8,128)S(1)}, u32[]{:S(2)}, u32[]{:S(2)}) collective-permute-start(f32[152,128]{1,0:T(8,128)S(1)} %add.9), channel_id=1, source_target_pairs={{0,4},{2,6},{4,0},{6,2},{8,12},{10,14},{12,8},{14,10},{1,5},{3,7},... | collective-permute-start | bytes 233480 | tf_op jit(solution)/shard_map/ppermute | solution.py:368
  22.0 5.4 %collective-permute-start.5 = (f32[152,128]{1,0:T(8,128)S(1)}, f32[152,128]{1,0:T(8,128)S(1)}, u32[]{:S(2)}, u32[]{:S(2)}) collective-permute-start(f32[152,128]{1,0:T(8,128)S(1)} %add.10), channel_id=1, source_target_pairs={{0,8},{2,10},{4,12},{6,14},{8,0},{10,2},{12,4},{14,6},{1,9},{3,11}... | collective-permute-start | bytes 233480 | tf_op jit(solution)/shard_map/ppermute | solution.py:368
  27.3 1.3 %collective-permute-start.6 = (f32[152,128]{1,0:T(8,128)S(1)}, f32[152,128]{1,0:T(8,128)S(1)}, u32[]{:S(2)}, u32[]{:S(2)}) collective-permute-start(f32[152,128]{1,0:T(8,128)S(1)} %add.11.mine_ref), channel_id=1, source_target_pairs={{0,1},{1,0},{2,3},{3,2},{4,5},{5,4},{6,7},{7,6},{8,9},{9,8},{10,11... | collective-permute-start | bytes 233480 | tf_op jit(solution)/shard_map/ppermute | solution.py:368

commit v8 on v7

--- a/solution.py
+++ b/solution.py
@@ -380,8 +380,12 @@
         return lax.psum(values, "span")
     bit = 1
     while bit < count:
-        values = values + swap(values, "span", bit)
-        bit *= 2
+        if 2 * bit < count:
+            first, second, third = (swap(values, "span", step * bit) for step in (1, 2, 3))
+            values = (values + first) + (second + third)
+        else:
+            values = values + swap(values, "span", bit)
+        bit *= 4
     return values
 
 

time: 35.9 us -> 34.7 us (0.967)
  waiting for transfers between devices: 10.9 us -> 9.89 us
    ppermute x5 -> x6, waiting for transfers between devices: 10.6 us -> 9.6 us  [swap(): return lax.ppermute(values, axis, [(i, i ^ bit) for i in range(count)])]
    ppermute x5 -> x6, starting transfers between devices: 6.63 us -> 6.44 us  [swap(): return lax.ppermute(values, axis, [(i, i ^ bit) for i in range(count)])]
  transfers between devices with their start and end apart: 7 -> 8, of which waited for: 6 -> 7; matrix products, arithmetic and copies ran while one was open for 0% -> 0% of each run, Pallas kernels for 5% -> 5%
where the time goes in v8:
time: 34.7 us; the launch traced here: 34.6 us
  starting transfers between devices  12.9 us (37%)
  Pallas kernels  11 us (32%)
  waiting for transfers between devices  9.89 us (29%)
  between operations  0.69 us (2%)
    ppermute x6, waiting for transfers between devices, swap(): return lax.ppermute(values, axis, [(i, i ^ bit) for i in range(count)])  9.6 us
    pallas_call x1, Pallas kernels, factorise(): pl.pallas_call(factor_kernel, out_shape=[shaped(coarse.shape, BF16), shap...  7.06 us
    ppermute x2, starting transfers between devices, swap_pairs(): return lax.ppermute(values, axis, pairs + [(j, i) for i, j in pairs])  6.46 us
    ppermute x6, starting transfers between devices, swap(): return lax.ppermute(values, axis, [(i, i ^ bit) for i in range(count)])  6.44 us
    pallas_call x1, Pallas kernels, local(): pl.pallas_call(sent_kernel, out_shape=[pltpu.VMEM((9, snapshots, LANES),...  1.96 us
    pallas_call x1, Pallas kernels, local(): pl.pallas_call(functools.partial(own_kernel, total), out_shape=[shaped((1...  1.55 us
  transfers between devices with their start and end apart: 8, of which 7 were waited for; matrix products, arithmetic and copies ran while one was open for 0% of the time, Pallas kernels for 5%

profile of v8, /device:TPU:0, one launch (start us, length us, event | category | flops | bytes accessed | tf_op | source)
XLA Modules:
  0.0 34.6 jit_solution(13806941169035440226)
XLA Ops:
  0.6 2.0 %filter_sent.1 = (f32[9,8,128]{2,1,0:T(8,128)S(1)}, f32[9,8,128]{2,1,0:T(8,128)S(1)}, bf16[24,256,128]{2,1,0:T(8,128)(2,1)S(1)}, bf16[64,256]{1,0:T(8,128)(2,1)S(1)}, bf16[1536,128]{1,0:T(8,128)(2,1)S(1)}) custom-call(bf16[24,256,128]{2,1,0:T(8,128)(2,1)} %bitcast.1, f32[3,17]{1,0:T(4,128)} %taps_hbm.1), custom_call_target="tpu_custom_call" | custom-call | tf_op jit(solution)/shard_map/filter_sent/pallas_call | solution.py:403
  2.6 0.7 %collective-permute-start = (f32[9,8,128]{2,1,0:T(8,128)S(1)}, f32[9,8,128]{2,1,0:T(8,128)S(1)}, u32[]{:S(2)}, u32[]{:S(2)}) collective-permute-start(f32[9,8,128]{2,1,0:T(8,128)S(1)} %get-tuple-element.21), channel_id=1, source_target_pairs={{2,4},{6,8},{10,12},{4,2},{8,6},{12,10},{3,5},{7,9},{11,13},{5,3},... | collective-permute-start | bytes 110600 | tf_op jit(solution)/shard_map/ppermute | solution.py:374
  3.3 5.8 %collective-permute-start.1 = (f32[9,8,128]{2,1,0:T(8,128)S(1)}, f32[9,8,128]{2,1,0:T(8,128)S(1)}, u32[]{:S(2)}, u32[]{:S(2)}) collective-permute-start(f32[9,8,128]{2,1,0:T(8,128)S(1)} %get-tuple-element.22), channel_id=1, source_target_pairs={{0,2},{4,6},{8,10},{12,14},{2,0},{6,4},{10,8},{14,12},{1,3},{5,7},... | collective-permute-start | bytes 110600 | tf_op jit(solution)/shard_map/ppermute | solution.py:374
  9.1 1.5 %filter_own.1 = (f32[18,8,128]{2,1,0:T(8,128)S(1)}, f32[136,128]{1,0:T(8,128)S(1)}, f32[136,128]{1,0:T(8,128)S(1)}, bf16[248,1536]{1,0:T(8,128)(2,1)S(1)}) custom-call(bf16[248,1536]{1,0:T(8,128)(2,1)} %stored_hbm.1, bf16[24,256,128]{2,1,0:T(8,128)(2,1)S(1)} %get-tuple-element.16.fine_ref, bf16[64,256]{1,0:T(8,128)(2,1)S(1)} %get-tuple-element.17.matrix_ref, ...), custom_call_target="tpu_custom_call" | custom-call | tf_op jit(solution)/shard_map/filter_own/pallas_call | solution.py:415
  10.6 0.0 collective-permute-done.far_ref
  10.6 0.1 join_far.1.own_ref
  10.7 0.3 collective-permute-done.1.near_ref
  11.0 0.1 join_near.1
  11.1 0.1 collective-permute-start.2
  11.2 1.3 %collective-permute-done.2.partner_ref = f32[184,128]{1,0:T(8,128)S(1)} collective-permute-done((f32[184,128]{1,0:T(8,128)S(1)}, f32[184,128]{1,0:T(8,128)S(1)}, u32[]{:S(2)}, u32[]{:S(2)}) %collective-permute-start.2) | collective-permute-done | bytes 94240 | tf_op jit(solution)/shard_map/ppermute | solution.py:368
  12.4 0.3 gram_new.1
  12.7 3.1 %collective-permute-start.5 = (f32[152,128]{1,0:T(8,128)S(1)}, f32[152,128]{1,0:T(8,128)S(1)}, u32[]{:S(2)}, u32[]{:S(2)}) collective-permute-start(f32[152,128]{1,0:T(8,128)S(1)} %get-tuple-element.27), channel_id=1, source_target_pairs={{0,6},{2,4},{4,2},{6,0},{8,14},{10,12},{12,10},{14,8},{1,7},{3,5},... | collective-permute-start | bytes 233480 | tf_op jit(solution)/shard_map/ppermute | solution.py:368
  15.8 0.4 %collective-permute-start.4 = (f32[152,128]{1,0:T(8,128)S(1)}, f32[152,128]{1,0:T(8,128)S(1)}, u32[]{:S(2)}, u32[]{:S(2)}) collective-permute-start(f32[152,128]{1,0:T(8,128)S(1)} %get-tuple-element.27), channel_id=1, source_target_pairs={{0,4},{2,6},{4,0},{6,2},{8,12},{10,14},{12,8},{14,10},{1,5},{3,7},... | collective-permute-start | bytes 233480 | tf_op jit(solution)/shard_map/ppermute | solution.py:368
  16.3 0.1 collective-permute-start.3
  16.4 2.5 %collective-permute-done.5 = f32[152,128]{1,0:T(8,128)S(1)} collective-permute-done((f32[152,128]{1,0:T(8,128)S(1)}, f32[152,128]{1,0:T(8,128)S(1)}, u32[]{:S(2)}, u32[]{:S(2)}) %collective-permute-start.5) | collective-permute-done | bytes 77856 | tf_op jit(solution)/shard_map/ppermute | solution.py:368
  18.9 1.4 %collective-permute-done.4 = f32[152,128]{1,0:T(8,128)S(1)} collective-permute-done((f32[152,128]{1,0:T(8,128)S(1)}, f32[152,128]{1,0:T(8,128)S(1)}, u32[]{:S(2)}, u32[]{:S(2)}) %collective-permute-start.4) | collective-permute-done | bytes 77856 | tf_op jit(solution)/shard_map/ppermute | solution.py:368
  20.3 0.3 collective-permute-done.3
  20.7 2.7 %collective-permute-start.6 = (f32[152,128]{1,0:T(8,128)S(1)}, f32[152,128]{1,0:T(8,128)S(1)}, u32[]{:S(2)}, u32[]{:S(2)}) collective-permute-start(f32[152,128]{1,0:T(8,128)S(1)} %add_add_fusion), channel_id=1, source_target_pairs={{0,8},{2,10},{4,12},{6,14},{8,0},{10,2},{12,4},{14,6},{1,9},{3,11}... | collective-permute-start | bytes 233480 | tf_op jit(solution)/shard_map/ppermute | solution.py:368
  23.3 2.8 %collective-permute-done.6 = f32[152,128]{1,0:T(8,128)S(1)} collective-permute-done((f32[152,128]{1,0:T(8,128)S(1)}, f32[152,128]{1,0:T(8,128)S(1)}, u32[]{:S(2)}, u32[]{:S(2)}) %collective-permute-start.6) | collective-permute-done | bytes 77856 | tf_op jit(solution)/shard_map/ppermute | solution.py:368
  26.2 0.1 collective-permute-start.7
  26.2 1.3 %collective-permute-done.7.other_ref = f32[152,128]{1,0:T(8,128)S(1)} collective-permute-done((f32[152,128]{1,0:T(8,128)S(1)}, f32[152,128]{1,0:T(8,128)S(1)}, u32[]{:S(2)}, u32[]{:S(2)}) %collective-permute-start.7) | collective-permute-done | bytes 77856 | tf_op jit(solution)/shard_map/ppermute | solution.py:368
  27.5 7.1 %factor.1 = (bf16[8,1536]{1,0:T(8,128)(2,1)}, f32[256,256]{1,0:T(8,128)}, f32[256,1536]{1,0:T(8,128)}) custom-call(f32[152,128]{1,0:T(8,128)S(1)} %add.15.mine_ref, f32[152,128]{1,0:T(8,128)S(1)} %collective-permute-done.7.other_ref, bf16[248,1536]{1,0:T(8,128)(2,1)S(1)} %get-tuple-element.19.stored_ref, bf16[8,1536]{1,0:T(8,128)(2,1)S(1)} %get-tuple-element.28.coarse_ref), custom_call_target="tpu_custom_call" | custom-call | tf_op jit(solution)/shard_map/factor/pallas_call | solution.py:340
  (2 shorter events, 0.0 us)
Async XLA Ops:
  2.6 8.0 %collective-permute-start = (f32[9,8,128]{2,1,0:T(8,128)S(1)}, f32[9,8,128]{2,1,0:T(8,128)S(1)}, u32[]{:S(2)}, u32[]{:S(2)}) collective-permute-start(f32[9,8,128]{2,1,0:T(8,128)S(1)} %get-tuple-element.21), channel_id=1, source_target_pairs={{2,4},{6,8},{10,12},{4,2},{8,6},{12,10},{3,5},{7,9},{11,13},{5,3},... | collective-permute-start | bytes 110600 | tf_op jit(solution)/shard_map/ppermute | solution.py:374
  3.3 7.7 %collective-permute-start.1 = (f32[9,8,128]{2,1,0:T(8,128)S(1)}, f32[9,8,128]{2,1,0:T(8,128)S(1)}, u32[]{:S(2)}, u32[]{:S(2)}) collective-permute-start(f32[9,8,128]{2,1,0:T(8,128)S(1)} %get-tuple-element.22), channel_id=1, source_target_pairs={{0,2},{4,6},{8,10},{12,14},{2,0},{6,4},{10,8},{14,12},{1,3},{5,7},... | collective-permute-start | bytes 110600 | tf_op jit(solution)/shard_map/ppermute | solution.py:374
  11.1 1.4 %collective-permute-start.2 = (f32[184,128]{1,0:T(8,128)S(1)}, f32[184,128]{1,0:T(8,128)S(1)}, u32[]{:S(2)}, u32[]{:S(2)}) collective-permute-start(f32[184,128]{1,0:T(8,128)S(1)} %get-tuple-element.25), channel_id=1, source_target_pairs={{0,1},{1,0},{2,3},{3,2},{4,5},{5,4},{6,7},{7,6},{8,9},{9,8},{10,11... | collective-permute-start | bytes 282632 | tf_op jit(solution)/shard_map/ppermute | solution.py:368
  12.7 6.2 %collective-permute-start.5 = (f32[152,128]{1,0:T(8,128)S(1)}, f32[152,128]{1,0:T(8,128)S(1)}, u32[]{:S(2)}, u32[]{:S(2)}) collective-permute-start(f32[152,128]{1,0:T(8,128)S(1)} %get-tuple-element.27), channel_id=1, source_target_pairs={{0,6},{2,4},{4,2},{6,0},{8,14},{10,12},{12,10},{14,8},{1,7},{3,5},... | collective-permute-start | bytes 233480 | tf_op jit(solution)/shard_map/ppermute | solution.py:368
  15.8 4.5 %collective-permute-start.4 = (f32[152,128]{1,0:T(8,128)S(1)}, f32[152,128]{1,0:T(8,128)S(1)}, u32[]{:S(2)}, u32[]{:S(2)}) collective-permute-start(f32[152,128]{1,0:T(8,128)S(1)} %get-tuple-element.27), channel_id=1, source_target_pairs={{0,4},{2,6},{4,0},{6,2},{8,12},{10,14},{12,8},{14,10},{1,5},{3,7},... | collective-permute-start | bytes 233480 | tf_op jit(solution)/shard_map/ppermute | solution.py:368
  16.3 4.4 %collective-permute-start.3 = (f32[152,128]{1,0:T(8,128)S(1)}, f32[152,128]{1,0:T(8,128)S(1)}, u32[]{:S(2)}, u32[]{:S(2)}) collective-permute-start(f32[152,128]{1,0:T(8,128)S(1)} %get-tuple-element.27), channel_id=1, source_target_pairs={{0,2},{2,0},{4,6},{6,4},{8,10},{10,8},{12,14},{14,12},{1,3},{3,1},... | collective-permute-start | bytes 233480 | tf_op jit(solution)/shard_map/ppermute | solution.py:368
  20.7 5.5 %collective-permute-start.6 = (f32[152,128]{1,0:T(8,128)S(1)}, f32[152,128]{1,0:T(8,128)S(1)}, u32[]{:S(2)}, u32[]{:S(2)}) collective-permute-start(f32[152,128]{1,0:T(8,128)S(1)} %add_add_fusion), channel_id=1, source_target_pairs={{0,8},{2,10},{4,12},{6,14},{8,0},{10,2},{12,4},{14,6},{1,9},{3,11}... | collective-permute-start | bytes 233480 | tf_op jit(solution)/shard_map/ppermute | solution.py:368
  26.2 1.3 %collective-permute-start.7 = (f32[152,128]{1,0:T(8,128)S(1)}, f32[152,128]{1,0:T(8,128)S(1)}, u32[]{:S(2)}, u32[]{:S(2)}) collective-permute-start(f32[152,128]{1,0:T(8,128)S(1)} %add.15.mine_ref), channel_id=1, source_target_pairs={{0,1},{1,0},{2,3},{3,2},{4,5},{5,4},{6,7},{7,6},{8,9},{9,8},{10,11... | collective-permute-start | bytes 233480 | tf_op jit(solution)/shard_map/ppermute | solution.py:368

commit v9 on v8

--- a/solution.py
+++ b/solution.py
@@ -16,7 +16,7 @@
 FAR = 8
 PARTS = 2
 OUTSIDE = -64
-HALF = LANES + 8
+HALF = LANES
 
 
 def iota(shape, dim):
@@ -129,13 +129,15 @@
 def fold(gram, kept_ref, sent_ref, first):
     row, col = iota((LANES, LANES), 0), iota((LANES, LANES), 1)
     across, lower = gram[LANES:, :LANES], gram[LANES:, LANES:]
+    corner = jnp.sum(jnp.where(row == col, lower, 0.0), axis=0, keepdims=True)
     packed = jnp.where(row <= col, gram[:LANES, :LANES], lower)
-    corner = jnp.sum(jnp.where(row == col, lower, 0.0), axis=0, keepdims=True)
-    corner = jnp.broadcast_to(corner, (8, LANES))
-    kept_ref[:LANES] = jnp.where(first, packed, across)
-    kept_ref[LANES:] = corner
-    sent_ref[:LANES] = jnp.where(first, across, packed)
-    sent_ref[LANES:] = corner
+    packed = jnp.where(in_corner(row, col), jnp.broadcast_to(corner, (LANES, LANES)), packed)
+    kept_ref[...] = jnp.where(first, packed, across)
+    sent_ref[...] = jnp.where(first, across, packed)
+
+
+def in_corner(row, col):
+    return (row == LANES - 1) & (col < LANES - 8)
 
 
 def own_kernel(
@@ -255,7 +257,8 @@
     row, col = iota((LANES, LANES), 0), iota((LANES, LANES), 1)
     packed = jnp.where(first, mine_ref[:LANES], other_ref[:LANES])
     across = jnp.where(first, other_ref[:LANES], mine_ref[:LANES])
-    corner = jnp.where(first, mine_ref[LANES : LANES + 1], other_ref[LANES : LANES + 1])
+    corner = jnp.where(col[:1] < LANES - 8, packed[LANES - 1 :], 0.0)
+    packed = jnp.where(in_corner(row, col), 0.0, packed)
     added = mine_ref[HALF : HALF + 8] + other_ref[HALF : HALF + 8]
     across = jnp.concatenate([across[:-8], across[-8:] + added], axis=0)
     added = mine_ref[HALF + 8 :] + other_ref[HALF + 8 :]
@@ -317,11 +320,10 @@
                 inverse_ref[end + PANEL :, :reach] = inverse_ref[end + PANEL :, :reach] - far[:, size - lost :]
         inverse = panel[:, size - skip :]
         inverse = jnp.where(iota(inverse.shape, 0) + begin >= iota(inverse.shape, 1), inverse, 0.0)
-        high, low = split2(inverse)
-        cells = window_ref[:reach, :]
-        basis_ref[begin:end, :] = jnp.dot(
-            jnp.concatenate([high, low], axis=1), jnp.concatenate([cells, cells], axis=0), preferred_element_type=F32
+        both = jnp.dot(
+            jnp.concatenate(split2(inverse), axis=0), window_ref[:reach, :], preferred_element_type=F32
         )
+        basis_ref[begin:end, :] = both[:PANEL] + both[PANEL:]
         send(basis_ref, basis_hbm, begin, end)
         if end == LANES:
             factor_ref[:LANES, :LANES] = jnp.where(row >= col, upper_ref[:LANES, :LANES].T, 0.0)

time: 34.7 us -> 34.4 us (level)
  no operation moved by 1% of the time
where the time goes in v9:
time: 34.4 us; the launch traced here: 34.2 us
  starting transfers between devices  12.9 us (38%)
  Pallas kernels  10.8 us (31%)
  waiting for transfers between devices  9.69 us (28%)
  between operations  0.69 us (2%)
    ppermute x6, waiting for transfers between devices, swap(): return lax.ppermute(values, axis, [(i, i ^ bit) for i in range(count)])  9.4 us
    pallas_call x1, Pallas kernels, factorise(): pl.pallas_call(factor_kernel, out_shape=[shaped(coarse.shape, BF16), shap...  6.87 us
    ppermute x2, starting transfers between devices, swap_pairs(): return lax.ppermute(values, axis, pairs + [(j, i) for i, j in pairs])  6.46 us
    ppermute x6, starting transfers between devices, swap(): return lax.ppermute(values, axis, [(i, i ^ bit) for i in range(count)])  6.44 us
    pallas_call x1, Pallas kernels, local(): pl.pallas_call(sent_kernel, out_shape=[pltpu.VMEM((9, snapshots, LANES),...  1.96 us
    pallas_call x1, Pallas kernels, local(): pl.pallas_call(functools.partial(own_kernel, total), out_shape=[shaped((1...  1.55 us
  transfers between devices with their start and end apart: 8, of which 7 were waited for; matrix products, arithmetic and copies ran while one was open for 0% of the time, Pallas kernels for 5%

profile of v9, /device:TPU:0, one launch (start us, length us, event | category | flops | bytes accessed | tf_op | source)
XLA Modules:
  0.0 34.2 jit_solution(5575270863050092691)
XLA Ops:
  0.6 2.0 %filter_sent.1 = (f32[9,8,128]{2,1,0:T(8,128)S(1)}, f32[9,8,128]{2,1,0:T(8,128)S(1)}, bf16[24,256,128]{2,1,0:T(8,128)(2,1)S(1)}, bf16[64,256]{1,0:T(8,128)(2,1)S(1)}, bf16[1536,128]{1,0:T(8,128)(2,1)S(1)}) custom-call(bf16[24,256,128]{2,1,0:T(8,128)(2,1)} %bitcast.1, f32[3,17]{1,0:T(4,128)} %taps_hbm.1), custom_call_target="tpu_custom_call" | custom-call | tf_op jit(solution)/shard_map/filter_sent/pallas_call | solution.py:405
  2.6 0.7 %collective-permute-start = (f32[9,8,128]{2,1,0:T(8,128)S(1)}, f32[9,8,128]{2,1,0:T(8,128)S(1)}, u32[]{:S(2)}, u32[]{:S(2)}) collective-permute-start(f32[9,8,128]{2,1,0:T(8,128)S(1)} %get-tuple-element.21), channel_id=1, source_target_pairs={{2,4},{6,8},{10,12},{4,2},{8,6},{12,10},{3,5},{7,9},{11,13},{5,3},... | collective-permute-start | bytes 110600 | tf_op jit(solution)/shard_map/ppermute | solution.py:376
  3.3 5.8 %collective-permute-start.1 = (f32[9,8,128]{2,1,0:T(8,128)S(1)}, f32[9,8,128]{2,1,0:T(8,128)S(1)}, u32[]{:S(2)}, u32[]{:S(2)}) collective-permute-start(f32[9,8,128]{2,1,0:T(8,128)S(1)} %get-tuple-element.22), channel_id=1, source_target_pairs={{0,2},{4,6},{8,10},{12,14},{2,0},{6,4},{10,8},{14,12},{1,3},{5,7},... | collective-permute-start | bytes 110600 | tf_op jit(solution)/shard_map/ppermute | solution.py:376
  9.1 1.5 %filter_own.1 = (f32[18,8,128]{2,1,0:T(8,128)S(1)}, f32[128,128]{1,0:T(8,128)S(1)}, f32[128,128]{1,0:T(8,128)S(1)}, bf16[248,1536]{1,0:T(8,128)(2,1)S(1)}) custom-call(bf16[248,1536]{1,0:T(8,128)(2,1)} %stored_hbm.1, bf16[24,256,128]{2,1,0:T(8,128)(2,1)S(1)} %get-tuple-element.16.fine_ref, bf16[64,256]{1,0:T(8,128)(2,1)S(1)} %get-tuple-element.17.matrix_ref, ...), custom_call_target="tpu_custom_call" | custom-call | tf_op jit(solution)/shard_map/filter_own/pallas_call | solution.py:417
  10.6 0.0 collective-permute-done.far_ref
  10.6 0.1 join_far.1.own_ref
  10.7 0.3 collective-permute-done.1.near_ref
  11.0 0.1 join_near.1
  11.1 0.1 collective-permute-start.2
  11.2 1.3 %collective-permute-done.2.partner_ref = f32[176,128]{1,0:T(8,128)S(1)} collective-permute-done((f32[176,128]{1,0:T(8,128)S(1)}, f32[176,128]{1,0:T(8,128)S(1)}, u32[]{:S(2)}, u32[]{:S(2)}) %collective-permute-start.2) | collective-permute-done | bytes 90144 | tf_op jit(solution)/shard_map/ppermute | solution.py:370
  12.4 0.3 gram_new.1
  12.7 3.1 %collective-permute-start.5 = (f32[144,128]{1,0:T(8,128)S(1)}, f32[144,128]{1,0:T(8,128)S(1)}, u32[]{:S(2)}, u32[]{:S(2)}) collective-permute-start(f32[144,128]{1,0:T(8,128)S(1)} %get-tuple-element.27), channel_id=1, source_target_pairs={{0,6},{2,4},{4,2},{6,0},{8,14},{10,12},{12,10},{14,8},{1,7},{3,5},... | collective-permute-start | bytes 221192 | tf_op jit(solution)/shard_map/ppermute | solution.py:370
  15.8 0.4 %collective-permute-start.4 = (f32[144,128]{1,0:T(8,128)S(1)}, f32[144,128]{1,0:T(8,128)S(1)}, u32[]{:S(2)}, u32[]{:S(2)}) collective-permute-start(f32[144,128]{1,0:T(8,128)S(1)} %get-tuple-element.27), channel_id=1, source_target_pairs={{0,4},{2,6},{4,0},{6,2},{8,12},{10,14},{12,8},{14,10},{1,5},{3,7},... | collective-permute-start | bytes 221192 | tf_op jit(solution)/shard_map/ppermute | solution.py:370
  16.2 0.1 collective-permute-start.3
  16.4 2.4 %collective-permute-done.5 = f32[144,128]{1,0:T(8,128)S(1)} collective-permute-done((f32[144,128]{1,0:T(8,128)S(1)}, f32[144,128]{1,0:T(8,128)S(1)}, u32[]{:S(2)}, u32[]{:S(2)}) %collective-permute-start.5) | collective-permute-done | bytes 73760 | tf_op jit(solution)/shard_map/ppermute | solution.py:370
  18.7 1.4 %collective-permute-done.4 = f32[144,128]{1,0:T(8,128)S(1)} collective-permute-done((f32[144,128]{1,0:T(8,128)S(1)}, f32[144,128]{1,0:T(8,128)S(1)}, u32[]{:S(2)}, u32[]{:S(2)}) %collective-permute-start.4) | collective-permute-done | bytes 73760 | tf_op jit(solution)/shard_map/ppermute | solution.py:370
  20.2 0.4 %collective-permute-done.3 = f32[144,128]{1,0:T(8,128)S(1)} collective-permute-done((f32[144,128]{1,0:T(8,128)S(1)}, f32[144,128]{1,0:T(8,128)S(1)}, u32[]{:S(2)}, u32[]{:S(2)}) %collective-permute-start.3) | collective-permute-done | bytes 73760 | tf_op jit(solution)/shard_map/ppermute | solution.py:370
  20.6 2.7 %collective-permute-start.6 = (f32[144,128]{1,0:T(8,128)S(1)}, f32[144,128]{1,0:T(8,128)S(1)}, u32[]{:S(2)}, u32[]{:S(2)}) collective-permute-start(f32[144,128]{1,0:T(8,128)S(1)} %add_add_fusion), channel_id=1, source_target_pairs={{0,8},{2,10},{4,12},{6,14},{8,0},{10,2},{12,4},{14,6},{1,9},{3,11}... | collective-permute-start | bytes 221192 | tf_op jit(solution)/shard_map/ppermute | solution.py:370
  23.3 2.7 %collective-permute-done.6 = f32[144,128]{1,0:T(8,128)S(1)} collective-permute-done((f32[144,128]{1,0:T(8,128)S(1)}, f32[144,128]{1,0:T(8,128)S(1)}, u32[]{:S(2)}, u32[]{:S(2)}) %collective-permute-start.6) | collective-permute-done | bytes 73760 | tf_op jit(solution)/shard_map/ppermute | solution.py:370
  26.0 0.1 collective-permute-start.7
  26.0 1.3 %collective-permute-done.7.other_ref = f32[144,128]{1,0:T(8,128)S(1)} collective-permute-done((f32[144,128]{1,0:T(8,128)S(1)}, f32[144,128]{1,0:T(8,128)S(1)}, u32[]{:S(2)}, u32[]{:S(2)}) %collective-permute-start.7) | collective-permute-done | bytes 73760 | tf_op jit(solution)/shard_map/ppermute | solution.py:370
  27.3 6.9 %factor.1 = (bf16[8,1536]{1,0:T(8,128)(2,1)}, f32[256,256]{1,0:T(8,128)}, f32[256,1536]{1,0:T(8,128)}) custom-call(f32[144,128]{1,0:T(8,128)S(1)} %add.15.mine_ref, f32[144,128]{1,0:T(8,128)S(1)} %collective-permute-done.7.other_ref, bf16[248,1536]{1,0:T(8,128)(2,1)S(1)} %get-tuple-element.19.stored_ref, bf16[8,1536]{1,0:T(8,128)(2,1)S(1)} %get-tuple-element.28.coarse_ref), custom_call_target="tpu_custom_call" | custom-call | tf_op jit(solution)/shard_map/factor/pallas_call | solution.py:342
  (2 shorter events, 0.0 us)
Async XLA Ops:
  2.6 8.0 %collective-permute-start = (f32[9,8,128]{2,1,0:T(8,128)S(1)}, f32[9,8,128]{2,1,0:T(8,128)S(1)}, u32[]{:S(2)}, u32[]{:S(2)}) collective-permute-start(f32[9,8,128]{2,1,0:T(8,128)S(1)} %get-tuple-element.21), channel_id=1, source_target_pairs={{2,4},{6,8},{10,12},{4,2},{8,6},{12,10},{3,5},{7,9},{11,13},{5,3},... | collective-permute-start | bytes 110600 | tf_op jit(solution)/shard_map/ppermute | solution.py:376
  3.3 7.7 %collective-permute-start.1 = (f32[9,8,128]{2,1,0:T(8,128)S(1)}, f32[9,8,128]{2,1,0:T(8,128)S(1)}, u32[]{:S(2)}, u32[]{:S(2)}) collective-permute-start(f32[9,8,128]{2,1,0:T(8,128)S(1)} %get-tuple-element.22), channel_id=1, source_target_pairs={{0,2},{4,6},{8,10},{12,14},{2,0},{6,4},{10,8},{14,12},{1,3},{5,7},... | collective-permute-start | bytes 110600 | tf_op jit(solution)/shard_map/ppermute | solution.py:376
  11.1 1.4 %collective-permute-start.2 = (f32[176,128]{1,0:T(8,128)S(1)}, f32[176,128]{1,0:T(8,128)S(1)}, u32[]{:S(2)}, u32[]{:S(2)}) collective-permute-start(f32[176,128]{1,0:T(8,128)S(1)} %get-tuple-element.25), channel_id=1, source_target_pairs={{0,1},{1,0},{2,3},{3,2},{4,5},{5,4},{6,7},{7,6},{8,9},{9,8},{10,11... | collective-permute-start | bytes 270344 | tf_op jit(solution)/shard_map/ppermute | solution.py:370
  12.7 6.0 %collective-permute-start.5 = (f32[144,128]{1,0:T(8,128)S(1)}, f32[144,128]{1,0:T(8,128)S(1)}, u32[]{:S(2)}, u32[]{:S(2)}) collective-permute-start(f32[144,128]{1,0:T(8,128)S(1)} %get-tuple-element.27), channel_id=1, source_target_pairs={{0,6},{2,4},{4,2},{6,0},{8,14},{10,12},{12,10},{14,8},{1,7},{3,5},... | collective-permute-start | bytes 221192 | tf_op jit(solution)/shard_map/ppermute | solution.py:370
  15.8 4.4 %collective-permute-start.4 = (f32[144,128]{1,0:T(8,128)S(1)}, f32[144,128]{1,0:T(8,128)S(1)}, u32[]{:S(2)}, u32[]{:S(2)}) collective-permute-start(f32[144,128]{1,0:T(8,128)S(1)} %get-tuple-element.27), channel_id=1, source_target_pairs={{0,4},{2,6},{4,0},{6,2},{8,12},{10,14},{12,8},{14,10},{1,5},{3,7},... | collective-permute-start | bytes 221192 | tf_op jit(solution)/shard_map/ppermute | solution.py:370
  16.2 4.4 %collective-permute-start.3 = (f32[144,128]{1,0:T(8,128)S(1)}, f32[144,128]{1,0:T(8,128)S(1)}, u32[]{:S(2)}, u32[]{:S(2)}) collective-permute-start(f32[144,128]{1,0:T(8,128)S(1)} %get-tuple-element.27), channel_id=1, source_target_pairs={{0,2},{2,0},{4,6},{6,4},{8,10},{10,8},{12,14},{14,12},{1,3},{3,1},... | collective-permute-start | bytes 221192 | tf_op jit(solution)/shard_map/ppermute | solution.py:370
  20.6 5.3 %collective-permute-start.6 = (f32[144,128]{1,0:T(8,128)S(1)}, f32[144,128]{1,0:T(8,128)S(1)}, u32[]{:S(2)}, u32[]{:S(2)}) collective-permute-start(f32[144,128]{1,0:T(8,128)S(1)} %add_add_fusion), channel_id=1, source_target_pairs={{0,8},{2,10},{4,12},{6,14},{8,0},{10,2},{12,4},{14,6},{1,9},{3,11}... | collective-permute-start | bytes 221192 | tf_op jit(solution)/shard_map/ppermute | solution.py:370
  26.0 1.3 %collective-permute-start.7 = (f32[144,128]{1,0:T(8,128)S(1)}, f32[144,128]{1,0:T(8,128)S(1)}, u32[]{:S(2)}, u32[]{:S(2)}) collective-permute-start(f32[144,128]{1,0:T(8,128)S(1)} %add.15.mine_ref), channel_id=1, source_target_pairs={{0,1},{1,0},{2,3},{3,2},{4,5},{5,4},{6,7},{7,6},{8,9},{9,8},{10,11... | collective-permute-start | bytes 221192 | tf_op jit(solution)/shard_map/ppermute | solution.py:370

commit v10 on v9

--- a/solution.py
+++ b/solution.py
@@ -12,8 +12,9 @@
 TAPS = 17
 LANES = 128
 PANEL = 64
-NEAR = 8
-FAR = 8
+NEAR = 16
+FAR = 16
+AHEAD = 3
 PARTS = 2
 OUTSIDE = -64
 HALF = LANES
@@ -103,9 +104,12 @@
 
 
 def sent_kernel(
-    fine_hbm, taps_hbm, near_ref, far_ref, fine_ref, own_matrix_ref, stream_ref, taps_ref, plane_ref, sems
+    fine_hbm, taps_hbm, stored_hbm, near_ref, far_ref, fine_ref, own_matrix_ref, stream_ref, stored_ref,
+    taps_ref, plane_ref, sems,
 ):
-    taps_copy, *copies = start_copies([(taps_hbm, taps_ref)] + cells_of(fine_hbm, fine_ref), sems)
+    taps_copy, *copies, stored_copy = start_copies(
+        [(taps_hbm, taps_ref)] + cells_of(fine_hbm, fine_ref) + [(stored_hbm, stored_ref)], sems
+    )
     even = lax.axis_index("span") % 2 == 0
     span_cells = [jnp.where(even, at, at - 6) for at in (4, 5)] + [jnp.where(even, at - 6, at) for at in (4, 5)]
     taps_copy.wait()
@@ -124,6 +128,7 @@
         result = filter_stream(plane_ref, tiles, matrix)
         for t in range(len(tiles)):
             out_ref[t] = result[8 * t : 8 * t + 8]
+    stored_copy.wait()
 
 
 def fold(gram, kept_ref, sent_ref, first):
@@ -140,16 +145,12 @@
     return (row == LANES - 1) & (col < LANES - 8)
 
 
-def own_kernel(
-    total, stored_hbm, fine_ref, matrix_ref, stream_ref, own_ref, kept_ref, sent_ref, stored_ref, plane_ref, sems
-):
-    (copy,) = start_copies([(stored_hbm, stored_ref)], sems)
+def own_kernel(total, stored_ref, fine_ref, matrix_ref, stream_ref, own_ref, kept_ref, sent_ref, plane_ref):
     filter_plane(matrix_ref[...], fine_ref, plane_ref)
     tiles = [(comp, [(s, k) for s in range(4)]) for comp in range(3) for k in range(6)]
     result = filter_stream(plane_ref, tiles, stream_ref[...])
     for t in range(len(tiles)):
         own_ref[t] = result[8 * t : 8 * t + 8]
-    copy.wait()
     old, cells = stored_ref.shape
     rows = jnp.concatenate([stored_ref[...], jnp.zeros((8, cells), BF16)], axis=0)
     gram = lax.dot_general(rows, rows, (((1,), (1,)), ((), ())), preferred_element_type=F32) / total
@@ -207,53 +208,58 @@
     sums_ref[half + 8 :] = gram[:, LANES:]
 
 
-def eliminate(groups, at, lane, none, scale_ref):
-    count = len(groups)
-    width = groups[at].shape[1]
-    wide = lambda column: jnp.concatenate([column] * (width // LANES), axis=1)
-    spread = lambda values, k: jnp.broadcast_to(values[k : k + 1, :], (8, values.shape[1]))
-    column = lambda g, j: jnp.broadcast_to(groups[g][:, lane + j : lane + j + 1], (8, LANES))
+def eliminate(active, lead, lane, parts, none, scale_ref):
+    spread = lambda values, k: jnp.broadcast_to(values[k : k + 1, :], (8, LANES))
+    column = lambda g, j: jnp.broadcast_to(active[g][lead][:, lane + j : lane + j + 1], (8, LANES))
     sub = iota((8, LANES), 0)
-    cols = {(j, g): column(g, j) for g in (at, at + 1) for j in range(8 * (g - at) + 8)}
-    for g in (at, at + 1):
+    cols = {(j, g): column(g, j) for g in (0, 1) for j in range(8 * g + 8)}
+    for g in (0, 1):
         cols[0, g] = cols[0, g] + none
     for k in range(16):
-        home, k_sub = at + k // 8, k % 8
-        for g in range(at + 2, count):
-            step = NEAR if g < at + 4 else FAR
+        home, k_sub = k // 8, k % 8
+        for g in range(2, len(active)):
+            step = NEAR if g < 4 else FAR
             if k % step == 0:
                 for j in range(k, k + step):
                     cols[j, g] = column(g, j)
         scale = lax.rsqrt(spread(cols[k, home], k_sub))
         square = scale * scale
-        scale_ref[8 * home + k_sub : 8 * home + k_sub + 1, :] = scale[k_sub : k_sub + 1, :]
-        share = {g: cols[k, g] * square for g in range(home, count)}
+        scale_ref[k : k + 1, :] = scale[k_sub : k_sub + 1, :]
+        share = {g: cols[k, g] * square for g in range(home, len(active))}
         share[home] = jnp.where(sub > k_sub, share[home], 0.0)
         for j in range(k + 1, 16):
-            j_home, j_sub = at + j // 8, j % 8
+            j_home, j_sub = j // 8, j % 8
             head = spread(cols[k, j_home], j_sub)
-            for g in range(j_home, count):
-                step = 16 if g < at + 2 else NEAR if g < at + 4 else FAR
+            for g in range(j_home, len(active)):
+                step = 16 if g < 2 else NEAR if g < 4 else FAR
                 if j // step == k // step:
                     if j == k + 1 and g == j_home:
                         cols[j, g] = cols[j, g] - (cols[k, g] * head) * square
                     else:
                         cols[j, g] = cols[j, g] - share[g] * head
-        row = spread(groups[home], k_sub)
-        for g in range(home, count):
-            groups[g] = groups[g] - wide(share[g]) * row
-    for g in (at, at + 1):
-        groups[g] = groups[g] * wide(scale_ref[8 * g : 8 * g + 8, :])
-    return groups
+        for v in parts:
+            row = spread(active[home][v], k_sub)
+            for g in range(home, len(active) if v < 2 else min(len(active), 4)):
+                active[g][v] = active[g][v] - share[g] * row
+    for g in (0, 1):
+        for v in parts:
+            active[g][v] = active[g][v] * scale_ref[8 * g : 8 * g + 8, :]
 
 
 def factor_kernel(
     mine_ref, other_ref, stored_ref, coarse_ref, new_hbm, factor_hbm, basis_hbm,
-    left_ref, inverse_ref, upper_ref, factor_ref, basis_ref, scale_ref, window_ref, sems,
+    work_ref, upper_ref, inverse_ref, factor_ref, basis_ref, scale_ref, window_ref, sems,
 ):
     first = lax.axis_index("sect") == 0
     none = jnp.full((8, LANES), jnp.minimum(lax.axis_index("sect"), 0).astype(F32))
-    size = left_ref.shape[0]
+    size = work_ref.shape[0]
+    copies = []
+
+    def send(source, target):
+        copies.append(pltpu.make_async_copy(source, target, sems.at[len(copies)]))
+        copies[-1].start()
+
+    send(coarse_ref, new_hbm)
     row, col = iota((LANES, LANES), 0), iota((LANES, LANES), 1)
     packed = jnp.where(first, mine_ref[:LANES], other_ref[:LANES])
     across = jnp.where(first, other_ref[:LANES], mine_ref[:LANES])
@@ -266,72 +272,67 @@
     corner = corner + jnp.sum(jnp.where(row == col, added, 0.0), axis=0, keepdims=True)
     packed = packed + jnp.where(row > col, added, 0.0)
     turned = packed.T
-    copies = [pltpu.make_async_copy(coarse_ref, new_hbm, sems.at[0])]
-    copies[0].start()
+    work_ref[:LANES, :LANES] = jnp.where(row <= col, packed, turned)
+    work_ref[:LANES, LANES:size] = across.T
+    work_ref[LANES:, :LANES] = across
+    work_ref[LANES:, LANES:size] = jnp.where(
+        row == col, jnp.broadcast_to(corner, (LANES, LANES)), jnp.where(row < col, turned, packed)
+    )
+    work_ref[:, size:] = jnp.where(iota((size, size), 0) == iota((size, size), 1), 1.0, 0.0)
     window_ref[: size - 8, :] = stored_ref[...]
     window_ref[size - 8 :, :] = coarse_ref[...]
-    left_ref[:LANES, :LANES] = jnp.where(row <= col, packed, turned)
-    left_ref[:LANES, LANES:] = across.T
-    left_ref[LANES:, :LANES] = jnp.zeros((LANES, LANES), F32)
-    left_ref[LANES:, LANES:] = jnp.where(
-        row == col, jnp.broadcast_to(corner, (LANES, LANES)), jnp.where(row < col, turned, packed)
-    )
-    inverse_ref[...] = jnp.where(iota((size, size), 0) == iota((size, size), 1), 1.0, 0.0)
     upper_ref[...] = jnp.zeros((size, size), F32)
-
-    def send(source, target, begin, end):
-        copies.append(pltpu.make_async_copy(source.at[begin:end], target.at[begin:end], sems.at[len(copies)]))
-        copies[-1].start()
-
-    for begin in range(0, size, PANEL):
-        end = begin + PANEL
-        skip = 0 if begin < LANES else LANES
-        reach = LANES if end <= LANES else size
-        groups = [
-            jnp.concatenate([left_ref[g : g + 8, skip:], inverse_ref[g : g + 8, :reach]], axis=1)
-            for g in range(begin, end, 8)
-        ]
-        for g in range(0, PANEL // 8, 2):
-            groups = eliminate(groups, g, begin + 8 * g - skip, none, scale_ref)
-        panel = jnp.concatenate(groups, axis=0)
-        upper_ref[begin:end, skip:] = panel[:, : size - skip]
-        if end < size:
-            high, middle, low = split3(panel)
-            right = jnp.concatenate([high, middle, high, low, high, middle], axis=0)
-            lost = LANES if end == LANES else skip
-            turned = panel[:, lost - skip : size - skip]
-            turned = jnp.concatenate([turned, turned], axis=0).T[end - lost :, :]
-            high = turned.astype(BF16).astype(F32)
-            rest = turned - high
-            middle = rest.astype(BF16).astype(F32)
-            low = rest - middle
-            early = iota(turned.shape, 1) < PANEL
-            left = jnp.concatenate(
-                [high, jnp.where(early, middle, high), jnp.where(early, low, middle)], axis=1
-            ).astype(BF16)
-            apart = lost - skip
-            near = jnp.dot(left[:PANEL], right[:, apart : size - skip], preferred_element_type=F32)
-            left_ref[end : end + PANEL, lost:] = left_ref[end : end + PANEL, lost:] - near
-            near = jnp.dot(left[:PANEL], right[:, size - skip :], preferred_element_type=F32)
-            inverse_ref[end : end + PANEL, :reach] = inverse_ref[end : end + PANEL, :reach] - near
-            if end + PANEL < size:
-                far = jnp.dot(left[PANEL:], right[:, apart:], preferred_element_type=F32)
-                left_ref[end + PANEL :, lost:] = left_ref[end + PANEL :, lost:] - far[:, : size - lost]
-                inverse_ref[end + PANEL :, :reach] = inverse_ref[end + PANEL :, :reach] - far[:, size - lost :]
-        inverse = panel[:, size - skip :]
-        inverse = jnp.where(iota(inverse.shape, 0) + begin >= iota(inverse.shape, 1), inverse, 0.0)
-        both = jnp.dot(
-            jnp.concatenate(split2(inverse), axis=0), window_ref[:reach, :], preferred_element_type=F32
-        )
-        basis_ref[begin:end, :] = both[:PANEL] + both[PANEL:]
-        send(basis_ref, basis_hbm, begin, end)
+    inverse_ref[...] = jnp.zeros((size, size), F32)
+    fetch = lambda at: [work_ref[at : at + 8, LANES * v : LANES * (v + 1)] for v in range(4)]
+    active = [fetch(g) for g in range(0, 16 * AHEAD, 8)]
+    for begin in range(0, size, 16):
+        lead = begin // LANES
+        parts = (0, 1, 2) if lead == 0 else (1, 2, 3)
+        for i in range(0 if begin == 0 else 2, min(len(active), 4)):
+            at = begin + 8 * i
+            for v in (2, 3):
+                active[i][v] = work_ref[at : at + 8, LANES * v : LANES * (v + 1)]
+        eliminate(active, lead, begin % LANES, parts, none, scale_ref)
+        done = {v: jnp.concatenate([active[0][v], active[1][v]], axis=0) for v in parts}
+        active = active[2:]
+        for v in parts:
+            target, at = (upper_ref, v) if v < 2 else (inverse_ref, v - 2)
+            target[begin : begin + 16, LANES * at : LANES * (at + 1)] = done[v]
+        far, near = begin + 16 * AHEAD, begin + 32
+        if near < size:
+            terms = {v: split3(done[v]) for v in parts}
+            right = jnp.concatenate(
+                [jnp.concatenate([terms[v][t] for v in parts], axis=1) for t in (0, 1, 0, 2, 0, 1)], axis=0
+            )
+            left = []
+            for v in range(near // LANES, 2):
+                stack = jnp.concatenate([terms[v][t].astype(F32) for t in (0, 0, 1, 0, 2, 1)], axis=0)
+                left.append(stack.T[max(near - LANES * v, 0) :].astype(BF16))
+            share = jnp.dot(jnp.concatenate(left, axis=0), right, preferred_element_type=F32)
+            for i, v in enumerate(parts):
+                lanes = slice(LANES * v, LANES * (v + 1))
+                top = far if v < 2 else near
+                if top < size:
+                    work_ref[top:, lanes] = work_ref[top:, lanes] - share[top - near :, LANES * i : LANES * (i + 1)]
+            if far < size:
+                active += [fetch(far), fetch(far + 8)]
+        end = begin + 16
+        if end % PANEL == 0:
+            reach = LANES if end <= LANES else size
+            inverse = inverse_ref[end - PANEL : end, :reach]
+            inverse = jnp.where(iota(inverse.shape, 0) + (end - PANEL) >= iota(inverse.shape, 1), inverse, 0.0)
+            both = jnp.dot(
+                jnp.concatenate(split2(inverse), axis=0), window_ref[:reach, :], preferred_element_type=F32
+            )
+            basis_ref[end - PANEL : end, :] = both[:PANEL] + both[PANEL:]
+            send(basis_ref.at[end - PANEL : end], basis_hbm.at[end - PANEL : end])
         if end == LANES:
             factor_ref[:LANES, :LANES] = jnp.where(row >= col, upper_ref[:LANES, :LANES].T, 0.0)
             factor_ref[:LANES, LANES:] = jnp.zeros((LANES, LANES), F32)
             factor_ref[LANES:, :LANES] = upper_ref[:LANES, LANES:].T
-            send(factor_ref, factor_hbm, 0, LANES)
+            send(factor_ref.at[:LANES], factor_hbm.at[:LANES])
     factor_ref[LANES:, LANES:] = jnp.where(row >= col, upper_ref[LANES:, LANES:].T, 0.0)
-    send(factor_ref, factor_hbm, LANES, size)
+    send(factor_ref.at[LANES:], factor_hbm.at[LANES:])
     for copy in copies:
         copy.wait()
 
@@ -344,10 +345,11 @@
         out_shape=[shaped(coarse.shape, BF16), shaped((size, size)), shaped((size, rows_dev))],
         in_specs=[VMEM] * 4,
         out_specs=[HBM] * 3,
-        scratch_shapes=[pltpu.VMEM((size, size), F32)] * 4
+        scratch_shapes=[pltpu.VMEM((size, 2 * size), F32)]
+        + [pltpu.VMEM((size, size), F32)] * 3
         + [
             pltpu.VMEM((size, rows_dev), F32),
-            pltpu.VMEM((PANEL, LANES), F32),
+            pltpu.VMEM((16, LANES), F32),
             pltpu.VMEM((size, rows_dev), BF16),
             pltpu.SemaphoreType.DMA((size // PANEL + 3,)),
         ],
@@ -402,29 +404,29 @@
     fine = pltpu.with_memory_space_constraint(fine, pltpu.HBM)
     taps = pltpu.with_memory_space_constraint(filter_taps, pltpu.HBM)
     plane = pltpu.VMEM((4, 8 * fields, LANES), F32)
-    near, far, fine, matrix, stream = pl.pallas_call(
+    near, far, fine, matrix, stream, stored = pl.pallas_call(
         sent_kernel,
         out_shape=[pltpu.VMEM((9, snapshots, LANES), F32)] * 2
-        + [pltpu.VMEM(fine.shape, BF16), pltpu.VMEM((64, 256), BF16), pltpu.VMEM((12 * LANES, LANES), BF16)],
-        in_specs=[HBM] * 2,
-        out_specs=[VMEM] * 5,
-        scratch_shapes=[pltpu.SMEM(taps.shape, F32), plane, pltpu.SemaphoreType.DMA((PARTS + 1,))],
+        + [pltpu.VMEM(fine.shape, BF16), pltpu.VMEM((64, 256), BF16), pltpu.VMEM((12 * LANES, LANES), BF16)]
+        + [pltpu.VMEM(stored.shape, BF16)],
+        in_specs=[HBM] * 3,
+        out_specs=[VMEM] * 6,
+        scratch_shapes=[pltpu.SMEM(taps.shape, F32), plane, pltpu.SemaphoreType.DMA((PARTS + 2,))],
         compiler_params=LIMIT,
         name="filter_sent",
-    )(fine, taps)
+    )(fine, taps, pltpu.with_memory_space_constraint(stored, pltpu.HBM))
     from_far = swap_pairs(far, "span", 1)
     from_near = swap_pairs(near, "span", 0)
-    own, kept, sent, stored = pl.pallas_call(
+    own, kept, sent = pl.pallas_call(
         functools.partial(own_kernel, total),
         out_shape=[shaped((18, snapshots, LANES))]
-        + [shaped((HALF, LANES))] * 2
-        + [pltpu.VMEM(stored.shape, BF16)],
-        in_specs=[HBM] + [VMEM] * 3,
-        out_specs=[VMEM] * 4,
-        scratch_shapes=[plane, pltpu.SemaphoreType.DMA((1,))],
+        + [shaped((HALF, LANES))] * 2,
+        in_specs=[VMEM] * 4,
+        out_specs=[VMEM] * 3,
+        scratch_shapes=[plane],
         compiler_params=LIMIT,
         name="filter_own",
-    )(pltpu.with_memory_space_constraint(stored, pltpu.HBM), fine, matrix, stream)
+    )(stored, fine, matrix, stream)
     own = pl.pallas_call(
         join_far_kernel,
         out_shape=shaped((18, snapshots, LANES)),

time: 34.4 us -> 34.1 us (level)
  Pallas kernels: 10.8 us -> 9.96 us
  waiting for transfers between devices: 9.69 us -> 10.4 us
    ppermute x2, waiting for transfers between devices: 0.29 us -> 0.95 us  [swap_pairs(): return lax.ppermute(values, axis, pairs + [(j, i) for i, j in pairs])]
    pallas_call x1, Pallas kernels: 1.55 us -> 0.89 us  [local(): pl.pallas_call(functools.partial(own_kernel, total), out_shape=[shaped((1...]
  transfers between devices with their start and end apart: 8 -> 8, of which waited for: 7 -> 7; matrix products, arithmetic and copies ran while one was open for 0% -> 0% of each run, Pallas kernels for 5% -> 3%
where the time goes in v10:
time: 34.1 us; the launch traced here: 33.9 us
  starting transfers between devices  12.9 us (38%)
  waiting for transfers between devices  10.4 us (30%)
  Pallas kernels  9.96 us (29%)
  between operations  0.69 us (2%)
    ppermute x6, waiting for transfers between devices, swap(): return lax.ppermute(values, axis, [(i, i ^ bit) for i in range(count)])  9.4 us
    pallas_call x1, Pallas kernels, factorise(): pl.pallas_call(factor_kernel, out_shape=[shaped(coarse.shape, BF16), shap...  6.64 us
    ppermute x2, starting transfers between devices, swap_pairs(): return lax.ppermute(values, axis, pairs + [(j, i) for i, j in pairs])  6.46 us
    ppermute x6, starting transfers between devices, swap(): return lax.ppermute(values, axis, [(i, i ^ bit) for i in range(count)])  6.44 us
    pallas_call x1, Pallas kernels, local(): pl.pallas_call(sent_kernel, out_shape=[pltpu.VMEM((9, snapshots, LANES),...  1.97 us
    ppermute x2, waiting for transfers between devices, swap_pairs(): return lax.ppermute(values, axis, pairs + [(j, i) for i, j in pairs])  0.95 us
    pallas_call x1, Pallas kernels, local(): pl.pallas_call(functools.partial(own_kernel, total), out_shape=[shaped((1...  0.89 us
  transfers between devices with their start and end apart: 8, of which 7 were waited for; matrix products, arithmetic and copies ran while one was open for 0% of the time, Pallas kernels for 3%

profile of v10, /device:TPU:0, one launch (start us, length us, event | category | flops | bytes accessed | tf_op | source)
XLA Modules:
  0.0 33.9 jit_solution(427736709585258013)
XLA Ops:
  0.6 2.0 %filter_sent.1 = (f32[9,8,128]{2,1,0:T(8,128)S(1)}, f32[9,8,128]{2,1,0:T(8,128)S(1)}, bf16[24,256,128]{2,1,0:T(8,128)(2,1)S(1)}, bf16[64,256]{1,0:T(8,128)(2,1)S...) custom-call(bf16[24,256,128]{2,1,0:T(8,128)(2,1)} %bitcast.1, f32[3,17]{1,0:T(4,128)} %taps_hbm.1, ...), custom_call_target="tpu_custom_call" | custom-call | tf_op jit(solution)/shard_map/filter_sent/pallas_call | solution.py:407
  2.6 0.7 %collective-permute-start = (f32[9,8,128]{2,1,0:T(8,128)S(1)}, f32[9,8,128]{2,1,0:T(8,128)S(1)}, u32[]{:S(2)}, u32[]{:S(2)}) collective-permute-start(f32[9,8,128]{2,1,0:T(8,128)S(1)} %get-tuple-element.21), channel_id=1, source_target_pairs={{2,4},{6,8},{10,12},{4,2},{8,6},{12,10},{3,5},{7,9},{11,13},{5,3},... | collective-permute-start | bytes 110600 | tf_op jit(solution)/shard_map/ppermute | solution.py:378
  3.3 5.8 %collective-permute-start.1 = (f32[9,8,128]{2,1,0:T(8,128)S(1)}, f32[9,8,128]{2,1,0:T(8,128)S(1)}, u32[]{:S(2)}, u32[]{:S(2)}) collective-permute-start(f32[9,8,128]{2,1,0:T(8,128)S(1)} %get-tuple-element.22), channel_id=1, source_target_pairs={{0,2},{4,6},{8,10},{12,14},{2,0},{6,4},{10,8},{14,12},{1,3},{5,7},... | collective-permute-start | bytes 110600 | tf_op jit(solution)/shard_map/ppermute | solution.py:378
  9.1 0.9 %filter_own.1 = (f32[18,8,128]{2,1,0:T(8,128)S(1)}, f32[128,128]{1,0:T(8,128)S(1)}, f32[128,128]{1,0:T(8,128)S(1)}) custom-call(bf16[248,1536]{1,0:T(8,128)(2,1)S(1)} %get-tuple-element.16.stored_ref, bf16[24,256,128]{2,1,0:T(8,128)(2,1)S(1)} %get-tuple-element.17.fine_ref, bf16[64,256]{1,0:T(8,128)(2,1)S(1)} %get-tuple-element.18.matrix_ref, ...), custom_call_target="tpu_custom_call" | custom-call | tf_op jit(solution)/shard_map/filter_own/pallas_call | solution.py:420
  10.0 0.0 collective-permute-done.far_ref
  10.0 0.1 join_far.1.own_ref
  10.1 0.9 %collective-permute-done.1.near_ref = f32[9,8,128]{2,1,0:T(8,128)S(1)} collective-permute-done((f32[9,8,128]{2,1,0:T(8,128)S(1)}, f32[9,8,128]{2,1,0:T(8,128)S(1)}, u32[]{:S(2)}, u32[]{:S(2)}) %collective-permute-start.1) | collective-permute-done | bytes 36896 | tf_op jit(solution)/shard_map/ppermute | solution.py:378
  11.0 0.1 join_near.1
  11.1 0.1 collective-permute-start.2
  11.2 1.3 %collective-permute-done.2.partner_ref = f32[176,128]{1,0:T(8,128)S(1)} collective-permute-done((f32[176,128]{1,0:T(8,128)S(1)}, f32[176,128]{1,0:T(8,128)S(1)}, u32[]{:S(2)}, u32[]{:S(2)}) %collective-permute-start.2) | collective-permute-done | bytes 90144 | tf_op jit(solution)/shard_map/ppermute | solution.py:372
  12.5 0.3 gram_new.1
  12.8 3.1 %collective-permute-start.5 = (f32[144,128]{1,0:T(8,128)S(1)}, f32[144,128]{1,0:T(8,128)S(1)}, u32[]{:S(2)}, u32[]{:S(2)}) collective-permute-start(f32[144,128]{1,0:T(8,128)S(1)} %get-tuple-element.27), channel_id=1, source_target_pairs={{0,6},{2,4},{4,2},{6,0},{8,14},{10,12},{12,10},{14,8},{1,7},{3,5},... | collective-permute-start | bytes 221192 | tf_op jit(solution)/shard_map/ppermute | solution.py:372
  15.8 0.4 %collective-permute-start.4 = (f32[144,128]{1,0:T(8,128)S(1)}, f32[144,128]{1,0:T(8,128)S(1)}, u32[]{:S(2)}, u32[]{:S(2)}) collective-permute-start(f32[144,128]{1,0:T(8,128)S(1)} %get-tuple-element.27), channel_id=1, source_target_pairs={{0,4},{2,6},{4,0},{6,2},{8,12},{10,14},{12,8},{14,10},{1,5},{3,7},... | collective-permute-start | bytes 221192 | tf_op jit(solution)/shard_map/ppermute | solution.py:372
  16.3 0.1 collective-permute-start.3
  16.4 2.4 %collective-permute-done.5 = f32[144,128]{1,0:T(8,128)S(1)} collective-permute-done((f32[144,128]{1,0:T(8,128)S(1)}, f32[144,128]{1,0:T(8,128)S(1)}, u32[]{:S(2)}, u32[]{:S(2)}) %collective-permute-start.5) | collective-permute-done | bytes 73760 | tf_op jit(solution)/shard_map/ppermute | solution.py:372
  18.8 1.4 %collective-permute-done.4 = f32[144,128]{1,0:T(8,128)S(1)} collective-permute-done((f32[144,128]{1,0:T(8,128)S(1)}, f32[144,128]{1,0:T(8,128)S(1)}, u32[]{:S(2)}, u32[]{:S(2)}) %collective-permute-start.4) | collective-permute-done | bytes 73760 | tf_op jit(solution)/shard_map/ppermute | solution.py:372
  20.2 0.4 %collective-permute-done.3 = f32[144,128]{1,0:T(8,128)S(1)} collective-permute-done((f32[144,128]{1,0:T(8,128)S(1)}, f32[144,128]{1,0:T(8,128)S(1)}, u32[]{:S(2)}, u32[]{:S(2)}) %collective-permute-start.3) | collective-permute-done | bytes 73760 | tf_op jit(solution)/shard_map/ppermute | solution.py:372
  20.6 2.7 %collective-permute-start.6 = (f32[144,128]{1,0:T(8,128)S(1)}, f32[144,128]{1,0:T(8,128)S(1)}, u32[]{:S(2)}, u32[]{:S(2)}) collective-permute-start(f32[144,128]{1,0:T(8,128)S(1)} %add_add_fusion), channel_id=1, source_target_pairs={{0,8},{2,10},{4,12},{6,14},{8,0},{10,2},{12,4},{14,6},{1,9},{3,11}... | collective-permute-start | bytes 221192 | tf_op jit(solution)/shard_map/ppermute | solution.py:372
  23.3 2.7 %collective-permute-done.6 = f32[144,128]{1,0:T(8,128)S(1)} collective-permute-done((f32[144,128]{1,0:T(8,128)S(1)}, f32[144,128]{1,0:T(8,128)S(1)}, u32[]{:S(2)}, u32[]{:S(2)}) %collective-permute-start.6) | collective-permute-done | bytes 73760 | tf_op jit(solution)/shard_map/ppermute | solution.py:372
  26.0 0.1 collective-permute-start.7
  26.0 1.3 %collective-permute-done.7.other_ref = f32[144,128]{1,0:T(8,128)S(1)} collective-permute-done((f32[144,128]{1,0:T(8,128)S(1)}, f32[144,128]{1,0:T(8,128)S(1)}, u32[]{:S(2)}, u32[]{:S(2)}) %collective-permute-start.7) | collective-permute-done | bytes 73760 | tf_op jit(solution)/shard_map/ppermute | solution.py:372
  27.3 6.6 %factor.1 = (bf16[8,1536]{1,0:T(8,128)(2,1)}, f32[256,256]{1,0:T(8,128)}, f32[256,1536]{1,0:T(8,128)}) custom-call(f32[144,128]{1,0:T(8,128)S(1)} %add.15.mine_ref, f32[144,128]{1,0:T(8,128)S(1)} %collective-permute-done.7.other_ref, bf16[248,1536]{1,0:T(8,128)(2,1)S(1)} %get-tuple-element.16.stored_ref, bf16[8,1536]{1,0:T(8,128)(2,1)S(1)} %get-tuple-element.28.coarse_ref), custom_call_target="tpu_custom_call" | custom-call | tf_op jit(solution)/shard_map/factor/pallas_call | solution.py:343
  (2 shorter events, 0.0 us)
Async XLA Ops:
  2.6 7.4 %collective-permute-start = (f32[9,8,128]{2,1,0:T(8,128)S(1)}, f32[9,8,128]{2,1,0:T(8,128)S(1)}, u32[]{:S(2)}, u32[]{:S(2)}) collective-permute-start(f32[9,8,128]{2,1,0:T(8,128)S(1)} %get-tuple-element.21), channel_id=1, source_target_pairs={{2,4},{6,8},{10,12},{4,2},{8,6},{12,10},{3,5},{7,9},{11,13},{5,3},... | collective-permute-start | bytes 110600 | tf_op jit(solution)/shard_map/ppermute | solution.py:378
  3.3 7.7 %collective-permute-start.1 = (f32[9,8,128]{2,1,0:T(8,128)S(1)}, f32[9,8,128]{2,1,0:T(8,128)S(1)}, u32[]{:S(2)}, u32[]{:S(2)}) collective-permute-start(f32[9,8,128]{2,1,0:T(8,128)S(1)} %get-tuple-element.22), channel_id=1, source_target_pairs={{0,2},{4,6},{8,10},{12,14},{2,0},{6,4},{10,8},{14,12},{1,3},{5,7},... | collective-permute-start | bytes 110600 | tf_op jit(solution)/shard_map/ppermute | solution.py:378
  11.1 1.4 %collective-permute-start.2 = (f32[176,128]{1,0:T(8,128)S(1)}, f32[176,128]{1,0:T(8,128)S(1)}, u32[]{:S(2)}, u32[]{:S(2)}) collective-permute-start(f32[176,128]{1,0:T(8,128)S(1)} %get-tuple-element.25), channel_id=1, source_target_pairs={{0,1},{1,0},{2,3},{3,2},{4,5},{5,4},{6,7},{7,6},{8,9},{9,8},{10,11... | collective-permute-start | bytes 270344 | tf_op jit(solution)/shard_map/ppermute | solution.py:372
  12.8 6.0 %collective-permute-start.5 = (f32[144,128]{1,0:T(8,128)S(1)}, f32[144,128]{1,0:T(8,128)S(1)}, u32[]{:S(2)}, u32[]{:S(2)}) collective-permute-start(f32[144,128]{1,0:T(8,128)S(1)} %get-tuple-element.27), channel_id=1, source_target_pairs={{0,6},{2,4},{4,2},{6,0},{8,14},{10,12},{12,10},{14,8},{1,7},{3,5},... | collective-permute-start | bytes 221192 | tf_op jit(solution)/shard_map/ppermute | solution.py:372
  15.8 4.4 %collective-permute-start.4 = (f32[144,128]{1,0:T(8,128)S(1)}, f32[144,128]{1,0:T(8,128)S(1)}, u32[]{:S(2)}, u32[]{:S(2)}) collective-permute-start(f32[144,128]{1,0:T(8,128)S(1)} %get-tuple-element.27), channel_id=1, source_target_pairs={{0,4},{2,6},{4,0},{6,2},{8,12},{10,14},{12,8},{14,10},{1,5},{3,7},... | collective-permute-start | bytes 221192 | tf_op jit(solution)/shard_map/ppermute | solution.py:372
  16.3 4.4 %collective-permute-start.3 = (f32[144,128]{1,0:T(8,128)S(1)}, f32[144,128]{1,0:T(8,128)S(1)}, u32[]{:S(2)}, u32[]{:S(2)}) collective-permute-start(f32[144,128]{1,0:T(8,128)S(1)} %get-tuple-element.27), channel_id=1, source_target_pairs={{0,2},{2,0},{4,6},{6,4},{8,10},{10,8},{12,14},{14,12},{1,3},{3,1},... | collective-permute-start | bytes 221192 | tf_op jit(solution)/shard_map/ppermute | solution.py:372
  20.6 5.3 %collective-permute-start.6 = (f32[144,128]{1,0:T(8,128)S(1)}, f32[144,128]{1,0:T(8,128)S(1)}, u32[]{:S(2)}, u32[]{:S(2)}) collective-permute-start(f32[144,128]{1,0:T(8,128)S(1)} %add_add_fusion), channel_id=1, source_target_pairs={{0,8},{2,10},{4,12},{6,14},{8,0},{10,2},{12,4},{14,6},{1,9},{3,11}... | collective-permute-start | bytes 221192 | tf_op jit(solution)/shard_map/ppermute | solution.py:372
  26.0 1.3 %collective-permute-start.7 = (f32[144,128]{1,0:T(8,128)S(1)}, f32[144,128]{1,0:T(8,128)S(1)}, u32[]{:S(2)}, u32[]{:S(2)}) collective-permute-start(f32[144,128]{1,0:T(8,128)S(1)} %add.15.mine_ref), channel_id=1, source_target_pairs={{0,1},{1,0},{2,3},{3,2},{4,5},{5,4},{6,7},{7,6},{8,9},{9,8},{10,11... | collective-permute-start | bytes 221192 | tf_op jit(solution)/shard_map/ppermute | solution.py:372

commit v11 on v10

--- a/solution.py
+++ b/solution.py
@@ -208,7 +208,7 @@
     sums_ref[half + 8 :] = gram[:, LANES:]
 
 
-def eliminate(active, lead, lane, parts, none, scale_ref):
+def eliminate(active, lead, lane, parts, whole, none, scale_ref):
     spread = lambda values, k: jnp.broadcast_to(values[k : k + 1, :], (8, LANES))
     column = lambda g, j: jnp.broadcast_to(active[g][lead][:, lane + j : lane + j + 1], (8, LANES))
     sub = iota((8, LANES), 0)
@@ -239,7 +239,7 @@
                         cols[j, g] = cols[j, g] - share[g] * head
         for v in parts:
             row = spread(active[home][v], k_sub)
-            for g in range(home, len(active) if v < 2 else min(len(active), 4)):
+            for g in range(home, len(active) if v in whole else min(len(active), 4)):
                 active[g][v] = active[g][v] - share[g] * row
     for g in (0, 1):
         for v in parts:
@@ -290,9 +290,10 @@
         parts = (0, 1, 2) if lead == 0 else (1, 2, 3)
         for i in range(0 if begin == 0 else 2, min(len(active), 4)):
             at = begin + 8 * i
-            for v in (2, 3):
+            for v in (2, 3) if begin > LANES - 16 else (1, 2, 3):
                 active[i][v] = work_ref[at : at + 8, LANES * v : LANES * (v + 1)]
-        eliminate(active, lead, begin % LANES, parts, none, scale_ref)
+        whole = (0, 1) if begin == LANES - 16 else (lead,)
+        eliminate(active, lead, begin % LANES, parts, whole, none, scale_ref)
         done = {v: jnp.concatenate([active[0][v], active[1][v]], axis=0) for v in parts}
         active = active[2:]
         for v in parts:
@@ -311,7 +312,7 @@
             share = jnp.dot(jnp.concatenate(left, axis=0), right, preferred_element_type=F32)
             for i, v in enumerate(parts):
                 lanes = slice(LANES * v, LANES * (v + 1))
-                top = far if v < 2 else near
+                top = far if v in whole else near
                 if top < size:
                     work_ref[top:, lanes] = work_ref[top:, lanes] - share[top - near :, LANES * i : LANES * (i + 1)]
             if far < size:

time: 34.1 us -> 34.1 us (level)
  no operation moved by 1% of the time
where the time goes in v11:
time: 34.1 us; the launch traced here: 33.9 us
  starting transfers between devices  12.9 us (38%)
  waiting for transfers between devices  10.4 us (30%)
  Pallas kernels  9.91 us (29%)
  between operations  0.69 us (2%)
    ppermute x6, waiting for transfers between devices, swap(): return lax.ppermute(values, axis, [(i, i ^ bit) for i in range(count)])  9.4 us
    pallas_call x1, Pallas kernels, factorise(): pl.pallas_call(factor_kernel, out_shape=[shaped(coarse.shape, BF16), shap...  6.58 us
    ppermute x2, starting transfers between devices, swap_pairs(): return lax.ppermute(values, axis, pairs + [(j, i) for i, j in pairs])  6.46 us
    ppermute x6, starting transfers between devices, swap(): return lax.ppermute(values, axis, [(i, i ^ bit) for i in range(count)])  6.44 us
    pallas_call x1, Pallas kernels, local(): pl.pallas_call(sent_kernel, out_shape=[pltpu.VMEM((9, snapshots, LANES),...  1.97 us
    ppermute x2, waiting for transfers between devices, swap_pairs(): return lax.ppermute(values, axis, pairs + [(j, i) for i, j in pairs])  0.95 us
    pallas_call x1, Pallas kernels, local(): pl.pallas_call(functools.partial(own_kernel, total), out_shape=[shaped((1...  0.89 us
  transfers between devices with their start and end apart: 8, of which 7 were waited for; matrix products, arithmetic and copies ran while one was open for 0% of the time, Pallas kernels for 3%

profile of v11, /device:TPU:0, one launch (start us, length us, event | category | flops | bytes accessed | tf_op | source)
XLA Modules:
  0.0 33.9 jit_solution(9205915711002055391)
XLA Ops:
  0.6 2.0 %filter_sent.1 = (f32[9,8,128]{2,1,0:T(8,128)S(1)}, f32[9,8,128]{2,1,0:T(8,128)S(1)}, bf16[24,256,128]{2,1,0:T(8,128)(2,1)S(1)}, bf16[64,256]{1,0:T(8,128)(2,1)S...) custom-call(bf16[24,256,128]{2,1,0:T(8,128)(2,1)} %bitcast.1, f32[3,17]{1,0:T(4,128)} %taps_hbm.1, ...), custom_call_target="tpu_custom_call" | custom-call | tf_op jit(solution)/shard_map/filter_sent/pallas_call | solution.py:408
  2.6 0.7 %collective-permute-start = (f32[9,8,128]{2,1,0:T(8,128)S(1)}, f32[9,8,128]{2,1,0:T(8,128)S(1)}, u32[]{:S(2)}, u32[]{:S(2)}) collective-permute-start(f32[9,8,128]{2,1,0:T(8,128)S(1)} %get-tuple-element.21), channel_id=1, source_target_pairs={{2,4},{6,8},{10,12},{4,2},{8,6},{12,10},{3,5},{7,9},{11,13},{5,3},... | collective-permute-start | bytes 110600 | tf_op jit(solution)/shard_map/ppermute | solution.py:379
  3.3 5.8 %collective-permute-start.1 = (f32[9,8,128]{2,1,0:T(8,128)S(1)}, f32[9,8,128]{2,1,0:T(8,128)S(1)}, u32[]{:S(2)}, u32[]{:S(2)}) collective-permute-start(f32[9,8,128]{2,1,0:T(8,128)S(1)} %get-tuple-element.22), channel_id=1, source_target_pairs={{0,2},{4,6},{8,10},{12,14},{2,0},{6,4},{10,8},{14,12},{1,3},{5,7},... | collective-permute-start | bytes 110600 | tf_op jit(solution)/shard_map/ppermute | solution.py:379
  9.1 0.9 %filter_own.1 = (f32[18,8,128]{2,1,0:T(8,128)S(1)}, f32[128,128]{1,0:T(8,128)S(1)}, f32[128,128]{1,0:T(8,128)S(1)}) custom-call(bf16[248,1536]{1,0:T(8,128)(2,1)S(1)} %get-tuple-element.16.stored_ref, bf16[24,256,128]{2,1,0:T(8,128)(2,1)S(1)} %get-tuple-element.17.fine_ref, bf16[64,256]{1,0:T(8,128)(2,1)S(1)} %get-tuple-element.18.matrix_ref, ...), custom_call_target="tpu_custom_call" | custom-call | tf_op jit(solution)/shard_map/filter_own/pallas_call | solution.py:421
  10.0 0.0 collective-permute-done.far_ref
  10.0 0.1 join_far.1.own_ref
  10.1 0.9 %collective-permute-done.1.near_ref = f32[9,8,128]{2,1,0:T(8,128)S(1)} collective-permute-done((f32[9,8,128]{2,1,0:T(8,128)S(1)}, f32[9,8,128]{2,1,0:T(8,128)S(1)}, u32[]{:S(2)}, u32[]{:S(2)}) %collective-permute-start.1) | collective-permute-done | bytes 36896 | tf_op jit(solution)/shard_map/ppermute | solution.py:379
  11.0 0.1 join_near.1
  11.1 0.1 collective-permute-start.2
  11.2 1.3 %collective-permute-done.2.partner_ref = f32[176,128]{1,0:T(8,128)S(1)} collective-permute-done((f32[176,128]{1,0:T(8,128)S(1)}, f32[176,128]{1,0:T(8,128)S(1)}, u32[]{:S(2)}, u32[]{:S(2)}) %collective-permute-start.2) | collective-permute-done | bytes 90144 | tf_op jit(solution)/shard_map/ppermute | solution.py:373
  12.5 0.3 gram_new.1
  12.8 3.1 %collective-permute-start.5 = (f32[144,128]{1,0:T(8,128)S(1)}, f32[144,128]{1,0:T(8,128)S(1)}, u32[]{:S(2)}, u32[]{:S(2)}) collective-permute-start(f32[144,128]{1,0:T(8,128)S(1)} %get-tuple-element.27), channel_id=1, source_target_pairs={{0,6},{2,4},{4,2},{6,0},{8,14},{10,12},{12,10},{14,8},{1,7},{3,5},... | collective-permute-start | bytes 221192 | tf_op jit(solution)/shard_map/ppermute | solution.py:373
  15.8 0.4 %collective-permute-start.4 = (f32[144,128]{1,0:T(8,128)S(1)}, f32[144,128]{1,0:T(8,128)S(1)}, u32[]{:S(2)}, u32[]{:S(2)}) collective-permute-start(f32[144,128]{1,0:T(8,128)S(1)} %get-tuple-element.27), channel_id=1, source_target_pairs={{0,4},{2,6},{4,0},{6,2},{8,12},{10,14},{12,8},{14,10},{1,5},{3,7},... | collective-permute-start | bytes 221192 | tf_op jit(solution)/shard_map/ppermute | solution.py:373
  16.3 0.1 collective-permute-start.3
  16.4 2.4 %collective-permute-done.5 = f32[144,128]{1,0:T(8,128)S(1)} collective-permute-done((f32[144,128]{1,0:T(8,128)S(1)}, f32[144,128]{1,0:T(8,128)S(1)}, u32[]{:S(2)}, u32[]{:S(2)}) %collective-permute-start.5) | collective-permute-done | bytes 73760 | tf_op jit(solution)/shard_map/ppermute | solution.py:373
  18.8 1.4 %collective-permute-done.4 = f32[144,128]{1,0:T(8,128)S(1)} collective-permute-done((f32[144,128]{1,0:T(8,128)S(1)}, f32[144,128]{1,0:T(8,128)S(1)}, u32[]{:S(2)}, u32[]{:S(2)}) %collective-permute-start.4) | collective-permute-done | bytes 73760 | tf_op jit(solution)/shard_map/ppermute | solution.py:373
  20.2 0.4 %collective-permute-done.3 = f32[144,128]{1,0:T(8,128)S(1)} collective-permute-done((f32[144,128]{1,0:T(8,128)S(1)}, f32[144,128]{1,0:T(8,128)S(1)}, u32[]{:S(2)}, u32[]{:S(2)}) %collective-permute-start.3) | collective-permute-done | bytes 73760 | tf_op jit(solution)/shard_map/ppermute | solution.py:373
  20.6 2.7 %collective-permute-start.6 = (f32[144,128]{1,0:T(8,128)S(1)}, f32[144,128]{1,0:T(8,128)S(1)}, u32[]{:S(2)}, u32[]{:S(2)}) collective-permute-start(f32[144,128]{1,0:T(8,128)S(1)} %add_add_fusion), channel_id=1, source_target_pairs={{0,8},{2,10},{4,12},{6,14},{8,0},{10,2},{12,4},{14,6},{1,9},{3,11}... | collective-permute-start | bytes 221192 | tf_op jit(solution)/shard_map/ppermute | solution.py:373
  23.3 2.7 %collective-permute-done.6 = f32[144,128]{1,0:T(8,128)S(1)} collective-permute-done((f32[144,128]{1,0:T(8,128)S(1)}, f32[144,128]{1,0:T(8,128)S(1)}, u32[]{:S(2)}, u32[]{:S(2)}) %collective-permute-start.6) | collective-permute-done | bytes 73760 | tf_op jit(solution)/shard_map/ppermute | solution.py:373
  26.0 0.1 collective-permute-start.7
  26.0 1.3 %collective-permute-done.7.other_ref = f32[144,128]{1,0:T(8,128)S(1)} collective-permute-done((f32[144,128]{1,0:T(8,128)S(1)}, f32[144,128]{1,0:T(8,128)S(1)}, u32[]{:S(2)}, u32[]{:S(2)}) %collective-permute-start.7) | collective-permute-done | bytes 73760 | tf_op jit(solution)/shard_map/ppermute | solution.py:373
  27.3 6.6 %factor.1 = (bf16[8,1536]{1,0:T(8,128)(2,1)}, f32[256,256]{1,0:T(8,128)}, f32[256,1536]{1,0:T(8,128)}) custom-call(f32[144,128]{1,0:T(8,128)S(1)} %add.15.mine_ref, f32[144,128]{1,0:T(8,128)S(1)} %collective-permute-done.7.other_ref, bf16[248,1536]{1,0:T(8,128)(2,1)S(1)} %get-tuple-element.16.stored_ref, bf16[8,1536]{1,0:T(8,128)(2,1)S(1)} %get-tuple-element.28.coarse_ref), custom_call_target="tpu_custom_call" | custom-call | tf_op jit(solution)/shard_map/factor/pallas_call | solution.py:344
  (2 shorter events, 0.0 us)
Async XLA Ops:
  2.6 7.4 %collective-permute-start = (f32[9,8,128]{2,1,0:T(8,128)S(1)}, f32[9,8,128]{2,1,0:T(8,128)S(1)}, u32[]{:S(2)}, u32[]{:S(2)}) collective-permute-start(f32[9,8,128]{2,1,0:T(8,128)S(1)} %get-tuple-element.21), channel_id=1, source_target_pairs={{2,4},{6,8},{10,12},{4,2},{8,6},{12,10},{3,5},{7,9},{11,13},{5,3},... | collective-permute-start | bytes 110600 | tf_op jit(solution)/shard_map/ppermute | solution.py:379
  3.3 7.7 %collective-permute-start.1 = (f32[9,8,128]{2,1,0:T(8,128)S(1)}, f32[9,8,128]{2,1,0:T(8,128)S(1)}, u32[]{:S(2)}, u32[]{:S(2)}) collective-permute-start(f32[9,8,128]{2,1,0:T(8,128)S(1)} %get-tuple-element.22), channel_id=1, source_target_pairs={{0,2},{4,6},{8,10},{12,14},{2,0},{6,4},{10,8},{14,12},{1,3},{5,7},... | collective-permute-start | bytes 110600 | tf_op jit(solution)/shard_map/ppermute | solution.py:379
  11.1 1.4 %collective-permute-start.2 = (f32[176,128]{1,0:T(8,128)S(1)}, f32[176,128]{1,0:T(8,128)S(1)}, u32[]{:S(2)}, u32[]{:S(2)}) collective-permute-start(f32[176,128]{1,0:T(8,128)S(1)} %get-tuple-element.25), channel_id=1, source_target_pairs={{0,1},{1,0},{2,3},{3,2},{4,5},{5,4},{6,7},{7,6},{8,9},{9,8},{10,11... | collective-permute-start | bytes 270344 | tf_op jit(solution)/shard_map/ppermute | solution.py:373
  12.8 6.0 %collective-permute-start.5 = (f32[144,128]{1,0:T(8,128)S(1)}, f32[144,128]{1,0:T(8,128)S(1)}, u32[]{:S(2)}, u32[]{:S(2)}) collective-permute-start(f32[144,128]{1,0:T(8,128)S(1)} %get-tuple-element.27), channel_id=1, source_target_pairs={{0,6},{2,4},{4,2},{6,0},{8,14},{10,12},{12,10},{14,8},{1,7},{3,5},... | collective-permute-start | bytes 221192 | tf_op jit(solution)/shard_map/ppermute | solution.py:373
  15.8 4.4 %collective-permute-start.4 = (f32[144,128]{1,0:T(8,128)S(1)}, f32[144,128]{1,0:T(8,128)S(1)}, u32[]{:S(2)}, u32[]{:S(2)}) collective-permute-start(f32[144,128]{1,0:T(8,128)S(1)} %get-tuple-element.27), channel_id=1, source_target_pairs={{0,4},{2,6},{4,0},{6,2},{8,12},{10,14},{12,8},{14,10},{1,5},{3,7},... | collective-permute-start | bytes 221192 | tf_op jit(solution)/shard_map/ppermute | solution.py:373
  16.3 4.4 %collective-permute-start.3 = (f32[144,128]{1,0:T(8,128)S(1)}, f32[144,128]{1,0:T(8,128)S(1)}, u32[]{:S(2)}, u32[]{:S(2)}) collective-permute-start(f32[144,128]{1,0:T(8,128)S(1)} %get-tuple-element.27), channel_id=1, source_target_pairs={{0,2},{2,0},{4,6},{6,4},{8,10},{10,8},{12,14},{14,12},{1,3},{3,1},... | collective-permute-start | bytes 221192 | tf_op jit(solution)/shard_map/ppermute | solution.py:373
  20.6 5.3 %collective-permute-start.6 = (f32[144,128]{1,0:T(8,128)S(1)}, f32[144,128]{1,0:T(8,128)S(1)}, u32[]{:S(2)}, u32[]{:S(2)}) collective-permute-start(f32[144,128]{1,0:T(8,128)S(1)} %add_add_fusion), channel_id=1, source_target_pairs={{0,8},{2,10},{4,12},{6,14},{8,0},{10,2},{12,4},{14,6},{1,9},{3,11}... | collective-permute-start | bytes 221192 | tf_op jit(solution)/shard_map/ppermute | solution.py:373
  26.0 1.3 %collective-permute-start.7 = (f32[144,128]{1,0:T(8,128)S(1)}, f32[144,128]{1,0:T(8,128)S(1)}, u32[]{:S(2)}, u32[]{:S(2)}) collective-permute-start(f32[144,128]{1,0:T(8,128)S(1)} %add.15.mine_ref), channel_id=1, source_target_pairs={{0,1},{1,0},{2,3},{3,2},{4,5},{5,4},{6,7},{7,6},{8,9},{9,8},{10,11... | collective-permute-start | bytes 221192 | tf_op jit(solution)/shard_map/ppermute | solution.py:373

commit v12 on v11

--- a/solution.py
+++ b/solution.py
@@ -104,12 +104,9 @@
 
 
 def sent_kernel(
-    fine_hbm, taps_hbm, stored_hbm, near_ref, far_ref, fine_ref, own_matrix_ref, stream_ref, stored_ref,
-    taps_ref, plane_ref, sems,
+    fine_hbm, taps_hbm, near_ref, far_ref, fine_ref, own_matrix_ref, stream_ref, taps_ref, plane_ref, sems
 ):
-    taps_copy, *copies, stored_copy = start_copies(
-        [(taps_hbm, taps_ref)] + cells_of(fine_hbm, fine_ref) + [(stored_hbm, stored_ref)], sems
-    )
+    taps_copy, *copies = start_copies([(taps_hbm, taps_ref)] + cells_of(fine_hbm, fine_ref), sems)
     even = lax.axis_index("span") % 2 == 0
     span_cells = [jnp.where(even, at, at - 6) for at in (4, 5)] + [jnp.where(even, at - 6, at) for at in (4, 5)]
     taps_copy.wait()
@@ -128,7 +125,6 @@
         result = filter_stream(plane_ref, tiles, matrix)
         for t in range(len(tiles)):
             out_ref[t] = result[8 * t : 8 * t + 8]
-    stored_copy.wait()
 
 
 def fold(gram, kept_ref, sent_ref, first):
@@ -145,12 +141,16 @@
     return (row == LANES - 1) & (col < LANES - 8)
 
 
-def own_kernel(total, stored_ref, fine_ref, matrix_ref, stream_ref, own_ref, kept_ref, sent_ref, plane_ref):
+def own_kernel(
+    total, stored_hbm, fine_ref, matrix_ref, stream_ref, own_ref, kept_ref, sent_ref, stored_ref, plane_ref, sems
+):
+    (copy,) = start_copies([(stored_hbm, stored_ref)], sems)
     filter_plane(matrix_ref[...], fine_ref, plane_ref)
     tiles = [(comp, [(s, k) for s in range(4)]) for comp in range(3) for k in range(6)]
     result = filter_stream(plane_ref, tiles, stream_ref[...])
     for t in range(len(tiles)):
         own_ref[t] = result[8 * t : 8 * t + 8]
+    copy.wait()
     old, cells = stored_ref.shape
     rows = jnp.concatenate([stored_ref[...], jnp.zeros((8, cells), BF16)], axis=0)
     gram = lax.dot_general(rows, rows, (((1,), (1,)), ((), ())), preferred_element_type=F32) / total
@@ -405,29 +405,29 @@
     fine = pltpu.with_memory_space_constraint(fine, pltpu.HBM)
     taps = pltpu.with_memory_space_constraint(filter_taps, pltpu.HBM)
     plane = pltpu.VMEM((4, 8 * fields, LANES), F32)
-    near, far, fine, matrix, stream, stored = pl.pallas_call(
+    near, far, fine, matrix, stream = pl.pallas_call(
         sent_kernel,
         out_shape=[pltpu.VMEM((9, snapshots, LANES), F32)] * 2
-        + [pltpu.VMEM(fine.shape, BF16), pltpu.VMEM((64, 256), BF16), pltpu.VMEM((12 * LANES, LANES), BF16)]
-        + [pltpu.VMEM(stored.shape, BF16)],
-        in_specs=[HBM] * 3,
-        out_specs=[VMEM] * 6,
-        scratch_shapes=[pltpu.SMEM(taps.shape, F32), plane, pltpu.SemaphoreType.DMA((PARTS + 2,))],
+        + [pltpu.VMEM(fine.shape, BF16), pltpu.VMEM((64, 256), BF16), pltpu.VMEM((12 * LANES, LANES), BF16)],
+        in_specs=[HBM] * 2,
+        out_specs=[VMEM] * 5,
+        scratch_shapes=[pltpu.SMEM(taps.shape, F32), plane, pltpu.SemaphoreType.DMA((PARTS + 1,))],
         compiler_params=LIMIT,
         name="filter_sent",
-    )(fine, taps, pltpu.with_memory_space_constraint(stored, pltpu.HBM))
+    )(fine, taps)
     from_far = swap_pairs(far, "span", 1)
     from_near = swap_pairs(near, "span", 0)
-    own, kept, sent = pl.pallas_call(
+    own, kept, sent, stored = pl.pallas_call(
         functools.partial(own_kernel, total),
         out_shape=[shaped((18, snapshots, LANES))]
-        + [shaped((HALF, LANES))] * 2,
-        in_specs=[VMEM] * 4,
-        out_specs=[VMEM] * 3,
-        scratch_shapes=[plane],
+        + [shaped((HALF, LANES))] * 2
+        + [pltpu.VMEM(stored.shape, BF16)],
+        in_specs=[HBM] + [VMEM] * 3,
+        out_specs=[VMEM] * 4,
+        scratch_shapes=[plane, pltpu.SemaphoreType.DMA((1,))],
         compiler_params=LIMIT,
         name="filter_own",
-    )(stored, fine, matrix, stream)
+    )(pltpu.with_memory_space_constraint(stored, pltpu.HBM), fine, matrix, stream)
     own = pl.pallas_call(
         join_far_kernel,
         out_shape=shaped((18, snapshots, LANES)),

time: 34.1 us -> 34.1 us (level)
  waiting for transfers between devices: 10.4 us -> 9.69 us
  Pallas kernels: 9.91 us -> 10.5 us
    ppermute x2, waiting for transfers between devices: 0.95 us -> 0.29 us  [swap_pairs(): return lax.ppermute(values, axis, pairs + [(j, i) for i, j in pairs])]
    pallas_call x1, Pallas kernels: 0.89 us -> 1.55 us  [local(): pl.pallas_call(functools.partial(own_kernel, total), out_shape=[shaped((1...]
  transfers between devices with their start and end apart: 8 -> 8, of which waited for: 7 -> 7; matrix products, arithmetic and copies ran while one was open for 0% -> 0% of each run, Pallas kernels for 3% -> 5%
where the time goes in v12:
time: 34.1 us; the launch traced here: 33.9 us
  starting transfers between devices  12.9 us (38%)
  Pallas kernels  10.5 us (31%)
  waiting for transfers between devices  9.69 us (28%)
  between operations  0.69 us (2%)
    ppermute x6, waiting for transfers between devices, swap(): return lax.ppermute(values, axis, [(i, i ^ bit) for i in range(count)])  9.4 us
    pallas_call x1, Pallas kernels, factorise(): pl.pallas_call(factor_kernel, out_shape=[shaped(coarse.shape, BF16), shap...  6.58 us
    ppermute x2, starting transfers between devices, swap_pairs(): return lax.ppermute(values, axis, pairs + [(j, i) for i, j in pairs])  6.46 us
    ppermute x6, starting transfers between devices, swap(): return lax.ppermute(values, axis, [(i, i ^ bit) for i in range(count)])  6.44 us
    pallas_call x1, Pallas kernels, local(): pl.pallas_call(sent_kernel, out_shape=[pltpu.VMEM((9, snapshots, LANES),...  1.96 us
    pallas_call x1, Pallas kernels, local(): pl.pallas_call(functools.partial(own_kernel, total), out_shape=[shaped((1...  1.55 us
  transfers between devices with their start and end apart: 8, of which 7 were waited for; matrix products, arithmetic and copies ran while one was open for 0% of the time, Pallas kernels for 5%

profile of v12, /device:TPU:0, one launch (start us, length us, event | category | flops | bytes accessed | tf_op | source)
XLA Modules:
  0.0 33.9 jit_solution(9081184284452871038)
XLA Ops:
  0.6 2.0 %filter_sent.1 = (f32[9,8,128]{2,1,0:T(8,128)S(1)}, f32[9,8,128]{2,1,0:T(8,128)S(1)}, bf16[24,256,128]{2,1,0:T(8,128)(2,1)S(1)}, bf16[64,256]{1,0:T(8,128)(2,1)S(1)}, bf16[1536,128]{1,0:T(8,128)(2,1)S(1)}) custom-call(bf16[24,256,128]{2,1,0:T(8,128)(2,1)} %bitcast.1, f32[3,17]{1,0:T(4,128)} %taps_hbm.1), custom_call_target="tpu_custom_call" | custom-call | tf_op jit(solution)/shard_map/filter_sent/pallas_call | solution.py:408
  2.6 0.7 %collective-permute-start = (f32[9,8,128]{2,1,0:T(8,128)S(1)}, f32[9,8,128]{2,1,0:T(8,128)S(1)}, u32[]{:S(2)}, u32[]{:S(2)}) collective-permute-start(f32[9,8,128]{2,1,0:T(8,128)S(1)} %get-tuple-element.21), channel_id=1, source_target_pairs={{2,4},{6,8},{10,12},{4,2},{8,6},{12,10},{3,5},{7,9},{11,13},{5,3},... | collective-permute-start | bytes 110600 | tf_op jit(solution)/shard_map/ppermute | solution.py:379
  3.3 5.8 %collective-permute-start.1 = (f32[9,8,128]{2,1,0:T(8,128)S(1)}, f32[9,8,128]{2,1,0:T(8,128)S(1)}, u32[]{:S(2)}, u32[]{:S(2)}) collective-permute-start(f32[9,8,128]{2,1,0:T(8,128)S(1)} %get-tuple-element.22), channel_id=1, source_target_pairs={{0,2},{4,6},{8,10},{12,14},{2,0},{6,4},{10,8},{14,12},{1,3},{5,7},... | collective-permute-start | bytes 110600 | tf_op jit(solution)/shard_map/ppermute | solution.py:379
  9.1 1.5 %filter_own.1 = (f32[18,8,128]{2,1,0:T(8,128)S(1)}, f32[128,128]{1,0:T(8,128)S(1)}, f32[128,128]{1,0:T(8,128)S(1)}, bf16[248,1536]{1,0:T(8,128)(2,1)S(1)}) custom-call(bf16[248,1536]{1,0:T(8,128)(2,1)} %stored_hbm.1, bf16[24,256,128]{2,1,0:T(8,128)(2,1)S(1)} %get-tuple-element.16.fine_ref, bf16[64,256]{1,0:T(8,128)(2,1)S(1)} %get-tuple-element.17.matrix_ref, ...), custom_call_target="tpu_custom_call" | custom-call | tf_op jit(solution)/shard_map/filter_own/pallas_call | solution.py:420
  10.6 0.0 collective-permute-done.far_ref
  10.6 0.1 join_far.1.own_ref
  10.7 0.3 collective-permute-done.1.near_ref
  11.0 0.1 join_near.1
  11.1 0.1 collective-permute-start.2
  11.2 1.3 %collective-permute-done.2.partner_ref = f32[176,128]{1,0:T(8,128)S(1)} collective-permute-done((f32[176,128]{1,0:T(8,128)S(1)}, f32[176,128]{1,0:T(8,128)S(1)}, u32[]{:S(2)}, u32[]{:S(2)}) %collective-permute-start.2) | collective-permute-done | bytes 90144 | tf_op jit(solution)/shard_map/ppermute | solution.py:373
  12.4 0.3 gram_new.1
  12.7 3.1 %collective-permute-start.5 = (f32[144,128]{1,0:T(8,128)S(1)}, f32[144,128]{1,0:T(8,128)S(1)}, u32[]{:S(2)}, u32[]{:S(2)}) collective-permute-start(f32[144,128]{1,0:T(8,128)S(1)} %get-tuple-element.27), channel_id=1, source_target_pairs={{0,6},{2,4},{4,2},{6,0},{8,14},{10,12},{12,10},{14,8},{1,7},{3,5},... | collective-permute-start | bytes 221192 | tf_op jit(solution)/shard_map/ppermute | solution.py:373
  15.8 0.4 %collective-permute-start.4 = (f32[144,128]{1,0:T(8,128)S(1)}, f32[144,128]{1,0:T(8,128)S(1)}, u32[]{:S(2)}, u32[]{:S(2)}) collective-permute-start(f32[144,128]{1,0:T(8,128)S(1)} %get-tuple-element.27), channel_id=1, source_target_pairs={{0,4},{2,6},{4,0},{6,2},{8,12},{10,14},{12,8},{14,10},{1,5},{3,7},... | collective-permute-start | bytes 221192 | tf_op jit(solution)/shard_map/ppermute | solution.py:373
  16.2 0.1 collective-permute-start.3
  16.4 2.4 %collective-permute-done.5 = f32[144,128]{1,0:T(8,128)S(1)} collective-permute-done((f32[144,128]{1,0:T(8,128)S(1)}, f32[144,128]{1,0:T(8,128)S(1)}, u32[]{:S(2)}, u32[]{:S(2)}) %collective-permute-start.5) | collective-permute-done | bytes 73760 | tf_op jit(solution)/shard_map/ppermute | solution.py:373
  18.7 1.4 %collective-permute-done.4 = f32[144,128]{1,0:T(8,128)S(1)} collective-permute-done((f32[144,128]{1,0:T(8,128)S(1)}, f32[144,128]{1,0:T(8,128)S(1)}, u32[]{:S(2)}, u32[]{:S(2)}) %collective-permute-start.4) | collective-permute-done | bytes 73760 | tf_op jit(solution)/shard_map/ppermute | solution.py:373
  20.2 0.4 %collective-permute-done.3 = f32[144,128]{1,0:T(8,128)S(1)} collective-permute-done((f32[144,128]{1,0:T(8,128)S(1)}, f32[144,128]{1,0:T(8,128)S(1)}, u32[]{:S(2)}, u32[]{:S(2)}) %collective-permute-start.3) | collective-permute-done | bytes 73760 | tf_op jit(solution)/shard_map/ppermute | solution.py:373
  20.6 2.7 %collective-permute-start.6 = (f32[144,128]{1,0:T(8,128)S(1)}, f32[144,128]{1,0:T(8,128)S(1)}, u32[]{:S(2)}, u32[]{:S(2)}) collective-permute-start(f32[144,128]{1,0:T(8,128)S(1)} %add_add_fusion), channel_id=1, source_target_pairs={{0,8},{2,10},{4,12},{6,14},{8,0},{10,2},{12,4},{14,6},{1,9},{3,11}... | collective-permute-start | bytes 221192 | tf_op jit(solution)/shard_map/ppermute | solution.py:373
  23.3 2.7 %collective-permute-done.6 = f32[144,128]{1,0:T(8,128)S(1)} collective-permute-done((f32[144,128]{1,0:T(8,128)S(1)}, f32[144,128]{1,0:T(8,128)S(1)}, u32[]{:S(2)}, u32[]{:S(2)}) %collective-permute-start.6) | collective-permute-done | bytes 73760 | tf_op jit(solution)/shard_map/ppermute | solution.py:373
  26.0 0.1 collective-permute-start.7
  26.0 1.3 %collective-permute-done.7.other_ref = f32[144,128]{1,0:T(8,128)S(1)} collective-permute-done((f32[144,128]{1,0:T(8,128)S(1)}, f32[144,128]{1,0:T(8,128)S(1)}, u32[]{:S(2)}, u32[]{:S(2)}) %collective-permute-start.7) | collective-permute-done | bytes 73760 | tf_op jit(solution)/shard_map/ppermute | solution.py:373
  27.3 6.6 %factor.1 = (bf16[8,1536]{1,0:T(8,128)(2,1)}, f32[256,256]{1,0:T(8,128)}, f32[256,1536]{1,0:T(8,128)}) custom-call(f32[144,128]{1,0:T(8,128)S(1)} %add.15.mine_ref, f32[144,128]{1,0:T(8,128)S(1)} %collective-permute-done.7.other_ref, bf16[248,1536]{1,0:T(8,128)(2,1)S(1)} %get-tuple-element.19.stored_ref, bf16[8,1536]{1,0:T(8,128)(2,1)S(1)} %get-tuple-element.28.coarse_ref), custom_call_target="tpu_custom_call" | custom-call | tf_op jit(solution)/shard_map/factor/pallas_call | solution.py:344
  (2 shorter events, 0.0 us)
Async XLA Ops:
  2.6 8.0 %collective-permute-start = (f32[9,8,128]{2,1,0:T(8,128)S(1)}, f32[9,8,128]{2,1,0:T(8,128)S(1)}, u32[]{:S(2)}, u32[]{:S(2)}) collective-permute-start(f32[9,8,128]{2,1,0:T(8,128)S(1)} %get-tuple-element.21), channel_id=1, source_target_pairs={{2,4},{6,8},{10,12},{4,2},{8,6},{12,10},{3,5},{7,9},{11,13},{5,3},... | collective-permute-start | bytes 110600 | tf_op jit(solution)/shard_map/ppermute | solution.py:379
  3.3 7.7 %collective-permute-start.1 = (f32[9,8,128]{2,1,0:T(8,128)S(1)}, f32[9,8,128]{2,1,0:T(8,128)S(1)}, u32[]{:S(2)}, u32[]{:S(2)}) collective-permute-start(f32[9,8,128]{2,1,0:T(8,128)S(1)} %get-tuple-element.22), channel_id=1, source_target_pairs={{0,2},{4,6},{8,10},{12,14},{2,0},{6,4},{10,8},{14,12},{1,3},{5,7},... | collective-permute-start | bytes 110600 | tf_op jit(solution)/shard_map/ppermute | solution.py:379
  11.1 1.4 %collective-permute-start.2 = (f32[176,128]{1,0:T(8,128)S(1)}, f32[176,128]{1,0:T(8,128)S(1)}, u32[]{:S(2)}, u32[]{:S(2)}) collective-permute-start(f32[176,128]{1,0:T(8,128)S(1)} %get-tuple-element.25), channel_id=1, source_target_pairs={{0,1},{1,0},{2,3},{3,2},{4,5},{5,4},{6,7},{7,6},{8,9},{9,8},{10,11... | collective-permute-start | bytes 270344 | tf_op jit(solution)/shard_map/ppermute | solution.py:373
  12.7 6.0 %collective-permute-start.5 = (f32[144,128]{1,0:T(8,128)S(1)}, f32[144,128]{1,0:T(8,128)S(1)}, u32[]{:S(2)}, u32[]{:S(2)}) collective-permute-start(f32[144,128]{1,0:T(8,128)S(1)} %get-tuple-element.27), channel_id=1, source_target_pairs={{0,6},{2,4},{4,2},{6,0},{8,14},{10,12},{12,10},{14,8},{1,7},{3,5},... | collective-permute-start | bytes 221192 | tf_op jit(solution)/shard_map/ppermute | solution.py:373
  15.8 4.4 %collective-permute-start.4 = (f32[144,128]{1,0:T(8,128)S(1)}, f32[144,128]{1,0:T(8,128)S(1)}, u32[]{:S(2)}, u32[]{:S(2)}) collective-permute-start(f32[144,128]{1,0:T(8,128)S(1)} %get-tuple-element.27), channel_id=1, source_target_pairs={{0,4},{2,6},{4,0},{6,2},{8,12},{10,14},{12,8},{14,10},{1,5},{3,7},... | collective-permute-start | bytes 221192 | tf_op jit(solution)/shard_map/ppermute | solution.py:373
  16.2 4.4 %collective-permute-start.3 = (f32[144,128]{1,0:T(8,128)S(1)}, f32[144,128]{1,0:T(8,128)S(1)}, u32[]{:S(2)}, u32[]{:S(2)}) collective-permute-start(f32[144,128]{1,0:T(8,128)S(1)} %get-tuple-element.27), channel_id=1, source_target_pairs={{0,2},{2,0},{4,6},{6,4},{8,10},{10,8},{12,14},{14,12},{1,3},{3,1},... | collective-permute-start | bytes 221192 | tf_op jit(solution)/shard_map/ppermute | solution.py:373
  20.6 5.3 %collective-permute-start.6 = (f32[144,128]{1,0:T(8,128)S(1)}, f32[144,128]{1,0:T(8,128)S(1)}, u32[]{:S(2)}, u32[]{:S(2)}) collective-permute-start(f32[144,128]{1,0:T(8,128)S(1)} %add_add_fusion), channel_id=1, source_target_pairs={{0,8},{2,10},{4,12},{6,14},{8,0},{10,2},{12,4},{14,6},{1,9},{3,11}... | collective-permute-start | bytes 221192 | tf_op jit(solution)/shard_map/ppermute | solution.py:373
  26.0 1.3 %collective-permute-start.7 = (f32[144,128]{1,0:T(8,128)S(1)}, f32[144,128]{1,0:T(8,128)S(1)}, u32[]{:S(2)}, u32[]{:S(2)}) collective-permute-start(f32[144,128]{1,0:T(8,128)S(1)} %add.15.mine_ref), channel_id=1, source_target_pairs={{0,1},{1,0},{2,3},{3,2},{4,5},{5,4},{6,7},{7,6},{8,9},{9,8},{10,11... | collective-permute-start | bytes 221192 | tf_op jit(solution)/shard_map/ppermute | solution.py:373
